TPU v7x, 32 devices: a whole 2x2x4 slice. The times are simulated.
32 devices in a mesh: ctx: 16 (over z, y, core), tp: 2 (over x).
Axes of the slice: x: 2, y: 2, z: 4, core: 2. Of those that a mesh axis runs over, the one named last changes fastest.
Arguments:
- queries: bfloat16 [8192, 4096], P('ctx', 'tp'), may hold values from -0.19921875 to 0.19921875
- keys: bfloat16 [8192, 4096], P('ctx', 'tp'), may hold values from -0.19921875 to 0.19921875
- values: bfloat16 [8192, 4096], P('ctx', 'tp'), may hold values from -0.19921875 to 0.19921875
- cotangent: bfloat16 [8192, 2048], P('ctx', 'tp'), may hold values from -6 to 6
- out_weight: bfloat16 [4096, 2048], P('tp'), may hold values from -0.125 to 0.125
- memory: float32 [32, 128, 128], P('tp'), may hold values from -0.6 to 0.6
Outputs:
- query_grad: bfloat16 [8192, 4096], P('ctx', 'tp')
- key_grad: bfloat16 [8192, 4096], P('ctx', 'tp')
- value_grad: bfloat16 [8192, 4096], P('ctx', 'tp')
- weight_grad: float32 [4096, 2048], P(('tp', 'ctx'))
All inputs are finite; a program needn't handle non-finite values.
Results may differ from a plain program's by a relative error of at most 0.0058.
Values may be sent and summed in bfloat16 or wider, within the bound.
No kernel may reach another device: no remote copies, remote signals or barrier semaphores. Data moves between devices by JAX's collectives and lax.ppermute only.
A program may use at most 320 MiB of HBM per device.

v0:
```python
import functools

import jax
import jax.numpy as jnp
from jax import lax
from jax.experimental import pallas as pl
from jax.experimental.pallas import tpu as pltpu
from jax.sharding import PartitionSpec as P

BF = jnp.bfloat16
F32 = jnp.float32
VMEM_LIMIT = 56 * 1024 * 1024


def dot(a, b, ca, cb):
    return lax.dot_general(a, b, (((ca,), (cb,)), ((), ())), preferred_element_type=F32)


def lanes(index, head):
    return pl.ds(pl.multiple_of(index * head, head), head)


def params():
    return pltpu.CompilerParams(vmem_limit_bytes=VMEM_LIMIT)


def cost(flops, nbytes):
    return pl.CostEstimate(flops=int(flops), bytes_accessed=int(nbytes), transcendentals=0)


def kv_kernel(head, a_ref, b_ref, o_ref):
    for j in range(a_ref.shape[1] // head):
        at = slice(j * head, (j + 1) * head)
        o_ref[at, :] = dot(a_ref[:, at], b_ref[:, at], 0, 0).astype(o_ref.dtype)


def block_sums(a, b, head):
    tok, width = a.shape
    step = 2 * head
    return pl.pallas_call(
        functools.partial(kv_kernel, head),
        grid=(width // step,),
        in_specs=[pl.BlockSpec((tok, step), lambda i: (0, i))] * 2,
        out_specs=pl.BlockSpec((step, head), lambda i: (i, 0)),
        out_shape=jax.ShapeDtypeStruct((width, head), BF),
        compiler_params=params(),
        cost_estimate=cost(2 * tok * width * head, 4 * tok * width),
        name="block_sums",
    )(a, b)


def masked(tok, upper):
    row = lax.broadcasted_iota(jnp.int32, (tok, tok), 0)
    col = lax.broadcasted_iota(jnp.int32, (tok, tok), 1)
    return row <= col if upper else row >= col


def causal_apply(a, b, c, upper):
    tok = a.shape[0]
    half = tok // 2
    keep = masked(half, upper)

    def tile(x, y, diagonal):
        s = dot(x, y, 1, 1)
        if diagonal:
            s = jnp.where(keep, s, 0.0)
        return s.astype(BF)

    a0, a1, b0, b1, c0, c1 = a[:half], a[half:], b[:half], b[half:], c[:half], c[half:]
    first = dot(tile(a0, b0, True), c0, 1, 0)
    second = dot(tile(a1, b1, True), c1, 1, 0)
    if upper:
        first = first + dot(tile(a0, b1, False), c1, 1, 0)
    else:
        second = second + dot(tile(a1, b0, False), c0, 1, 0)
    return first, second


def intra_kernel(head, q_ref, k_ref, v_ref, o_ref):
    half = q_ref.shape[0] // 2
    for j in range(q_ref.shape[1] // head):
        at = slice(j * head, (j + 1) * head)
        first, second = causal_apply(q_ref[:, at], k_ref[:, at], v_ref[:, at], False)
        o_ref[:half, at] = first
        o_ref[half:, at] = second


def intra(q, k, v, head):
    tok, width = q.shape
    step = 2 * head
    spec = pl.BlockSpec((tok, step), lambda i: (0, i))
    return pl.pallas_call(
        functools.partial(intra_kernel, head),
        grid=(width // step,),
        in_specs=[spec] * 3,
        out_specs=spec,
        out_shape=jax.ShapeDtypeStruct((tok, width), F32),
        compiler_params=params(),
        cost_estimate=cost(4 * tok * tok * width, 10 * tok * width),
        name="intra",
    )(q, k, v)


def grad_kernel(head, tp_ref, own_ref, far_ref, wo_ref, wf_ref, q_ref, g_ref, s_ref):
    g = dot(own_ref[...], wo_ref[...], 1, 1) + dot(far_ref[...], wf_ref[...], 1, 1)
    g = g.astype(BF)
    g_ref[...] = g
    for j in range(g.shape[1] // head):
        at = slice(j * head, (j + 1) * head)
        s_ref[at, :] = dot(q_ref[:, at], g[:, at], 0, 0).astype(s_ref.dtype)


def out_grad_and_sums(tp, own, far, w, q, head):
    tok, feat = own.shape
    width = q.shape[1]
    step = 2 * head
    whole = pl.BlockSpec((tok, feat), lambda i, t: (0, 0))
    return pl.pallas_call(
        functools.partial(grad_kernel, head),
        grid_spec=pltpu.PrefetchScalarGridSpec(
            num_scalar_prefetch=1,
            grid=(width // step,),
            in_specs=[
                whole,
                whole,
                pl.BlockSpec((step, feat), lambda i, t: (i, t[0])),
                pl.BlockSpec((step, feat), lambda i, t: (i, 1 - t[0])),
                pl.BlockSpec((tok, step), lambda i, t: (0, i)),
            ],
            out_specs=[
                pl.BlockSpec((tok, step), lambda i, t: (0, i)),
                pl.BlockSpec((step, head), lambda i, t: (i, 0)),
            ],
        ),
        out_shape=[
            jax.ShapeDtypeStruct((tok, width), BF),
            jax.ShapeDtypeStruct((width, head), BF),
        ],
        compiler_params=params(),
        cost_estimate=cost(4 * tok * feat * width, 4 * feat * width + 4 * tok * width),
        name="out_grad",
    )(tp, own, far, w, w, q)


def attended_kernel(head, q_ref, s_ref, i_ref, o_ref):
    for j in range(q_ref.shape[1] // head):
        at = slice(j * head, (j + 1) * head)
        o_ref[:, at] = (dot(q_ref[:, at], s_ref[at, :], 1, 0) + i_ref[:, at]).astype(BF)


def attended_of(q, state, inner, head):
    tok, width = q.shape
    step = 2 * head
    spec = pl.BlockSpec((tok, step), lambda i: (0, i))
    return pl.pallas_call(
        functools.partial(attended_kernel, head),
        grid=(width // step,),
        in_specs=[spec, pl.BlockSpec((step, head), lambda i: (i, 0)), spec],
        out_specs=spec,
        out_shape=jax.ShapeDtypeStruct((tok, width), BF),
        compiler_params=params(),
        cost_estimate=cost(2 * tok * head * width, 8 * tok * width),
        name="attended",
    )(q, state, inner)


def weight_kernel(a_ref, own_ref, far_ref, o_ref):
    feat = own_ref.shape[1]
    a = a_ref[...]
    o_ref[:, :feat] = dot(a, own_ref[...], 0, 0).astype(o_ref.dtype)
    o_ref[:, feat:] = dot(a, far_ref[...], 0, 0).astype(o_ref.dtype)


def weight_term(a, own, far):
    tok, width = a.shape
    feat = own.shape[1]
    step = 256
    whole = pl.BlockSpec((tok, feat), lambda i: (0, 0))
    return pl.pallas_call(
        weight_kernel,
        grid=(width // step,),
        in_specs=[pl.BlockSpec((tok, step), lambda i: (0, i)), whole, whole],
        out_specs=pl.BlockSpec((step, 2 * feat), lambda i: (i, 0)),
        out_shape=jax.ShapeDtypeStruct((width, 2 * feat), BF),
        compiler_params=params(),
        cost_estimate=cost(4 * tok * feat * width, 4 * feat * width + 2 * tok * width),
        name="weight_term",
    )(a, own, far)


def query_kernel(head, g_ref, v_ref, k_ref, s_ref, o_ref):
    half = g_ref.shape[0] // 2
    for j in range(g_ref.shape[1] // head):
        at = slice(j * head, (j + 1) * head)
        g = g_ref[:, at]
        first, second = causal_apply(g, v_ref[:, at], k_ref[:, at], False)
        carried = dot(g, s_ref[at, :], 1, 1)
        o_ref[:half, at] = (first + carried[:half]).astype(BF)
        o_ref[half:, at] = (second + carried[half:]).astype(BF)


def query_grad_of(g, v, k, state, head):
    tok, width = g.shape
    step = 2 * head
    spec = pl.BlockSpec((tok, step), lambda i: (0, i))
    return pl.pallas_call(
        functools.partial(query_kernel, head),
        grid=(width // step,),
        in_specs=[spec, spec, spec, pl.BlockSpec((step, head), lambda i: (i, 0))],
        out_specs=spec,
        out_shape=jax.ShapeDtypeStruct((tok, width), BF),
        compiler_params=params(),
        cost_estimate=cost(4 * tok * tok * width, 8 * tok * width),
        name="query_grad",
    )(g, v, k, state)


def key_value_kernel(head, q_ref, k_ref, v_ref, g_ref, a_ref, ko_ref, vo_ref):
    half = g_ref.shape[0] // 2
    for j in range(g_ref.shape[1] // head):
        at = slice(j * head, (j + 1) * head)
        q, k, v, g, adj = q_ref[:, at], k_ref[:, at], v_ref[:, at], g_ref[:, at], a_ref[at, :]
        first, second = causal_apply(v, g, q, True)
        carried = dot(v, adj, 1, 1)
        ko_ref[:half, at] = (first + carried[:half]).astype(BF)
        ko_ref[half:, at] = (second + carried[half:]).astype(BF)
        first, second = causal_apply(k, q, g, True)
        carried = dot(k, adj, 1, 0)
        vo_ref[:half, at] = (first + carried[:half]).astype(BF)
        vo_ref[half:, at] = (second + carried[half:]).astype(BF)


def key_value_grad_of(q, k, v, g, adjoint, head):
    tok, width = g.shape
    step = 2 * head
    spec = pl.BlockSpec((tok, step), lambda i: (0, i))
    shape = jax.ShapeDtypeStruct((tok, width), BF)
    return pl.pallas_call(
        functools.partial(key_value_kernel, head),
        grid=(width // step,),
        in_specs=[spec, spec, spec, spec, pl.BlockSpec((step, head), lambda i: (i, 0))],
        out_specs=[spec, spec],
        out_shape=[shape, shape],
        compiler_params=params(),
        cost_estimate=cost(8 * tok * tok * width, 12 * tok * width),
        name="key_value_grad",
    )(q, k, v, g, adjoint)


ANY = pl.BlockSpec(memory_space=pl.ANY)


def scan_kernel(n, reverse, waits, x_ref, start_ref, *refs):
    o_ref = refs[waits]
    rows = start_ref.shape[0]
    total = start_ref[...]
    for i in range(n):
        c = n - 1 - i if reverse else i
        at = slice(c * rows, (c + 1) * rows)
        o_ref[at, :] = total.astype(BF)
        total = total + x_ref[at, :].astype(F32)


def scan_blocks(x, start, n, reverse, after=(), passed=None):
    more = () if passed is None else (passed,)
    out = pl.pallas_call(
        functools.partial(scan_kernel, n, reverse, len(after) + len(more)),
        in_specs=[pl.BlockSpec(x.shape, lambda: (0, 0)), pl.BlockSpec(start.shape, lambda: (0, 0))]
        + [ANY] * (len(after) + len(more)),
        out_specs=[pl.BlockSpec(x.shape, lambda: (0, 0))] + [ANY] * len(more),
        out_shape=[jax.ShapeDtypeStruct(x.shape, BF)]
        + [jax.ShapeDtypeStruct(p.shape, p.dtype) for p in more],
        input_output_aliases={2 + len(after): 1} if more else {},
        compiler_params=params(),
        cost_estimate=cost(0, 0),
        name="scan_blocks",
    )(x, start, *after, *more)
    return out if more else out[0]


def carried(x, start, axis, reverse):
    n = lax.axis_size(axis)
    mine = lax.all_to_all(x, axis, 0, 0, tiled=True)
    return lax.all_to_all(scan_blocks(mine, start, n, reverse), axis, 0, 0, tiled=True)


def pair_sums_kernel(head, me_ref, a_ref, b_ref, mine_ref, send_ref):
    core = me_ref[0] % 2
    for j in range(a_ref.shape[1] // (2 * head)):
        at = slice(j * head, (j + 1) * head)
        for o_ref, side in ((send_ref, 1 - core), (mine_ref, core)):
            pick = lanes(2 * j + side, head)
            o_ref[at, :] = dot(a_ref[:, pick], b_ref[:, pick], 0, 0).astype(BF)


def pair_sums(me, a, b, head):
    tok, width = a.shape
    step = min(4 * head, width)
    spec = pl.BlockSpec((tok, step), lambda i, m: (0, i))
    out = pl.BlockSpec((step // 2, head), lambda i, m: (i, 0))
    shape = jax.ShapeDtypeStruct((width // 2, head), BF)
    return pl.pallas_call(
        functools.partial(pair_sums_kernel, head),
        grid_spec=pltpu.PrefetchScalarGridSpec(
            num_scalar_prefetch=1,
            grid=(width // step,),
            in_specs=[spec] * 2,
            out_specs=[out] * 2,
        ),
        out_shape=[shape] * 2,
        compiler_params=params(),
        cost_estimate=cost(2 * tok * width * head, 4 * tok * width),
        name="pair_sums",
    )(me, a, b)


def pair_intra_kernel(head, waits, me_ref, *refs):
    q_ref, k_ref, v_ref, mine_ref, send_ref = refs[waits:]
    core = me_ref[0] % 2
    half = q_ref.shape[0] // 2
    mine, other = lanes(core, head), lanes(1 - core, head)
    first, second = causal_apply(q_ref[:, other], k_ref[:, other], v_ref[:, other], False)
    send_ref[:half, head:] = first.astype(BF)
    send_ref[half:, head:] = second.astype(BF)
    send_ref[:, :head] = q_ref[:, other]
    first, second = causal_apply(q_ref[:, mine], k_ref[:, mine], v_ref[:, mine], False)
    mine_ref[:half, :] = first.astype(BF)
    mine_ref[half:, :] = second.astype(BF)


def pair_intra(me, after, q, k, v, head):
    tok, width = q.shape
    steps = width // (2 * head)
    spec = pl.BlockSpec((tok, 2 * head), lambda i, m: (0, i))
    return pl.pallas_call(
        functools.partial(pair_intra_kernel, head, len(after)),
        grid_spec=pltpu.PrefetchScalarGridSpec(
            num_scalar_prefetch=1,
            grid=(steps,),
            in_specs=[ANY] * len(after) + [spec] * 3,
            out_specs=[
                pl.BlockSpec((tok, head), lambda i, m: (0, i)),
                pl.BlockSpec((tok, 2 * head), lambda i, m: (0, i)),
            ],
        ),
        out_shape=[
            jax.ShapeDtypeStruct((tok, width // 2), BF),
            jax.ShapeDtypeStruct((tok, width), BF),
        ],
        compiler_params=params(),
        cost_estimate=cost(4 * tok * tok * width, 9 * tok * width),
        name="pair_intra",
    )(me, *after, q, k, v)


def pair_attended_kernel(head, me_ref, after_ref, q0_ref, q1_ref, i_ref, far_ref, s_ref, own_ref, oth_ref, mine_ref, send_ref):
    core = (me_ref[0] % 2).astype(F32)
    south = (me_ref[0] // 2) % 2
    for q_ref, side, o_ref in ((q0_ref, south, mine_ref), (q1_ref, 1 - south, send_ref)):
        rows = lanes(side, head)
        state = s_ref[rows, :].astype(F32)
        near = (state + core * oth_ref[rows, :].astype(F32)).astype(BF)
        away = (state + (1.0 - core) * own_ref[rows, :].astype(F32)).astype(BF)
        here = dot(q_ref[...], near, 1, 0) + i_ref[:, lanes(side, head)].astype(F32)
        there = dot(far_ref[:, lanes(2 * side, head)], away, 1, 0)
        there = there + far_ref[:, lanes(2 * side + 1, head)].astype(F32)
        o_ref[0, 0] = here.astype(BF)
        o_ref[0, 1] = there.astype(BF)


def pair_attended(me, after, q, inner, far, state, own, oth, head):
    tok, width = q.shape
    places = width // (4 * head)

    def place(i, m):
        return (m[0] // 4) ^ i

    rows = pl.BlockSpec((2 * head, head), lambda i, m: (place(i, m), 0))
    out = pl.BlockSpec((1, 2, tok, head), lambda i, m: (i, 0, 0, 0))
    shape = jax.ShapeDtypeStruct((places, 2, tok, head), BF)
    return pl.pallas_call(
        functools.partial(pair_attended_kernel, head),
        grid_spec=pltpu.PrefetchScalarGridSpec(
            num_scalar_prefetch=1,
            grid=(places,),
            in_specs=[
                ANY,
                pl.BlockSpec((tok, head), lambda i, m: (0, 4 * place(i, m) + m[0] % 4)),
                pl.BlockSpec((tok, head), lambda i, m: (0, 4 * place(i, m) + (m[0] % 4 ^ 2))),
                pl.BlockSpec((tok, 2 * head), lambda i, m: (0, place(i, m))),
                pl.BlockSpec((tok, 4 * head), lambda i, m: (0, place(i, m))),
            ]
            + [rows] * 3,
            out_specs=[out, out],
        ),
        out_shape=[shape, shape],
        compiler_params=params(),
        cost_estimate=cost(2 * tok * head * width, 10 * tok * width),
        name="pair_attended",
    )(me, after, q, q, inner, far, state, own, oth)


def quad_weight_kernel(waits, a_ref, b_ref, *refs):
    half, _, tok, head = a_ref.shape
    ins, outs, at_ref = refs[:8], refs[8 + waits : -1], refs[-1]

    @pl.when(pl.program_id(0) == 0)
    def _():
        for i in range(half):
            for k in range(4):
                block = (a_ref if k < 2 else b_ref)[i, k % 2]
                at_ref[i * head : (i + 1) * head, k * tok : (k + 1) * tok] = block.T

    for part in range(2):
        total = None
        for k in range(4):
            term = dot(at_ref[:, k * tok : (k + 1) * tok], ins[2 * k + part][...], 1, 0)
            total = term if total is None else total + term
        for i, o_ref in enumerate(outs):
            o_ref[part] = total[i * head : (i + 1) * head].astype(BF)


def quad_weight(after, a, b, cots, far_side):
    places, _, tok, head = a.shape
    half = places // 2
    feat = cots[0].shape[1]
    step = min(256, feat)
    whole = pl.BlockSpec((half,) + a.shape[1:], lambda i: (far_side, 0, 0, 0))
    return pl.pallas_call(
        functools.partial(quad_weight_kernel, len(after)),
        grid=(feat // step,),
        in_specs=[whole, whole]
        + [pl.BlockSpec((tok, step), lambda i: (0, i))] * 8
        + [ANY] * len(after),
        out_specs=[pl.BlockSpec((2, head, step), lambda i: (0, 0, i))] * half,
        out_shape=[jax.ShapeDtypeStruct((2, head, feat), BF)] * half,
        scratch_shapes=[pltpu.VMEM((half * head, 4 * tok), BF)],
        compiler_params=params(),
        cost_estimate=cost(16 * tok * feat * half * head * far_side, 20 * feat * tok * far_side),
        name="quad_weight",
    )(a, b, *cots, *after)


def final_kernel(tp_ref, *refs):
    total = refs[0][0].astype(F32)
    for r in refs[1:-1]:
        total = total + r[0].astype(F32)
    refs[-1][...] = total


def final_sum(tp, parts):
    _, rows, feat = parts[0].shape
    return pl.pallas_call(
        final_kernel,
        grid_spec=pltpu.PrefetchScalarGridSpec(
            num_scalar_prefetch=1,
            grid=(2,),
            in_specs=[pl.BlockSpec((1, rows, feat), lambda i, t: (i, 0, 0))] * len(parts),
            out_specs=pl.BlockSpec((rows, feat), lambda i, t: (0, i ^ t[0])),
        ),
        out_shape=jax.ShapeDtypeStruct((rows, 2 * feat), F32),
        compiler_params=params(),
        cost_estimate=cost(len(parts) * rows * feat, 20 * rows * feat),
        name="final_sum",
    )(tp, *parts)


def pair_query_kernel(head, me_ref, after_ref, g_ref, v_ref, k_ref, s_ref, kv_ref, t_ref, o_ref):
    core = me_ref[0] % 2
    half = g_ref.shape[0] // 2
    near = (s_ref[...].astype(F32) + core.astype(F32) * kv_ref[...].astype(F32)).astype(BF)
    for j in range(2):
        at = slice(j * head, (j + 1) * head)
        g = g_ref[:, at]
        state = jnp.where(core == j, near, t_ref[...])
        first_half, second_half = causal_apply(g, v_ref[:, at], k_ref[:, at], False)
        over = dot(g, state, 1, 1)
        o_ref[:half, at] = (first_half + over[:half]).astype(BF)
        o_ref[half:, at] = (second_half + over[half:]).astype(BF)


def pair_query_grad(me, after, g, v, k, state, kv, other, head):
    tok, width = g.shape
    spec = pl.BlockSpec((tok, 2 * head), lambda i, m: (0, i))
    rows = pl.BlockSpec((head, head), lambda i, m: (i, 0))
    return pl.pallas_call(
        functools.partial(pair_query_kernel, head),
        grid_spec=pltpu.PrefetchScalarGridSpec(
            num_scalar_prefetch=1,
            grid=(width // (2 * head),),
            in_specs=[ANY, spec, spec, spec, rows, rows, rows],
            out_specs=spec,
        ),
        out_shape=jax.ShapeDtypeStruct((tok, width), BF),
        compiler_params=params(),
        cost_estimate=cost(0, 0),
        name="query_grad",
    )(me, after, g, v, k, state, kv, other)


def pair_grad_kernel(head, me_ref, tp_ref, after_ref, own_ref, far_ref, w_ref, q_ref, g_ref, mine_ref, send_ref, cot_ref):
    feat = own_ref.shape[1]

    @pl.when(pl.program_id(0) == 0)
    def _():
        cot_ref[:, lanes(tp_ref[0], feat)] = own_ref[...]
        cot_ref[:, lanes(1 - tp_ref[0], feat)] = far_ref[...]

    core = me_ref[0] % 2
    g_ref[...] = dot(cot_ref[...], w_ref[...], 1, 1).astype(BF)
    for j in range(g_ref.shape[1] // (2 * head)):
        at = slice(j * head, (j + 1) * head)
        for o_ref, side in ((send_ref, 1 - core), (mine_ref, core)):
            pick = lanes(2 * j + side, head)
            o_ref[at, :] = dot(q_ref[:, pick], g_ref[:, pick], 0, 0).astype(BF)


def pair_grad(me, tp, after, own, far, w, q, head):
    tok, feat = own.shape
    width = q.shape[1]
    step = min(4 * head, width)
    whole = pl.BlockSpec((tok, feat), lambda i, m, t: (0, 0))
    rows = pl.BlockSpec((step // 2, head), lambda i, m, t: (i, 0))
    cols = pl.BlockSpec((tok, step), lambda i, m, t: (0, i))
    sums = jax.ShapeDtypeStruct((width // 2, head), BF)
    return pl.pallas_call(
        functools.partial(pair_grad_kernel, head),
        grid_spec=pltpu.PrefetchScalarGridSpec(
            num_scalar_prefetch=2,
            grid=(width // step,),
            in_specs=[
                ANY,
                whole,
                whole,
                pl.BlockSpec((step, 2 * feat), lambda i, m, t: (i, 0)),
                cols,
            ],
            out_specs=[cols, rows, rows],
            scratch_shapes=[pltpu.VMEM((tok, 2 * feat), BF)],
        ),
        out_shape=[jax.ShapeDtypeStruct((tok, width), BF), sums, sums],
        compiler_params=params(),
        cost_estimate=cost(4 * tok * feat * width, 4 * feat * width + 4 * tok * width),
        name="out_grad",
    )(me, tp, after, own, far, w, q)


def add_kernel(after_ref, a_ref, b_ref, o_ref):
    o_ref[...] = (a_ref[...].astype(F32) + b_ref[...].astype(F32)).astype(BF)


def add_after(after, a, b):
    spec = pl.BlockSpec(a.shape, lambda: (0, 0))
    return pl.pallas_call(
        add_kernel,
        in_specs=[ANY, spec, spec],
        out_specs=spec,
        out_shape=jax.ShapeDtypeStruct(a.shape, BF),
        compiler_params=params(),
        cost_estimate=cost(0, 0),
        name="add_after",
    )(after, a, b)


def pair_key_value_kernel(head, me_ref, after_ref, q_ref, k_ref, v_ref, g_ref, s_ref, qd_ref, t_ref, ko_ref, vo_ref):
    core = me_ref[0] % 2
    half = g_ref.shape[0] // 2
    near = (s_ref[...].astype(F32) + (1 - core).astype(F32) * qd_ref[...].astype(F32)).astype(BF)
    for j in range(2):
        at = slice(j * head, (j + 1) * head)
        q, k, v, g = q_ref[:, at], k_ref[:, at], v_ref[:, at], g_ref[:, at]
        adj = jnp.where(core == j, near, t_ref[...])
        first, second = causal_apply(v, g, q, True)
        over = dot(v, adj, 1, 1)
        ko_ref[:half, at] = (first + over[:half]).astype(BF)
        ko_ref[half:, at] = (second + over[half:]).astype(BF)
        first, second = causal_apply(k, q, g, True)
        over = dot(k, adj, 1, 0)
        vo_ref[:half, at] = (first + over[:half]).astype(BF)
        vo_ref[half:, at] = (second + over[half:]).astype(BF)


def pair_key_value_grad(me, after, q, k, v, g, adjoint, qd, other, head):
    tok, width = g.shape
    spec = pl.BlockSpec((tok, 2 * head), lambda i, m: (0, i))
    rows = pl.BlockSpec((head, head), lambda i, m: (i, 0))
    shape = jax.ShapeDtypeStruct((tok, width), BF)
    return pl.pallas_call(
        functools.partial(pair_key_value_kernel, head),
        grid_spec=pltpu.PrefetchScalarGridSpec(
            num_scalar_prefetch=1,
            grid=(width // (2 * head),),
            in_specs=[ANY, spec, spec, spec, spec, rows, rows, rows],
            out_specs=[spec, spec],
        ),
        out_shape=[shape, shape],
        compiler_params=params(),
        cost_estimate=cost(0, 0),
        name="key_value_grad",
    )(me, after, q, k, v, g, adjoint, qd, other)


def local_paired(queries, keys, values, cotangent, out_weight, memory):
    head = memory.shape[2]
    n = lax.axis_size("ctx")
    me, tp = lax.axis_index("ctx"), lax.axis_index("tp")
    who, which = me.reshape(1), tp.reshape(1)
    core = (me % 2).astype(F32)
    groups = [[c for c in range(n) if c % 2 == side] for side in range(2)]

    def swap(x, bit):
        return lax.ppermute(x, "ctx", [(c, c ^ bit) for c in range(n)])

    def swap_tp(x):
        return lax.ppermute(x, "tp", [(0, 1), (1, 0)])

    def across(x):
        return lax.all_to_all(x, "ctx", 0, 0, axis_index_groups=groups, tiled=True)

    def added(x, factor, y):
        return (x.astype(F32) + factor * y.astype(F32)).astype(BF)

    far = swap_tp(cotangent)
    south = swap(cotangent, 2)

    kv_mine, kv_send = pair_sums(who, keys, values, head)
    kv_other = swap(kv_send, 1)
    chip = added(kv_mine, 1.0, kv_other)
    inner, sent = pair_intra(who, (chip,), queries, keys, values, head)
    start = lax.dynamic_index_in_dim(memory, me, 0, False)
    scanned, sent = scan_blocks(across(chip), start, n // 2, False, (inner, far, south), sent)
    state = across(scanned)

    far_south = swap_tp(south)
    grad, qd_mine, qd_send = pair_grad(who, which, scanned, cotangent, far, out_weight, queries, head)
    mine, send = pair_attended(who, grad, queries, inner, swap(sent, 1), state, kv_mine, kv_other, head)
    received = swap(send, 2)
    state_other = swap(added(state, 1.0 - core, kv_mine), 1)

    qd_other = swap(qd_send, 1)
    chip = add_after(send, qd_mine, qd_other)
    query_g = pair_query_grad(who, chip, grad, values, keys, state, kv_other, state_other, head)
    scanned, far_south = scan_blocks(
        across(chip), jnp.zeros_like(start), n // 2, True, (query_g, received), far_south
    )
    after_chip = across(scanned)
    cots = [cotangent, far, swap(cotangent, 1), swap(far, 1)]
    cots += [south, far_south, swap(south, 1), swap(far_south, 1)]

    crossing = quad_weight((scanned,), mine, received, cots, 1)
    crossed = swap(added(crossing[0], 1.0, swap(crossing[1], 4)), 8)
    same = quad_weight((crossing[0],), mine, received, cots, 0)
    neighbour = swap(same[1], 4)
    adjoint_other = swap(added(after_chip, core, qd_mine), 1)
    key_g, value_g = pair_key_value_grad(
        who, same[0], queries, keys, values, grad, after_chip, qd_other, adjoint_other, head
    )
    return query_g, key_g, value_g, final_sum(which, [same[0], neighbour, crossed])


def local_any(queries, keys, values, cotangent, out_weight, memory):
    head = memory.shape[2]
    width = queries.shape[1]
    feat = cotangent.shape[1]
    n = lax.axis_size("ctx")
    rows = width // n
    me, tp = lax.axis_index("ctx"), lax.axis_index("tp")

    far = lax.ppermute(cotangent, "tp", [(0, 1), (1, 0)])
    kv = block_sums(keys, values, head)
    start = lax.dynamic_slice_in_dim(memory.reshape(width, head), me * rows, rows, 0)
    state = carried(kv, start, "ctx", False)
    inner = intra(queries, keys, values, head)
    grad, qd = out_grad_and_sums(tp.reshape(1), cotangent, far, out_weight, queries, head)
    adjoint = carried(qd, jnp.zeros_like(start), "ctx", True)
    attended = attended_of(queries, state, inner, head)
    term = weight_term(attended, cotangent, far)
    total = lax.psum_scatter(term, "ctx", scatter_dimension=0, tiled=True)
    query_g = query_grad_of(grad, values, keys, state, head)
    key_g, value_g = key_value_grad_of(queries, keys, values, grad, adjoint, head)
    total = total.astype(F32)
    total = jnp.where(tp == 0, total, jnp.concatenate([total[:, feat:], total[:, :feat]], 1))
    return query_g, key_g, value_g, total


def local(*args):
    heads = args[5].shape[0]
    n = lax.axis_size("ctx")
    if n == heads == 16 and lax.axis_size("tp") == 2:
        return local_paired(*args)
    return local_any(*args)


def solution(mesh):
    in_specs = (
        P("ctx", "tp"),
        P("ctx", "tp"),
        P("ctx", "tp"),
        P("ctx", "tp"),
        P("tp", None),
        P("tp", None, None),
    )
    out_specs = (P("ctx", "tp"), P("ctx", "tp"), P("ctx", "tp"), P(("tp", "ctx"), None))
    return jax.shard_map(local, mesh=mesh, in_specs=in_specs, out_specs=out_specs, check_vma=False)
```

profile of v0, /device:TPU:0, one launch (start us, length us, event | category | flops | bytes accessed | tf_op | source)
XLA Modules:
  0.0 142.3 jit_solution(9119151158502487910)
XLA Ops:
  0.6 3.0 %collective-permute-start.2 = (bf16[512,1024]{1,0:T(8,128)(2,1)}, bf16[512,1024]{1,0:T(8,128)(2,1)S(1)}, u32[]{:S(2)}, u32[]{:S(2)}) collective-permute-start(bf16[512,1024]{1,0:T(8,128)(2,1)} %refs_0_.3), channel_id=1, source_target_pairs={{0,4},{2,6},{4,0},{6,2},{8,12},{10,14},{12,8},{14,10},{16,20},{18,... | collective-permute-start | bytes 3145736 | tf_op jit(solution)/shard_map/ppermute | solution.py:612
  3.7 1.5 %collective-permute-start.1 = (bf16[512,1024]{1,0:T(8,128)(2,1)}, bf16[512,1024]{1,0:T(8,128)(2,1)S(1)}, u32[]{:S(2)}, u32[]{:S(2)}) collective-permute-start(bf16[512,1024]{1,0:T(8,128)(2,1)} %refs_0_.3), channel_id=1, source_target_pairs={{0,1},{1,0},{2,3},{3,2},{4,5},{5,4},{6,7},{7,6},{8,9},{9,8},{10,11... | collective-permute-start | bytes 3145736 | tf_op jit(solution)/shard_map/ppermute | solution.py:615
  5.2 4.5 %pair_sums.1 = (bf16[1024,128]{1,0:T(8,128)(2,1)}, bf16[1024,128]{1,0:T(8,128)(2,1)}) custom-call(s32[1]{0:T(128)} %bitcast.me_ref, bf16[512,2048]{1,0:T(8,128)(2,1)} %k_ref.3, bf16[512,2048]{1,0:T(8,128)(2,1)} %v_ref.3), custom_call_target="tpu_custom_call" | custom-call | flops 268435456 | bytes 4194304 | tf_op jit(solution)/shard_map/pair_sums/pallas_call | solution.py:302
  9.6 1.7 %collective-permute-done.oth_ref.kv_ref = bf16[1024,128]{1,0:T(8,128)(2,1)S(1)} collective-permute-done((bf16[1024,128]{1,0:T(8,128)(2,1)}, bf16[1024,128]{1,0:T(8,128)(2,1)S(1)}, u32[]{:S(2)}, u32[]{:S(2)}) %collective-permute-start) | collective-permute-done | bytes 262176 | tf_op jit(solution)/shard_map/ppermute | solution.py:612
  11.4 1.8 %fusion.refs_0_ = bf16[1024,128]{1,0:T(8,128)(2,1)} fusion(bf16[1024,128]{1,0:T(8,128)(2,1)} %get-tuple-element.23.own_ref, bf16[1024,128]{1,0:T(8,128)(2,1)S(1)} %collective-permute-done.oth_ref.kv_ref), kind=kLoop, calls=%fused_computation.3 | loop fusion | flops 524288 | bytes 786432 | tf_op jit(solution)/shard_map/convert_element_type | solution.py:621
  13.2 4.9 %all-to-all-start = ((bf16[8,128,128]{2,1,0:T(8,128)(2,1)}), bf16[8,128,128]{2,1,0:T(8,128)(2,1)}, u32[]{:S(2)}, u32[]{:S(2)}) async-start(bf16[8,128,128]{2,1,0:T(8,128)(2,1)} %bitcast.18), calls=%async_computation | async-start | bytes 524288 | tf_op jit(solution)/shard_map/all_to_all | solution.py:618
  18.1 0.6 dynamic-slice_bitcast_fusion.start_ref
  18.7 10.1 %pair_intra.1 = (bf16[512,1024]{1,0:T(8,128)(2,1)}, bf16[512,2048]{1,0:T(8,128)(2,1)}) custom-call(s32[1]{0:T(128)} %bitcast.me_ref, bf16[1024,128]{1,0:T(8,128)(2,1)} %fusion.refs_0_, bf16[512,2048]{1,0:T(8,128)(2,1)} %q_ref.3, bf16[512,2048]{1,0:T(8,128)(2,1)} %k_ref.3, bf16[512,2048]{1,0:T(8,128)(2,1)} %v_ref.3), custom_call_target="tpu_custom_call" | custom-call | flops 2147483648 | bytes 9437184 | tf_op jit(solution)/shard_map/pair_intra/pallas_call | solution.py:335
  28.8 1.2 all-to-all-done
  30.0 1.0 copy-done.3
  31.0 0.3 copy-done.4
  31.3 1.7 %scan_blocks.2 = (bf16[1024,128]{1,0:T(8,128)(2,1)}, bf16[512,2048]{1,0:T(8,128)(2,1)}) custom-call(bf16[1024,128]{1,0:T(8,128)(2,1)} %bitcast.3.x_ref, f32[128,128]{1,0:T(8,128)} %dynamic-slice_bitcast_fusion.start_ref, bf16[512,1024]{1,0:T(8,128)(2,1)} %get-tuple-element.25.refs_0_.i_ref, ...), custom_call_target="tpu_custom_call", output_to_operand_aliasing={{1}: (5, {})} | custom-call | tf_op jit(solution)/shard_map/scan_blocks/pallas_call | solution.py:266
  33.0 6.1 %all-to-all-start.1 = ((bf16[8,128,128]{2,1,0:T(8,128)(2,1)}), bf16[8,128,128]{2,1,0:T(8,128)(2,1)S(1)}, u32[]{:S(2)}, u32[]{:S(2)}) async-start(bf16[8,128,128]{2,1,0:T(8,128)(2,1)} %bitcast.19), calls=%async_computation.1 | async-start | bytes 524288 | tf_op jit(solution)/shard_map/all_to_all | solution.py:618
  39.1 1.5 %collective-permute-start.9 = (bf16[512,1024]{1,0:T(8,128)(2,1)}, bf16[512,1024]{1,0:T(8,128)(2,1)S(1)}, u32[]{:S(2)}, u32[]{:S(2)}) collective-permute-start(bf16[512,1024]{1,0:T(8,128)(2,1)} %copy-done.3), channel_id=1, source_target_pairs={{0,1},{1,0},{2,3},{3,2},{4,5},{5,4},{6,7},{7,6},{8,9},{9,8},{10,11... | collective-permute-start | bytes 3145736 | tf_op jit(solution)/shard_map/ppermute | solution.py:615
  40.5 9.8 %out_grad.1 = (bf16[512,2048]{1,0:T(8,128)(2,1)}, bf16[1024,128]{1,0:T(8,128)(2,1)}, bf16[1024,128]{1,0:T(8,128)(2,1)}) custom-call(s32[1]{0:T(128)} %bitcast.me_ref, s32[1]{0:T(128)} %bitcast.1.tp_ref, bf16[1024,128]{1,0:T(8,128)(2,1)} %get-tuple-element.27.after_ref, bf16[512,1024]{1,0:T(8,128)(2,1)} %refs_0_.3, bf16[512,1024]{1,0:T(8,128)(2,1)} %copy-done.4, ...), custom_call_target="tpu_custom_call" | custom-call | flops 4294967296 | bytes 12582912 | tf_op jit(solution)/shard_map/out_grad/pallas_call | solution.py:526
  50.3 0.7 copy-done.5
  51.1 4.6 %pair_attended.1 = (bf16[4,2,512,128]{3,2,1,0:T(8,128)(2,1)}, bf16[4,2,512,128]{3,2,1,0:T(8,128)(2,1)}) custom-call(s32[1]{0:T(128)} %bitcast.me_ref, bf16[512,2048]{1,0:T(8,128)(2,1)} %get-tuple-element.28.after_ref.g_ref, bf16[512,2048]{1,0:T(8,128)(2,1)} %q_ref.3, bf16[512,2048]{1,0:T(8,128)(2,1)} %q_ref.3, ...), custom_call_target="tpu_custom_call" | custom-call | flops 268435456 | bytes 10485760 | tf_op jit(solution)/shard_map/pair_attended/pallas_call | solution.py:381
  55.7 2.1 %collective-permute-start.6 = (bf16[4,2,512,128]{3,2,1,0:T(8,128)(2,1)}, bf16[4,2,512,128]{3,2,1,0:T(8,128)(2,1)S(1)}, u32[]{:S(2)}, u32[]{:S(2)}) collective-permute-start(bf16[4,2,512,128]{3,2,1,0:T(8,128)(2,1)} %get-tuple-element.30.after_ref), channel_id=1, source_target_pairs={{0,4},{2,6},{4,0},{6,2},{8,12},{10,14},{12,8},{14,10},{16,20},{18,... | collective-permute-start | bytes 3145736 | tf_op jit(solution)/shard_map/ppermute | solution.py:612
  57.8 1.9 %collective-permute-done.4.b_ref.qd_ref = bf16[1024,128]{1,0:T(8,128)(2,1)} collective-permute-done((bf16[1024,128]{1,0:T(8,128)(2,1)}, bf16[1024,128]{1,0:T(8,128)(2,1)}, u32[]{:S(2)}, u32[]{:S(2)}) %collective-permute-start.4) | collective-permute-done | bytes 262176 | tf_op jit(solution)/shard_map/ppermute | solution.py:612
  59.7 1.8 %add_after.1.after_ref = bf16[1024,128]{1,0:T(8,128)(2,1)} custom-call(bf16[4,2,512,128]{3,2,1,0:T(8,128)(2,1)} %get-tuple-element.30.after_ref, bf16[1024,128]{1,0:T(8,128)(2,1)} %get-tuple-element.31.a_ref, bf16[1024,128]{1,0:T(8,128)(2,1)} %collective-permute-done.4.b_ref.qd_ref), custom_call_target="tpu_custom_call" | custom-call | tf_op jit(solution)/shard_map/add_after/pallas_call | solution.py:554
  61.5 4.5 %all-to-all-start.2 = ((bf16[8,128,128]{2,1,0:T(8,128)(2,1)}), bf16[8,128,128]{2,1,0:T(8,128)(2,1)}, u32[]{:S(2)}, u32[]{:S(2)}) async-start(bf16[8,128,128]{2,1,0:T(8,128)(2,1)} %bitcast.16), calls=%async_computation.2 | async-start | bytes 524288 | tf_op jit(solution)/shard_map/all_to_all | solution.py:618
  66.0 1.0 fusion.2
  67.1 0.5 collective-permute-start.7
  67.7 0.9 collective-permute-done.5.t_ref
  68.8 0.6 copy-done.14
  69.4 9.9 %query_grad.1.refs_0_ = bf16[512,2048]{1,0:T(8,128)(2,1)} custom-call(s32[1]{0:T(128)} %bitcast.me_ref, bf16[1024,128]{1,0:T(8,128)(2,1)} %add_after.1.after_ref, bf16[512,2048]{1,0:T(8,128)(2,1)} %get-tuple-element.28.after_ref.g_ref, bf16[512,2048]{1,0:T(8,128)(2,1)} %v_ref.3, bf16[512,2048]{1,0:T(8,128)(2,1)} %k_ref.3, bf16[1024,128]{1,0:T(8,128)(2,1)} %bitcast.15, ...), custom_call_target="tpu_custom_call" | custom-call | tf_op jit(solution)/shard_map/query_grad/pallas_call | solution.py:486
  79.3 4.6 %all-to-all-done.2 = bf16[8,128,128]{2,1,0:T(8,128)(2,1)} async-done(((bf16[8,128,128]{2,1,0:T(8,128)(2,1)}), bf16[8,128,128]{2,1,0:T(8,128)(2,1)}, u32[]{:S(2)}, u32[]{:S(2)}) %all-to-all-start.2) | async-done | bytes 262176 | tf_op jit(solution)/shard_map/all_to_all | solution.py:618
  83.9 0.7 broadcast_in_dim.3.start_ref
  84.6 0.3 copy-done.1
  84.9 1.7 %scan_blocks.3 = (bf16[1024,128]{1,0:T(8,128)(2,1)}, bf16[512,1024]{1,0:T(8,128)(2,1)}) custom-call(bf16[1024,128]{1,0:T(8,128)(2,1)} %bitcast.8.x_ref, f32[128,128]{1,0:T(8,128)} %broadcast_in_dim.3.start_ref, bf16[512,2048]{1,0:T(8,128)(2,1)} %query_grad.1.refs_0_, bf16[4,2,512,128]{3,2,1,0:T(8,128)(2,1)} %copy-done.1, ...), custom_call_target="tpu_custom_call", output_to_operand_aliasing={{1}: (4, {})} | custom-call | tf_op jit(solution)/shard_map/scan_blocks/pallas_call | solution.py:266
  86.6 2.8 %collective-permute-done.11.refs_7_ = bf16[512,1024]{1,0:T(8,128)(2,1)S(1)} collective-permute-done((bf16[512,1024]{1,0:T(8,128)(2,1)}, bf16[512,1024]{1,0:T(8,128)(2,1)S(1)}, u32[]{:S(2)}, u32[]{:S(2)}) %collective-permute-start.11) | collective-permute-done | bytes 1048608 | tf_op jit(solution)/shard_map/ppermute | solution.py:612
  89.5 1.0 copy-done.7
  90.4 7.1 %quad_weight.2 = (bf16[2,128,1024]{2,1,0:T(8,128)(2,1)}, bf16[2,128,1024]{2,1,0:T(8,128)(2,1)}) custom-call(bf16[4,2,512,128]{3,2,1,0:T(8,128)(2,1)} %get-tuple-element.33.a_ref, bf16[4,2,512,128]{3,2,1,0:T(8,128)(2,1)} %copy-done.1, bf16[512,1024]{1,0:T(8,128)(2,1)} %refs_0_.3, bf16[512,1024]{1,0:T(8,128)(2,1)} %copy-done.4, ...), custom_call_target="tpu_custom_call" | custom-call | flops 2147483648 | bytes 10485760 | tf_op jit(solution)/shard_map/quad_weight/pallas_call | solution.py:429
  97.5 1.8 %collective-permute-start.14 = (bf16[2,128,1024]{2,1,0:T(8,128)(2,1)}, bf16[2,128,1024]{2,1,0:T(8,128)(2,1)S(1)}, u32[]{:S(2)}, u32[]{:S(2)}) collective-permute-start(bf16[2,128,1024]{2,1,0:T(8,128)(2,1)} %get-tuple-element.41), channel_id=1, source_target_pairs={{0,8},{2,10},{4,12},{6,14},{8,0},{10,2},{12,4},{14,6},{16,24},{18,... | collective-permute-start | bytes 1572872 | tf_op jit(solution)/shard_map/ppermute | solution.py:612
  99.3 4.6 %all-to-all-start.3 = ((bf16[8,128,128]{2,1,0:T(8,128)(2,1)}), bf16[8,128,128]{2,1,0:T(8,128)(2,1)S(1)}, u32[]{:S(2)}, u32[]{:S(2)}) async-start(bf16[8,128,128]{2,1,0:T(8,128)(2,1)} %bitcast.9), calls=%async_computation.3 | async-start | bytes 524288 | tf_op jit(solution)/shard_map/all_to_all | solution.py:618
  103.9 7.2 %quad_weight.3 = (bf16[2,128,1024]{2,1,0:T(8,128)(2,1)}, bf16[2,128,1024]{2,1,0:T(8,128)(2,1)}) custom-call(bf16[4,2,512,128]{3,2,1,0:T(8,128)(2,1)} %get-tuple-element.33.a_ref, bf16[4,2,512,128]{3,2,1,0:T(8,128)(2,1)} %copy-done.1, bf16[512,1024]{1,0:T(8,128)(2,1)} %refs_0_.3, bf16[512,1024]{1,0:T(8,128)(2,1)} %copy-done.4, ...), custom_call_target="tpu_custom_call" | custom-call | tf_op jit(solution)/shard_map/quad_weight/pallas_call | solution.py:429
  111.1 2.1 %collective-permute-start.13 = (bf16[2,128,1024]{2,1,0:T(8,128)(2,1)}, bf16[2,128,1024]{2,1,0:T(8,128)(2,1)S(1)}, u32[]{:S(2)}, u32[]{:S(2)}) collective-permute-start(bf16[2,128,1024]{2,1,0:T(8,128)(2,1)} %get-tuple-element.40), channel_id=1, source_target_pairs={{0,8},{2,10},{4,12},{6,14},{8,0},{10,2},{12,4},{14,6},{16,24},{18,... | collective-permute-start | bytes 1572872 | tf_op jit(solution)/shard_map/ppermute | solution.py:612
  113.1 1.1 collective-permute-done.14
  114.2 0.2 add_convert_fusion
  114.4 2.8 %collective-permute-start.15 = (bf16[2,128,1024]{2,1,0:T(8,128)(2,1)S(1)}, bf16[2,128,1024]{2,1,0:T(8,128)(2,1)S(1)}, u32[]{:S(2)}, u32[]{:S(2)}) collective-permute-start(bf16[2,128,1024]{2,1,0:T(8,128)(2,1)S(1)} %add_convert_fusion), channel_id=1, source_target_pairs={{0,16},{2,18},{4,20},{6,22},{8,24},{10,26},{12,28},{14,30},{16,0},... | collective-permute-start | bytes 1572872 | tf_op jit(solution)/shard_map/ppermute | solution.py:612
  117.2 1.9 %all-to-all-done.3 = bf16[8,128,128]{2,1,0:T(8,128)(2,1)S(1)} async-done(((bf16[8,128,128]{2,1,0:T(8,128)(2,1)}), bf16[8,128,128]{2,1,0:T(8,128)(2,1)S(1)}, u32[]{:S(2)}, u32[]{:S(2)}) %all-to-all-start.3) | async-done | bytes 262176 | tf_op jit(solution)/shard_map/all_to_all | solution.py:618
  119.3 1.5 %collective-permute-done.12.t_ref = bf16[1024,128]{1,0:T(8,128)(2,1)S(1)} collective-permute-done((bf16[1024,128]{1,0:T(8,128)(2,1)S(1)}, bf16[1024,128]{1,0:T(8,128)(2,1)S(1)}, u32[]{:S(2)}, u32[]{:S(2)}) %collective-permute-start.12) | collective-permute-done | bytes 262176 | tf_op jit(solution)/shard_map/ppermute | solution.py:612
  120.9 0.7 copy-done.15
  121.6 14.1 %key_value_grad.1 = (bf16[512,2048]{1,0:T(8,128)(2,1)}, bf16[512,2048]{1,0:T(8,128)(2,1)}) custom-call(s32[1]{0:T(128)} %bitcast.me_ref, bf16[2,128,1024]{2,1,0:T(8,128)(2,1)} %get-tuple-element.37.after_ref.refs_0_, bf16[512,2048]{1,0:T(8,128)(2,1)} %q_ref.3, bf16[512,2048]{1,0:T(8,128)(2,1)} %k_ref.3, bf16[512,2048]{1,0:T(8,128)(2,1)} %v_ref.3, ...), custom_call_target="tpu_custom_call" | custom-call | tf_op jit(solution)/shard_map/key_value_grad/pallas_call | solution.py:588
  135.6 2.8 %collective-permute-done.13.refs_1_ = bf16[2,128,1024]{2,1,0:T(8,128)(2,1)S(1)} collective-permute-done((bf16[2,128,1024]{2,1,0:T(8,128)(2,1)}, bf16[2,128,1024]{2,1,0:T(8,128)(2,1)S(1)}, u32[]{:S(2)}, u32[]{:S(2)}) %collective-permute-start.13) | collective-permute-done | bytes 524320 | tf_op jit(solution)/shard_map/ppermute | solution.py:612
  138.5 0.8 copy-done.12
  139.3 0.8 copy-done.13
  140.1 2.2 %final_sum.1 = f32[128,2048]{1,0:T(8,128)} custom-call(s32[1]{0:T(128)} %bitcast.1.tp_ref, bf16[2,128,1024]{2,1,0:T(8,128)(2,1)} %get-tuple-element.37.after_ref.refs_0_, bf16[2,128,1024]{2,1,0:T(8,128)(2,1)} %copy-done.12, bf16[2,128,1024]{2,1,0:T(8,128)(2,1)} %copy-done.13), custom_call_target="tpu_custom_call" | custom-call | flops 393216 | bytes 2621440 | tf_op jit(solution)/shard_map/final_sum/pallas_call | solution.py:453
  (42 shorter events, 0.5 us)
Async XLA Ops:
  0.6 17.4 %copy-start = (f32[16,128,128]{2,1,0:T(8,128)S(1)}, f32[16,128,128]{2,1,0:T(8,128)}, u32[]{:S(2)}) copy-start(f32[16,128,128]{2,1,0:T(8,128)} %param.11) | copy-start | bytes 3145732
  0.6 29.3 %collective-permute-start.2 = (bf16[512,1024]{1,0:T(8,128)(2,1)}, bf16[512,1024]{1,0:T(8,128)(2,1)S(1)}, u32[]{:S(2)}, u32[]{:S(2)}) collective-permute-start(bf16[512,1024]{1,0:T(8,128)(2,1)} %refs_0_.3), channel_id=1, source_target_pairs={{0,4},{2,6},{4,0},{6,2},{8,12},{10,14},{12,8},{14,10},{16,20},{18,... | collective-permute-start | bytes 3145736 | tf_op jit(solution)/shard_map/ppermute | solution.py:612
  3.7 26.3 %collective-permute-start.1 = (bf16[512,1024]{1,0:T(8,128)(2,1)}, bf16[512,1024]{1,0:T(8,128)(2,1)S(1)}, u32[]{:S(2)}, u32[]{:S(2)}) collective-permute-start(bf16[512,1024]{1,0:T(8,128)(2,1)} %refs_0_.3), channel_id=1, source_target_pairs={{0,1},{1,0},{2,3},{3,2},{4,5},{5,4},{6,7},{7,6},{8,9},{9,8},{10,11... | collective-permute-start | bytes 3145736 | tf_op jit(solution)/shard_map/ppermute | solution.py:615
  9.6 1.7 %collective-permute-start = (bf16[1024,128]{1,0:T(8,128)(2,1)}, bf16[1024,128]{1,0:T(8,128)(2,1)S(1)}, u32[]{:S(2)}, u32[]{:S(2)}) collective-permute-start(bf16[1024,128]{1,0:T(8,128)(2,1)} %get-tuple-element.24), channel_id=1, source_target_pairs={{0,2},{2,0},{4,6},{6,4},{8,10},{10,8},{12,14},{14,12},{16,18},{18,... | collective-permute-start | bytes 786440 | tf_op jit(solution)/shard_map/ppermute | solution.py:612
  11.4 17.4 %copy-start.8 = (bf16[1024,128]{1,0:T(8,128)(2,1)}, bf16[1024,128]{1,0:T(8,128)(2,1)S(1)}, u32[]{:S(2)}) copy-start(bf16[1024,128]{1,0:T(8,128)(2,1)S(1)} %collective-permute-done.oth_ref.kv_ref) | copy-start | bytes 786436
  13.2 16.8 %all-to-all-start = ((bf16[8,128,128]{2,1,0:T(8,128)(2,1)}), bf16[8,128,128]{2,1,0:T(8,128)(2,1)}, u32[]{:S(2)}, u32[]{:S(2)}) async-start(bf16[8,128,128]{2,1,0:T(8,128)(2,1)} %bitcast.18), calls=%async_computation | async-start | bytes 524288 | tf_op jit(solution)/shard_map/all_to_all | solution.py:618
  30.0 1.0 copy-start.3
  30.0 1.3 copy-start.4
  33.0 17.3 %collective-permute-start.3 = (bf16[512,2048]{1,0:T(8,128)(2,1)}, bf16[512,2048]{1,0:T(8,128)(2,1)}, u32[]{:S(2)}, u32[]{:S(2)}) collective-permute-start(bf16[512,2048]{1,0:T(8,128)(2,1)} %get-tuple-element.29), channel_id=1, source_target_pairs={{0,2},{2,0},{4,6},{6,4},{8,10},{10,8},{12,14},{14,12},{16,18},{18,... | collective-permute-start | bytes 6291464 | tf_op jit(solution)/shard_map/ppermute | solution.py:612
  33.0 17.3 %all-to-all-start.1 = ((bf16[8,128,128]{2,1,0:T(8,128)(2,1)}), bf16[8,128,128]{2,1,0:T(8,128)(2,1)S(1)}, u32[]{:S(2)}, u32[]{:S(2)}) async-start(bf16[8,128,128]{2,1,0:T(8,128)(2,1)} %bitcast.19), calls=%async_computation.1 | async-start | bytes 524288 | tf_op jit(solution)/shard_map/all_to_all | solution.py:618
  39.1 40.2 %collective-permute-start.9 = (bf16[512,1024]{1,0:T(8,128)(2,1)}, bf16[512,1024]{1,0:T(8,128)(2,1)S(1)}, u32[]{:S(2)}, u32[]{:S(2)}) collective-permute-start(bf16[512,1024]{1,0:T(8,128)(2,1)} %copy-done.3), channel_id=1, source_target_pairs={{0,1},{1,0},{2,3},{3,2},{4,5},{5,4},{6,7},{7,6},{8,9},{9,8},{10,11... | collective-permute-start | bytes 3145736 | tf_op jit(solution)/shard_map/ppermute | solution.py:615
  50.3 0.7 copy-start.5
  55.7 10.3 %copy-start.6 = (bf16[8,128,128]{2,1,0:T(8,128)(2,1)S(1)}, bf16[8,128,128]{2,1,0:T(8,128)(2,1)}, u32[]{:S(2)}) copy-start(bf16[8,128,128]{2,1,0:T(8,128)(2,1)} %copy-done.5) | copy-start | bytes 786436
  55.7 28.2 %collective-permute-start.6 = (bf16[4,2,512,128]{3,2,1,0:T(8,128)(2,1)}, bf16[4,2,512,128]{3,2,1,0:T(8,128)(2,1)S(1)}, u32[]{:S(2)}, u32[]{:S(2)}) collective-permute-start(bf16[4,2,512,128]{3,2,1,0:T(8,128)(2,1)} %get-tuple-element.30.after_ref), channel_id=1, source_target_pairs={{0,4},{2,6},{4,0},{6,2},{8,12},{10,14},{12,8},{14,10},{16,20},{18,... | collective-permute-start | bytes 3145736 | tf_op jit(solution)/shard_map/ppermute | solution.py:612
  57.8 1.9 %collective-permute-start.4 = (bf16[1024,128]{1,0:T(8,128)(2,1)}, bf16[1024,128]{1,0:T(8,128)(2,1)}, u32[]{:S(2)}, u32[]{:S(2)}) collective-permute-start(bf16[1024,128]{1,0:T(8,128)(2,1)} %get-tuple-element.32), channel_id=1, source_target_pairs={{0,2},{2,0},{4,6},{6,4},{8,10},{10,8},{12,14},{14,12},{16,18},{18,... | collective-permute-start | bytes 786440 | tf_op jit(solution)/shard_map/ppermute | solution.py:612
  61.5 22.4 %all-to-all-start.2 = ((bf16[8,128,128]{2,1,0:T(8,128)(2,1)}), bf16[8,128,128]{2,1,0:T(8,128)(2,1)}, u32[]{:S(2)}, u32[]{:S(2)}) async-start(bf16[8,128,128]{2,1,0:T(8,128)(2,1)} %bitcast.16), calls=%async_computation.2 | async-start | bytes 524288 | tf_op jit(solution)/shard_map/all_to_all | solution.py:618
  67.0 1.6 %collective-permute-start.5 = (bf16[1024,128]{1,0:T(8,128)(2,1)S(1)}, bf16[1024,128]{1,0:T(8,128)(2,1)S(1)}, u32[]{:S(2)}, u32[]{:S(2)}) collective-permute-start(bf16[1024,128]{1,0:T(8,128)(2,1)S(1)} %fusion.2), channel_id=1, source_target_pairs={{0,2},{2,0},{4,6},{6,4},{8,10},{10,8},{12,14},{14,12},{16,18},{18,... | collective-permute-start | bytes 786440 | tf_op jit(solution)/shard_map/ppermute | solution.py:612
  67.1 19.5 %collective-permute-start.7 = (bf16[512,1024]{1,0:T(8,128)(2,1)}, bf16[512,1024]{1,0:T(8,128)(2,1)}, u32[]{:S(2)}, u32[]{:S(2)}) collective-permute-start(bf16[512,1024]{1,0:T(8,128)(2,1)} %refs_0_.3), channel_id=1, source_target_pairs={{0,2},{2,0},{4,6},{6,4},{8,10},{10,8},{12,14},{14,12},{16,18},{18,... | collective-permute-start | bytes 3145736 | tf_op jit(solution)/shard_map/ppermute | solution.py:612
  67.6 19.0 %collective-permute-start.10 = (bf16[512,1024]{1,0:T(8,128)(2,1)}, bf16[512,1024]{1,0:T(8,128)(2,1)}, u32[]{:S(2)}, u32[]{:S(2)}) collective-permute-start(bf16[512,1024]{1,0:T(8,128)(2,1)} %copy-done.3), channel_id=1, source_target_pairs={{0,2},{2,0},{4,6},{6,4},{8,10},{10,8},{12,14},{14,12},{16,18},{18,... | collective-permute-start | bytes 3145736 | tf_op jit(solution)/shard_map/ppermute | solution.py:612
  68.6 0.7 copy-start.14
  68.7 18.0 %collective-permute-start.8 = (bf16[512,1024]{1,0:T(8,128)(2,1)}, bf16[512,1024]{1,0:T(8,128)(2,1)}, u32[]{:S(2)}, u32[]{:S(2)}) collective-permute-start(bf16[512,1024]{1,0:T(8,128)(2,1)} %copy-done.4), channel_id=1, source_target_pairs={{0,2},{2,0},{4,6},{6,4},{8,10},{10,8},{12,14},{14,12},{16,18},{18,... | collective-permute-start | bytes 3145736 | tf_op jit(solution)/shard_map/ppermute | solution.py:612
  79.2 5.3 %copy-start.2 = (bf16[512,1024]{1,0:T(8,128)(2,1)}, bf16[512,1024]{1,0:T(8,128)(2,1)S(1)}, u32[]{:S(2)}) copy-start(bf16[512,1024]{1,0:T(8,128)(2,1)S(1)} %collective-permute-done.9.refs_2_) | copy-start | bytes 3145732
  83.9 1.0 copy-start.1
  86.6 2.9 %collective-permute-start.11 = (bf16[512,1024]{1,0:T(8,128)(2,1)}, bf16[512,1024]{1,0:T(8,128)(2,1)S(1)}, u32[]{:S(2)}, u32[]{:S(2)}) collective-permute-start(bf16[512,1024]{1,0:T(8,128)(2,1)} %get-tuple-element.34.refs_5_), channel_id=1, source_target_pairs={{0,2},{2,0},{4,6},{6,4},{8,10},{10,8},{12,14},{14,12},{16,18},{18,... | collective-permute-start | bytes 3145736 | tf_op jit(solution)/shard_map/ppermute | solution.py:612
  89.5 1.0 copy-start.7
  97.5 16.7 %collective-permute-start.14 = (bf16[2,128,1024]{2,1,0:T(8,128)(2,1)}, bf16[2,128,1024]{2,1,0:T(8,128)(2,1)S(1)}, u32[]{:S(2)}, u32[]{:S(2)}) collective-permute-start(bf16[2,128,1024]{2,1,0:T(8,128)(2,1)} %get-tuple-element.41), channel_id=1, source_target_pairs={{0,8},{2,10},{4,12},{6,14},{8,0},{10,2},{12,4},{14,6},{16,24},{18,... | collective-permute-start | bytes 1572872 | tf_op jit(solution)/shard_map/ppermute | solution.py:612
  99.3 19.8 %all-to-all-start.3 = ((bf16[8,128,128]{2,1,0:T(8,128)(2,1)}), bf16[8,128,128]{2,1,0:T(8,128)(2,1)S(1)}, u32[]{:S(2)}, u32[]{:S(2)}) async-start(bf16[8,128,128]{2,1,0:T(8,128)(2,1)} %bitcast.9), calls=%async_computation.3 | async-start | bytes 524288 | tf_op jit(solution)/shard_map/all_to_all | solution.py:618
  103.9 10.3 %copy-start.10 = (bf16[2,128,1024]{2,1,0:T(8,128)(2,1)S(1)}, bf16[2,128,1024]{2,1,0:T(8,128)(2,1)}, u32[]{:S(2)}) copy-start(bf16[2,128,1024]{2,1,0:T(8,128)(2,1)} %get-tuple-element.36.refs_8_) | copy-start | bytes 1572868
  103.9 15.2 %copy-start.11 = (bf16[1024,128]{1,0:T(8,128)(2,1)S(1)}, bf16[1024,128]{1,0:T(8,128)(2,1)}, u32[]{:S(2)}) copy-start(bf16[1024,128]{1,0:T(8,128)(2,1)} %get-tuple-element.31.a_ref) | copy-start | bytes 786436
  111.1 27.4 %collective-permute-start.13 = (bf16[2,128,1024]{2,1,0:T(8,128)(2,1)}, bf16[2,128,1024]{2,1,0:T(8,128)(2,1)S(1)}, u32[]{:S(2)}, u32[]{:S(2)}) collective-permute-start(bf16[2,128,1024]{2,1,0:T(8,128)(2,1)} %get-tuple-element.40), channel_id=1, source_target_pairs={{0,8},{2,10},{4,12},{6,14},{8,0},{10,2},{12,4},{14,6},{16,24},{18,... | collective-permute-start | bytes 1572872 | tf_op jit(solution)/shard_map/ppermute | solution.py:612
  114.4 24.0 %collective-permute-start.15 = (bf16[2,128,1024]{2,1,0:T(8,128)(2,1)S(1)}, bf16[2,128,1024]{2,1,0:T(8,128)(2,1)S(1)}, u32[]{:S(2)}, u32[]{:S(2)}) collective-permute-start(bf16[2,128,1024]{2,1,0:T(8,128)(2,1)S(1)} %add_convert_fusion), channel_id=1, source_target_pairs={{0,16},{2,18},{4,20},{6,22},{8,24},{10,26},{12,28},{14,30},{16,0},... | collective-permute-start | bytes 1572872 | tf_op jit(solution)/shard_map/ppermute | solution.py:612
  119.1 1.7 %copy-start.9 = (bf16[8,128,128]{2,1,0:T(8,128)(2,1)}, bf16[8,128,128]{2,1,0:T(8,128)(2,1)S(1)}, u32[]{:S(2)}) copy-start(bf16[8,128,128]{2,1,0:T(8,128)(2,1)S(1)} %all-to-all-done.3) | copy-start | bytes 786436
  119.2 1.6 %collective-permute-start.12 = (bf16[1024,128]{1,0:T(8,128)(2,1)S(1)}, bf16[1024,128]{1,0:T(8,128)(2,1)S(1)}, u32[]{:S(2)}, u32[]{:S(2)}) collective-permute-start(bf16[1024,128]{1,0:T(8,128)(2,1)S(1)} %add_convert_fusion.1), channel_id=1, source_target_pairs={{0,2},{2,0},{4,6},{6,4},{8,10},{10,8},{12,14},{14,12},{16,18},{18,... | collective-permute-start | bytes 786440 | tf_op jit(solution)/shard_map/ppermute | solution.py:612
  120.8 0.7 copy-start.15
  138.5 0.8 copy-start.12
  139.3 0.8 copy-start.13
where the time goes:
time: 144 us; the launch traced here: 142 us
  Pallas kernels  74.6 us (52%)
  starting transfers between devices  35.6 us (25%)
  waiting for transfers between devices  20.6 us (14%)
  local copies, waits for them, and re-layouts  7.55 us (5%)
  other arithmetic  3.15 us (2%)
    all_to_all x4, starting transfers between devices, across(): return lax.all_to_all(x, 'ctx', 0, 0, axis_index_groups=groups, tiled=True)  20 us
    pallas_call x2, Pallas kernels, quad_weight(): pl.pallas_call(functools.partial(quad_weight_kernel, len(after)), grid=(f...  14.3 us
    pallas_call x1, Pallas kernels, pair_key_value_grad(): pl.pallas_call(functools.partial(pair_key_value_kernel, head), grid_spec=...  14.1 us
    ppermute x14, waiting for transfers between devices, swap(): return lax.ppermute(x, 'ctx', [(c, c ^ bit) for c in range(n)])  12.9 us
    ppermute x14, starting transfers between devices, swap(): return lax.ppermute(x, 'ctx', [(c, c ^ bit) for c in range(n)])  12.6 us
    pallas_call x1, Pallas kernels, pair_intra(): pl.pallas_call(functools.partial(pair_intra_kernel, head, len(after)), gr...  10.1 us
    pallas_call x1, Pallas kernels, pair_query_grad(): pl.pallas_call(functools.partial(pair_query_kernel, head), grid_spec=pltp...  9.89 us
    pallas_call x1, Pallas kernels, pair_grad(): pl.pallas_call(functools.partial(pair_grad_kernel, head), grid_spec=pltpu...  9.76 us
  transfers between devices with their start and end apart: 20, of which 10 were waited for; matrix products, arithmetic and copies ran while one was open for 3% of the time, Pallas kernels for 45%

commit v1 on v0

--- a/solution.py
+++ b/solution.py
@@ -320,12 +320,12 @@
     half = q_ref.shape[0] // 2
     mine, other = lanes(core, head), lanes(1 - core, head)
     first, second = causal_apply(q_ref[:, other], k_ref[:, other], v_ref[:, other], False)
-    send_ref[:half, head:] = first.astype(BF)
-    send_ref[half:, head:] = second.astype(BF)
-    send_ref[:, :head] = q_ref[:, other]
+    send_ref[head:, :half] = first.astype(BF).T
+    send_ref[head:, half:] = second.astype(BF).T
+    send_ref[:head, :] = q_ref[:, other].T
     first, second = causal_apply(q_ref[:, mine], k_ref[:, mine], v_ref[:, mine], False)
-    mine_ref[:half, :] = first.astype(BF)
-    mine_ref[half:, :] = second.astype(BF)
+    mine_ref[:, :half] = first.astype(BF).T
+    mine_ref[:, half:] = second.astype(BF).T
 
 
 def pair_intra(me, after, q, k, v, head):
@@ -339,13 +339,13 @@
             grid=(steps,),
             in_specs=[ANY] * len(after) + [spec] * 3,
             out_specs=[
-                pl.BlockSpec((tok, head), lambda i, m: (0, i)),
-                pl.BlockSpec((tok, 2 * head), lambda i, m: (0, i)),
+                pl.BlockSpec((head, tok), lambda i, m: (i, 0)),
+                pl.BlockSpec((2 * head, tok), lambda i, m: (i, 0)),
             ],
         ),
         out_shape=[
-            jax.ShapeDtypeStruct((tok, width // 2), BF),
-            jax.ShapeDtypeStruct((tok, width), BF),
+            jax.ShapeDtypeStruct((width // 2, tok), BF),
+            jax.ShapeDtypeStruct((width, tok), BF),
         ],
         compiler_params=params(),
         cost_estimate=cost(4 * tok * tok * width, 9 * tok * width),
@@ -361,9 +361,9 @@
         state = s_ref[rows, :].astype(F32)
         near = (state + core * oth_ref[rows, :].astype(F32)).astype(BF)
         away = (state + (1.0 - core) * own_ref[rows, :].astype(F32)).astype(BF)
-        here = dot(q_ref[...], near, 1, 0) + i_ref[:, lanes(side, head)].astype(F32)
-        there = dot(far_ref[:, lanes(2 * side, head)], away, 1, 0)
-        there = there + far_ref[:, lanes(2 * side + 1, head)].astype(F32)
+        here = dot(near, q_ref[...], 0, 1) + i_ref[rows, :].astype(F32)
+        there = dot(away, far_ref[lanes(2 * side, head), :], 0, 0)
+        there = there + far_ref[lanes(2 * side + 1, head), :].astype(F32)
         o_ref[0, 0] = here.astype(BF)
         o_ref[0, 1] = there.astype(BF)
 
@@ -376,8 +376,8 @@
         return (m[0] // 4) ^ i
 
     rows = pl.BlockSpec((2 * head, head), lambda i, m: (place(i, m), 0))
-    out = pl.BlockSpec((1, 2, tok, head), lambda i, m: (i, 0, 0, 0))
-    shape = jax.ShapeDtypeStruct((places, 2, tok, head), BF)
+    out = pl.BlockSpec((1, 2, head, tok), lambda i, m: (i, 0, 0, 0))
+    shape = jax.ShapeDtypeStruct((places, 2, head, tok), BF)
     return pl.pallas_call(
         functools.partial(pair_attended_kernel, head),
         grid_spec=pltpu.PrefetchScalarGridSpec(
@@ -387,8 +387,8 @@
                 ANY,
                 pl.BlockSpec((tok, head), lambda i, m: (0, 4 * place(i, m) + m[0] % 4)),
                 pl.BlockSpec((tok, head), lambda i, m: (0, 4 * place(i, m) + (m[0] % 4 ^ 2))),
-                pl.BlockSpec((tok, 2 * head), lambda i, m: (0, place(i, m))),
-                pl.BlockSpec((tok, 4 * head), lambda i, m: (0, place(i, m))),
+                pl.BlockSpec((2 * head, tok), lambda i, m: (place(i, m), 0)),
+                pl.BlockSpec((4 * head, tok), lambda i, m: (place(i, m), 0)),
             ]
             + [rows] * 3,
             out_specs=[out, out],
@@ -400,69 +400,49 @@
     )(me, after, q, q, inner, far, state, own, oth)
 
 
-def quad_weight_kernel(waits, a_ref, b_ref, *refs):
-    half, _, tok, head = a_ref.shape
-    ins, outs, at_ref = refs[:8], refs[8 + waits : -1], refs[-1]
-
-    @pl.when(pl.program_id(0) == 0)
-    def _():
-        for i in range(half):
-            for k in range(4):
-                block = (a_ref if k < 2 else b_ref)[i, k % 2]
-                at_ref[i * head : (i + 1) * head, k * tok : (k + 1) * tok] = block.T
-
-    for part in range(2):
+def quad_weight_kernel(waits, tp_ref, a_ref, b_ref, *refs):
+    half, _, head, tok = a_ref.shape
+    ins, outs = refs[:8], refs[8 + waits :]
+
+    def product(part):
         total = None
         for k in range(4):
-            term = dot(at_ref[:, k * tok : (k + 1) * tok], ins[2 * k + part][...], 1, 0)
+            block = (a_ref if k < 2 else b_ref)[:, k % 2].reshape(half * head, tok)
+            term = dot(block, ins[2 * k + part][...], 1, 0)
             total = term if total is None else total + term
         for i, o_ref in enumerate(outs):
-            o_ref[part] = total[i * head : (i + 1) * head].astype(BF)
-
-
-def quad_weight(after, a, b, cots, far_side):
-    places, _, tok, head = a.shape
+            o_ref[...] = total[i * head : (i + 1) * head].astype(BF)
+
+    steps = pl.num_programs(0) // 2
+    pl.when(pl.program_id(0) < steps)(lambda: product(0))
+    pl.when(pl.program_id(0) >= steps)(lambda: product(1))
+
+
+def quad_weight(tp, after, a, b, cots, far_side):
+    places, _, head, tok = a.shape
     half = places // 2
     feat = cots[0].shape[1]
-    step = min(256, feat)
-    whole = pl.BlockSpec((half,) + a.shape[1:], lambda i: (far_side, 0, 0, 0))
+    step = min(512, feat)
+    steps = feat // step
+    whole = pl.BlockSpec((half,) + a.shape[1:], lambda i, t: (far_side, 0, 0, 0))
+    own = pl.BlockSpec((tok, step), lambda i, t: (0, jnp.minimum(i, steps - 1)))
+    other = pl.BlockSpec((tok, step), lambda i, t: (0, jnp.maximum(i - steps, 0)))
     return pl.pallas_call(
         functools.partial(quad_weight_kernel, len(after)),
-        grid=(feat // step,),
-        in_specs=[whole, whole]
-        + [pl.BlockSpec((tok, step), lambda i: (0, i))] * 8
-        + [ANY] * len(after),
-        out_specs=[pl.BlockSpec((2, head, step), lambda i: (0, 0, i))] * half,
-        out_shape=[jax.ShapeDtypeStruct((2, head, feat), BF)] * half,
-        scratch_shapes=[pltpu.VMEM((half * head, 4 * tok), BF)],
+        grid_spec=pltpu.PrefetchScalarGridSpec(
+            num_scalar_prefetch=1,
+            grid=(2 * steps,),
+            in_specs=[whole, whole] + [own, other] * 4 + [ANY] * len(after),
+            out_specs=[
+                pl.BlockSpec((head, step), lambda i, t: (0, (i + t[0] * steps) % (2 * steps)))
+            ]
+            * half,
+        ),
+        out_shape=[jax.ShapeDtypeStruct((head, 2 * feat), BF)] * half,
         compiler_params=params(),
         cost_estimate=cost(16 * tok * feat * half * head * far_side, 20 * feat * tok * far_side),
         name="quad_weight",
-    )(a, b, *cots, *after)
-
-
-def final_kernel(tp_ref, *refs):
-    total = refs[0][0].astype(F32)
-    for r in refs[1:-1]:
-        total = total + r[0].astype(F32)
-    refs[-1][...] = total
-
-
-def final_sum(tp, parts):
-    _, rows, feat = parts[0].shape
-    return pl.pallas_call(
-        final_kernel,
-        grid_spec=pltpu.PrefetchScalarGridSpec(
-            num_scalar_prefetch=1,
-            grid=(2,),
-            in_specs=[pl.BlockSpec((1, rows, feat), lambda i, t: (i, 0, 0))] * len(parts),
-            out_specs=pl.BlockSpec((rows, feat), lambda i, t: (0, i ^ t[0])),
-        ),
-        out_shape=jax.ShapeDtypeStruct((rows, 2 * feat), F32),
-        compiler_params=params(),
-        cost_estimate=cost(len(parts) * rows * feat, 20 * rows * feat),
-        name="final_sum",
-    )(tp, *parts)
+    )(tp, a, b, *cots, *after)
 
 
 def pair_query_kernel(head, me_ref, after_ref, g_ref, v_ref, k_ref, s_ref, kv_ref, t_ref, o_ref):
@@ -498,7 +478,9 @@
     )(me, after, g, v, k, state, kv, other)
 
 
-def pair_grad_kernel(head, me_ref, tp_ref, after_ref, own_ref, far_ref, w_ref, q_ref, g_ref, mine_ref, send_ref, cot_ref):
+def pair_grad_kernel(head, waits, me_ref, tp_ref, own_ref, far_ref, w_ref, q_ref, *refs):
+    g_ref, mine_ref, send_ref = refs[waits : waits + 3]
+    cot_ref = refs[-1]
     feat = own_ref.shape[1]
 
     @pl.when(pl.program_id(0) == 0)
@@ -515,34 +497,55 @@
             o_ref[at, :] = dot(q_ref[:, pick], g_ref[:, pick], 0, 0).astype(BF)
 
 
-def pair_grad(me, tp, after, own, far, w, q, head):
+def pair_grad(me, tp, part, after, passed, own, far, w, q, head):
     tok, feat = own.shape
     width = q.shape[1]
-    step = min(4 * head, width)
+    step = min(4 * head, width // 2)
+    base = part * (width // 2 // step)
     whole = pl.BlockSpec((tok, feat), lambda i, m, t: (0, 0))
-    rows = pl.BlockSpec((step // 2, head), lambda i, m, t: (i, 0))
-    cols = pl.BlockSpec((tok, step), lambda i, m, t: (0, i))
+    rows = pl.BlockSpec((step // 2, head), lambda i, m, t: (i + base, 0))
+    cols = pl.BlockSpec((tok, step), lambda i, m, t: (0, i + base))
     sums = jax.ShapeDtypeStruct((width // 2, head), BF)
-    return pl.pallas_call(
-        functools.partial(pair_grad_kernel, head),
+    shapes = [jax.ShapeDtypeStruct((tok, width), BF), sums, sums]
+    shapes += [jax.ShapeDtypeStruct(p.shape, p.dtype) for p in passed[3:]]
+    return pl.pallas_call(
+        functools.partial(pair_grad_kernel, head, len(after) + len(passed)),
         grid_spec=pltpu.PrefetchScalarGridSpec(
             num_scalar_prefetch=2,
-            grid=(width // step,),
+            grid=(width // 2 // step,),
             in_specs=[
-                ANY,
                 whole,
                 whole,
-                pl.BlockSpec((step, 2 * feat), lambda i, m, t: (i, 0)),
+                pl.BlockSpec((step, 2 * feat), lambda i, m, t: (i + base, 0)),
                 cols,
-            ],
-            out_specs=[cols, rows, rows],
+            ]
+            + [ANY] * (len(after) + len(passed)),
+            out_specs=[cols, rows, rows] + [ANY] * len(passed[3:]),
             scratch_shapes=[pltpu.VMEM((tok, 2 * feat), BF)],
         ),
-        out_shape=[jax.ShapeDtypeStruct((tok, width), BF), sums, sums],
-        compiler_params=params(),
-        cost_estimate=cost(4 * tok * feat * width, 4 * feat * width + 4 * tok * width),
+        out_shape=shapes,
+        input_output_aliases={6 + len(after) + i: i for i in range(len(passed))},
+        compiler_params=params(),
+        cost_estimate=cost(2 * tok * feat * width * (1 - part), 3 * feat * width * (1 - part)),
         name="out_grad",
-    )(me, tp, after, own, far, w, q)
+    )(me, tp, own, far, w, q, *after, *passed)
+
+
+def pass_kernel(*refs):
+    pass
+
+
+def passed_after(x, after, flops):
+    return pl.pallas_call(
+        pass_kernel,
+        in_specs=[ANY] * (1 + len(after)),
+        out_specs=ANY,
+        out_shape=jax.ShapeDtypeStruct(x.shape, x.dtype),
+        input_output_aliases={0: 0},
+        compiler_params=params(),
+        cost_estimate=cost(flops, 0),
+        name="passed_after",
+    )(x, *after)
 
 
 def add_kernel(after_ref, a_ref, b_ref, o_ref):
@@ -620,11 +623,10 @@
     def added(x, factor, y):
         return (x.astype(F32) + factor * y.astype(F32)).astype(BF)
 
+    kv_mine, kv_send = pair_sums(who, keys, values, head)
+    kv_other = swap(kv_send, 1)
     far = swap_tp(cotangent)
     south = swap(cotangent, 2)
-
-    kv_mine, kv_send = pair_sums(who, keys, values, head)
-    kv_other = swap(kv_send, 1)
     chip = added(kv_mine, 1.0, kv_other)
     inner, sent = pair_intra(who, (chip,), queries, keys, values, head)
     start = lax.dynamic_index_in_dim(memory, me, 0, False)
@@ -632,30 +634,37 @@
     state = across(scanned)
 
     far_south = swap_tp(south)
-    grad, qd_mine, qd_send = pair_grad(who, which, scanned, cotangent, far, out_weight, queries, head)
-    mine, send = pair_attended(who, grad, queries, inner, swap(sent, 1), state, kv_mine, kv_other, head)
+    early = pair_grad(who, which, 0, (scanned, south), (), cotangent, far, out_weight, queries, head)
+    mine, send = pair_attended(
+        who, early[0], queries, inner, swap(sent, 1), state, kv_mine, kv_other, head
+    )
     received = swap(send, 2)
     state_other = swap(added(state, 1.0 - core, kv_mine), 1)
 
+    grad, qd_mine, qd_send = pair_grad(
+        who, which, 1, (send,), early, cotangent, far, out_weight, queries, head
+    )
     qd_other = swap(qd_send, 1)
     chip = add_after(send, qd_mine, qd_other)
     query_g = pair_query_grad(who, chip, grad, values, keys, state, kv_other, state_other, head)
-    scanned, far_south = scan_blocks(
-        across(chip), jnp.zeros_like(start), n // 2, True, (query_g, received), far_south
+    received = passed_after(received, (query_g,), 2e10)
+    scanned = scan_blocks(
+        across(chip), jnp.zeros_like(start), n // 2, True, (query_g, received)
     )
     after_chip = across(scanned)
     cots = [cotangent, far, swap(cotangent, 1), swap(far, 1)]
     cots += [south, far_south, swap(south, 1), swap(far_south, 1)]
 
-    crossing = quad_weight((scanned,), mine, received, cots, 1)
+    crossing = quad_weight(which, (scanned,), mine, received, cots, 1)
     crossed = swap(added(crossing[0], 1.0, swap(crossing[1], 4)), 8)
-    same = quad_weight((crossing[0],), mine, received, cots, 0)
+    same = quad_weight(which, (crossing[0],), mine, received, cots, 0)
     neighbour = swap(same[1], 4)
     adjoint_other = swap(added(after_chip, core, qd_mine), 1)
     key_g, value_g = pair_key_value_grad(
         who, same[0], queries, keys, values, grad, after_chip, qd_other, adjoint_other, head
     )
-    return query_g, key_g, value_g, final_sum(which, [same[0], neighbour, crossed])
+    total = same[0].astype(F32) + neighbour.astype(F32) + crossed.astype(F32)
+    return query_g, key_g, value_g, total
 
 
 def local_any(queries, keys, values, cotangent, out_weight, memory):

time: 144 us -> 138 us (0.958)
  the two profiles are of different devices: /device:TPU:0 before, /device:TPU:25 now
where the time goes in v1:
time: 138 us; the launch traced here: 137 us
  Pallas kernels  75.7 us (55%)
  starting transfers between devices  43.7 us (32%)
  waiting for transfers between devices  7.79 us (6%)
  local copies, waits for them, and re-layouts  4.86 us (4%)
  other arithmetic  4.04 us (3%)
    ppermute x14, starting transfers between devices, swap(): return lax.ppermute(x, 'ctx', [(c, c ^ bit) for c in range(n)])  21.1 us
    all_to_all x4, starting transfers between devices, across(): return lax.all_to_all(x, 'ctx', 0, 0, axis_index_groups=groups, tiled=True)  20.2 us
    pallas_call x2, Pallas kernels, quad_weight(): pl.pallas_call(functools.partial(quad_weight_kernel, len(after)), grid_sp...  14.2 us
    pallas_call x1, Pallas kernels, pair_key_value_grad(): pl.pallas_call(functools.partial(pair_key_value_kernel, head), grid_spec=...  14.2 us
    pallas_call x2, Pallas kernels, pair_grad(): pl.pallas_call(functools.partial(pair_grad_kernel, head, len(after) + len...  12.9 us
    pallas_call x1, Pallas kernels, pair_intra(): pl.pallas_call(functools.partial(pair_intra_kernel, head, len(after)), gr...  10.1 us
    pallas_call x1, Pallas kernels, pair_query_grad(): pl.pallas_call(functools.partial(pair_query_kernel, head), grid_spec=pltp...  9.89 us
    ppermute x14, waiting for transfers between devices, swap(): return lax.ppermute(x, 'ctx', [(c, c ^ bit) for c in range(n)])  5.11 us
  transfers between devices with their start and end apart: 20, of which 5 were waited for; matrix products, arithmetic and copies ran while one was open for 3% of the time, Pallas kernels for 49%

profile of v1, /device:TPU:25, one launch (start us, length us, event | category | flops | bytes accessed | tf_op | source)
XLA Modules:
  0.0 136.9 jit_solution(4640493539829743408)
XLA Ops:
  0.6 1.3 collective-permute-start.2
  2.0 1.2 collective-permute-start
  3.2 4.4 %pair_sums.1 = (bf16[1024,128]{1,0:T(8,128)(2,1)}, bf16[1024,128]{1,0:T(8,128)(2,1)}) custom-call(s32[1]{0:T(128)} %bitcast.me_ref, bf16[512,2048]{1,0:T(8,128)(2,1)} %k_ref.3, bf16[512,2048]{1,0:T(8,128)(2,1)} %v_ref.3), custom_call_target="tpu_custom_call" | custom-call | flops 268435456 | bytes 4194304 | tf_op jit(solution)/shard_map/pair_sums/pallas_call | solution.py:302
  7.6 1.2 collective-permute-start.1
  8.8 1.4 %collective-permute-done.1.oth_ref.kv_ref = bf16[1024,128]{1,0:T(8,128)(2,1)S(1)} collective-permute-done((bf16[1024,128]{1,0:T(8,128)(2,1)}, bf16[1024,128]{1,0:T(8,128)(2,1)S(1)}, u32[]{:S(2)}, u32[]{:S(2)}) %collective-permute-start.1) | collective-permute-done | bytes 262176 | tf_op jit(solution)/shard_map/ppermute | solution.py:615
  10.2 1.8 %fusion.refs_0_ = bf16[1024,128]{1,0:T(8,128)(2,1)} fusion(bf16[1024,128]{1,0:T(8,128)(2,1)} %get-tuple-element.24.own_ref, bf16[1024,128]{1,0:T(8,128)(2,1)S(1)} %collective-permute-done.1.oth_ref.kv_ref), kind=kLoop, calls=%fused_computation.4 | loop fusion | flops 524288 | bytes 786432 | tf_op jit(solution)/shard_map/convert_element_type | solution.py:624
  12.0 4.5 %all-to-all-start = ((bf16[8,128,128]{2,1,0:T(8,128)(2,1)}), bf16[8,128,128]{2,1,0:T(8,128)(2,1)S(1)}, u32[]{:S(2)}, u32[]{:S(2)}) async-start(bf16[8,128,128]{2,1,0:T(8,128)(2,1)} %bitcast.2), calls=%async_computation | async-start | bytes 524288 | tf_op jit(solution)/shard_map/all_to_all | solution.py:621
  16.6 0.6 dynamic-slice_bitcast_fusion.start_ref
  17.2 10.1 %pair_intra.1 = (bf16[1024,512]{1,0:T(8,128)(2,1)}, bf16[2048,512]{1,0:T(8,128)(2,1)}) custom-call(s32[1]{0:T(128)} %bitcast.me_ref, bf16[1024,128]{1,0:T(8,128)(2,1)} %fusion.refs_0_, bf16[512,2048]{1,0:T(8,128)(2,1)} %q_ref.5, bf16[512,2048]{1,0:T(8,128)(2,1)} %k_ref.3, bf16[512,2048]{1,0:T(8,128)(2,1)} %v_ref.3), custom_call_target="tpu_custom_call" | custom-call | flops 2147483648 | bytes 9437184 | tf_op jit(solution)/shard_map/pair_intra/pallas_call | solution.py:335
  27.4 0.5 all-to-all-done
  27.9 0.7 copy-done.15
  28.6 0.3 copy-done.1
  28.9 1.7 %scan_blocks.2 = (bf16[1024,128]{1,0:T(8,128)(2,1)}, bf16[2048,512]{1,0:T(8,128)(2,1)}) custom-call(bf16[1024,128]{1,0:T(8,128)(2,1)} %bitcast.19, f32[128,128]{1,0:T(8,128)} %dynamic-slice_bitcast_fusion.start_ref, bf16[1024,512]{1,0:T(8,128)(2,1)} %get-tuple-element.26.refs_0_.i_ref, bf16[512,1024]{1,0:T(8,128)(2,1)} %copy-done.1, ...), custom_call_target="tpu_custom_call", output_to_operand_aliasing={{1}: (5, {})} | custom-call | tf_op jit(solution)/shard_map/scan_blocks/pallas_call | solution.py:266
  30.6 1.4 %collective-permute-start.3 = (bf16[2048,512]{1,0:T(8,128)(2,1)}, bf16[2048,512]{1,0:T(8,128)(2,1)S(1)}, u32[]{:S(2)}, u32[]{:S(2)}) collective-permute-start(bf16[2048,512]{1,0:T(8,128)(2,1)} %get-tuple-element.30), channel_id=1, source_target_pairs={{0,2},{2,0},{4,6},{6,4},{8,10},{10,8},{12,14},{14,12},{16,18},{18,... | collective-permute-start | bytes 6291464 | tf_op jit(solution)/shard_map/ppermute | solution.py:615
  32.1 5.5 %all-to-all-start.1 = ((bf16[8,128,128]{2,1,0:T(8,128)(2,1)}), bf16[8,128,128]{2,1,0:T(8,128)(2,1)S(1)}, u32[]{:S(2)}, u32[]{:S(2)}) async-start(bf16[8,128,128]{2,1,0:T(8,128)(2,1)} %bitcast.20), calls=%async_computation.1 | async-start | bytes 524288 | tf_op jit(solution)/shard_map/all_to_all | solution.py:621
  37.6 1.2 collective-permute-start.9
  38.8 6.4 %out_grad.2 = (bf16[512,2048]{1,0:T(8,128)(2,1)}, bf16[1024,128]{1,0:T(8,128)(2,1)}, bf16[1024,128]{1,0:T(8,128)(2,1)}) custom-call(s32[1]{0:T(128)} %bitcast.me_ref, s32[1]{0:T(128)} %bitcast.1.tp_ref, bf16[512,1024]{1,0:T(8,128)(2,1)} %refs_0_.3, bf16[512,1024]{1,0:T(8,128)(2,1)} %copy-done.1, bf16[2048,2048]{1,0:T(8,128)(2,1)} %w_ref.3, ...), custom_call_target="tpu_custom_call" | custom-call | flops 2147483648 | bytes 6291456 | tf_op jit(solution)/shard_map/out_grad/pallas_call | solution.py:511
  45.2 0.7 copy-done.4
  45.9 0.7 copy-done.10
  46.6 4.7 %pair_attended.1 = (bf16[4,2,128,512]{3,2,1,0:T(8,128)(2,1)}, bf16[4,2,128,512]{3,2,1,0:T(8,128)(2,1)}) custom-call(s32[1]{0:T(128)} %bitcast.me_ref, bf16[512,2048]{1,0:T(8,128)(2,1)} %get-tuple-element.29.after_ref.refs_1_, bf16[512,2048]{1,0:T(8,128)(2,1)} %q_ref.5, bf16[512,2048]{1,0:T(8,128)(2,1)} %q_ref.5, ...), custom_call_target="tpu_custom_call" | custom-call | flops 268435456 | bytes 10485760 | tf_op jit(solution)/shard_map/pair_attended/pallas_call | solution.py:381
  51.3 1.2 collective-permute-start.6
  52.5 6.5 %out_grad.3 = (bf16[512,2048]{1,0:T(8,128)(2,1)}, bf16[1024,128]{1,0:T(8,128)(2,1)}, bf16[1024,128]{1,0:T(8,128)(2,1)}) custom-call(s32[1]{0:T(128)} %bitcast.me_ref, s32[1]{0:T(128)} %bitcast.1.tp_ref, bf16[512,1024]{1,0:T(8,128)(2,1)} %refs_0_.3, bf16[512,1024]{1,0:T(8,128)(2,1)} %copy-done.1, ...), custom_call_target="tpu_custom_call", output_to_operand_aliasing={{0}: (7, {}), {1}: (8, {}), {2}: (9, {})} | custom-call | tf_op jit(solution)/shard_map/out_grad/pallas_call | solution.py:511
  59.0 1.2 collective-permute-start.4
  60.2 0.8 fusion.2
  61.0 0.5 collective-permute-start.7
  61.5 0.4 collective-permute-start.10
  61.9 0.3 copy-done.14
  62.2 1.8 %add_after.1.after_ref = bf16[1024,128]{1,0:T(8,128)(2,1)} custom-call(bf16[4,2,128,512]{3,2,1,0:T(8,128)(2,1)} %get-tuple-element.31.refs_0_.after_ref, bf16[1024,128]{1,0:T(8,128)(2,1)} %get-tuple-element.34.a_ref, bf16[1024,128]{1,0:T(8,128)(2,1)} %copy-done.14), custom_call_target="tpu_custom_call" | custom-call | tf_op jit(solution)/shard_map/add_after/pallas_call | solution.py:557
  64.0 4.7 %all-to-all-start.2 = ((bf16[8,128,128]{2,1,0:T(8,128)(2,1)}), bf16[8,128,128]{2,1,0:T(8,128)(2,1)S(1)}, u32[]{:S(2)}, u32[]{:S(2)}) async-start(bf16[8,128,128]{2,1,0:T(8,128)(2,1)} %bitcast.16), calls=%async_computation.2 | async-start | bytes 524288 | tf_op jit(solution)/shard_map/all_to_all | solution.py:621
  68.8 0.8 collective-permute-start.8
  69.6 0.1 collective-permute-start.11
  69.7 9.9 %query_grad.1.refs_1_.refs_0_ = bf16[512,2048]{1,0:T(8,128)(2,1)} custom-call(s32[1]{0:T(128)} %bitcast.me_ref, bf16[1024,128]{1,0:T(8,128)(2,1)} %add_after.1.after_ref, bf16[512,2048]{1,0:T(8,128)(2,1)} %get-tuple-element.36.g_ref, bf16[512,2048]{1,0:T(8,128)(2,1)} %v_ref.3, bf16[512,2048]{1,0:T(8,128)(2,1)} %k_ref.3, bf16[1024,128]{1,0:T(8,128)(2,1)} %bitcast.15, ...), custom_call_target="tpu_custom_call" | custom-call | tf_op jit(solution)/shard_map/query_grad/pallas_call | solution.py:466
  79.6 0.7 broadcast_in_dim.3.start_ref
  80.3 1.7 %scan_blocks.3.refs_8_ = bf16[1024,128]{1,0:T(8,128)(2,1)} custom-call(bf16[1024,128]{1,0:T(8,128)(2,1)} %bitcast.18, f32[128,128]{1,0:T(8,128)} %broadcast_in_dim.3.start_ref, bf16[512,2048]{1,0:T(8,128)(2,1)} %query_grad.1.refs_1_.refs_0_, bf16[4,2,128,512]{3,2,1,0:T(8,128)(2,1)} %passed_after.1.refs_1_.b_ref), custom_call_target="tpu_custom_call" | custom-call | tf_op jit(solution)/shard_map/scan_blocks/pallas_call | solution.py:266
  82.0 7.1 %quad_weight.2 = (bf16[128,2048]{1,0:T(8,128)(2,1)}, bf16[128,2048]{1,0:T(8,128)(2,1)}) custom-call(s32[1]{0:T(128)} %bitcast.1.tp_ref, bf16[4,2,128,512]{3,2,1,0:T(8,128)(2,1)} %get-tuple-element.37.a_ref, bf16[4,2,128,512]{3,2,1,0:T(8,128)(2,1)} %passed_after.1.refs_1_.b_ref, bf16[512,1024]{1,0:T(8,128)(2,1)} %refs_0_.3, bf16[512,1024]{1,0:T(8,128)(2,1)} %copy-done.1, ...), custom_call_target="tpu_custom_call" | custom-call | flops 2147483648 | bytes 10485760 | tf_op jit(solution)/shard_map/quad_weight/pallas_call | solution.py:430
  89.1 0.3 collective-permute-start.14
  89.5 5.4 %all-to-all-start.3 = ((bf16[8,128,128]{2,1,0:T(8,128)(2,1)}), bf16[8,128,128]{2,1,0:T(8,128)(2,1)S(1)}, u32[]{:S(2)}, u32[]{:S(2)}) async-start(bf16[8,128,128]{2,1,0:T(8,128)(2,1)} %bitcast.9), calls=%async_computation.3 | async-start | bytes 524288 | tf_op jit(solution)/shard_map/all_to_all | solution.py:621
  94.9 7.2 %quad_weight.3 = (bf16[128,2048]{1,0:T(8,128)(2,1)}, bf16[128,2048]{1,0:T(8,128)(2,1)}) custom-call(s32[1]{0:T(128)} %bitcast.1.tp_ref, bf16[4,2,128,512]{3,2,1,0:T(8,128)(2,1)} %get-tuple-element.37.a_ref, bf16[4,2,128,512]{3,2,1,0:T(8,128)(2,1)} %passed_after.1.refs_1_.b_ref, bf16[512,1024]{1,0:T(8,128)(2,1)} %refs_0_.3, bf16[512,1024]{1,0:T(8,128)(2,1)} %copy-done.1, ...), custom_call_target="tpu_custom_call" | custom-call | tf_op jit(solution)/shard_map/quad_weight/pallas_call | solution.py:430
  102.1 0.3 collective-permute-start.13
  102.4 2.5 %collective-permute-done.14 = bf16[128,2048]{1,0:T(8,128)(2,1)S(1)} collective-permute-done((bf16[128,2048]{1,0:T(8,128)(2,1)}, bf16[128,2048]{1,0:T(8,128)(2,1)S(1)}, u32[]{:S(2)}, u32[]{:S(2)}) %collective-permute-start.14) | collective-permute-done | bytes 524320 | tf_op jit(solution)/shard_map/ppermute | solution.py:615
  104.9 0.1 add_convert_fusion
  105.1 2.2 %all-to-all-done.3 = bf16[8,128,128]{2,1,0:T(8,128)(2,1)S(1)} async-done(((bf16[8,128,128]{2,1,0:T(8,128)(2,1)}), bf16[8,128,128]{2,1,0:T(8,128)(2,1)S(1)}, u32[]{:S(2)}, u32[]{:S(2)}) %all-to-all-start.3) | async-done | bytes 262176 | tf_op jit(solution)/shard_map/all_to_all | solution.py:621
  107.3 0.1 add_convert_fusion.1
  107.4 12.2 %collective-permute-start.12 = (bf16[1024,128]{1,0:T(8,128)(2,1)S(1)}, bf16[1024,128]{1,0:T(8,128)(2,1)S(1)}, u32[]{:S(2)}, u32[]{:S(2)}) collective-permute-start(bf16[1024,128]{1,0:T(8,128)(2,1)S(1)} %add_convert_fusion.1), channel_id=1, source_target_pairs={{0,2},{2,0},{4,6},{6,4},{8,10},{10,8},{12,14},{14,12},{16,18},{18,... | collective-permute-start | bytes 786440 | tf_op jit(solution)/shard_map/ppermute | solution.py:615
  119.7 1.2 collective-permute-done.12.t_ref
  120.8 0.7 copy-done.16
  121.6 14.2 %key_value_grad.1 = (bf16[512,2048]{1,0:T(8,128)(2,1)}, bf16[512,2048]{1,0:T(8,128)(2,1)}) custom-call(s32[1]{0:T(128)} %bitcast.me_ref, bf16[128,2048]{1,0:T(8,128)(2,1)} %get-tuple-element.39.after_ref, bf16[512,2048]{1,0:T(8,128)(2,1)} %q_ref.5, bf16[512,2048]{1,0:T(8,128)(2,1)} %k_ref.3, bf16[512,2048]{1,0:T(8,128)(2,1)} %v_ref.3, ...), custom_call_target="tpu_custom_call" | custom-call | tf_op jit(solution)/shard_map/key_value_grad/pallas_call | solution.py:591
  135.7 1.2 convert_add_fusion
  (46 shorter events, 0.3 us)
Async XLA Ops:
  0.6 16.0 %copy-start = (f32[16,128,128]{2,1,0:T(8,128)S(1)}, f32[16,128,128]{2,1,0:T(8,128)}, u32[]{:S(2)}) copy-start(f32[16,128,128]{2,1,0:T(8,128)} %param.11) | copy-start | bytes 3145732
  0.6 27.2 %collective-permute-start.2 = (bf16[512,1024]{1,0:T(8,128)(2,1)}, bf16[512,1024]{1,0:T(8,128)(2,1)}, u32[]{:S(2)}, u32[]{:S(2)}) collective-permute-start(bf16[512,1024]{1,0:T(8,128)(2,1)} %refs_0_.3), channel_id=1, source_target_pairs={{0,4},{2,6},{4,0},{6,2},{8,12},{10,14},{12,8},{14,10},{16,20},{18,... | collective-permute-start | bytes 3145736 | tf_op jit(solution)/shard_map/ppermute | solution.py:615
  2.0 25.9 %collective-permute-start = (bf16[512,1024]{1,0:T(8,128)(2,1)}, bf16[512,1024]{1,0:T(8,128)(2,1)S(1)}, u32[]{:S(2)}, u32[]{:S(2)}) collective-permute-start(bf16[512,1024]{1,0:T(8,128)(2,1)} %refs_0_.3), channel_id=1, source_target_pairs={{0,1},{1,0},{2,3},{3,2},{4,5},{5,4},{6,7},{7,6},{8,9},{9,8},{10,11... | collective-permute-start | bytes 3145736 | tf_op jit(solution)/shard_map/ppermute | solution.py:618
  7.6 2.6 %collective-permute-start.1 = (bf16[1024,128]{1,0:T(8,128)(2,1)}, bf16[1024,128]{1,0:T(8,128)(2,1)S(1)}, u32[]{:S(2)}, u32[]{:S(2)}) collective-permute-start(bf16[1024,128]{1,0:T(8,128)(2,1)} %get-tuple-element.25), channel_id=1, source_target_pairs={{0,2},{2,0},{4,6},{6,4},{8,10},{10,8},{12,14},{14,12},{16,18},{18,... | collective-permute-start | bytes 786440 | tf_op jit(solution)/shard_map/ppermute | solution.py:615
  10.2 17.1 %copy-start.7 = (bf16[1024,128]{1,0:T(8,128)(2,1)}, bf16[1024,128]{1,0:T(8,128)(2,1)S(1)}, u32[]{:S(2)}) copy-start(bf16[1024,128]{1,0:T(8,128)(2,1)S(1)} %collective-permute-done.1.oth_ref.kv_ref) | copy-start | bytes 786436
  12.0 15.8 %all-to-all-start = ((bf16[8,128,128]{2,1,0:T(8,128)(2,1)}), bf16[8,128,128]{2,1,0:T(8,128)(2,1)S(1)}, u32[]{:S(2)}, u32[]{:S(2)}) async-start(bf16[8,128,128]{2,1,0:T(8,128)(2,1)} %bitcast.2), calls=%async_computation | async-start | bytes 524288 | tf_op jit(solution)/shard_map/all_to_all | solution.py:621
  27.9 0.7 copy-start.15
  27.9 1.0 copy-start.1
  30.6 14.5 %collective-permute-start.3 = (bf16[2048,512]{1,0:T(8,128)(2,1)}, bf16[2048,512]{1,0:T(8,128)(2,1)S(1)}, u32[]{:S(2)}, u32[]{:S(2)}) collective-permute-start(bf16[2048,512]{1,0:T(8,128)(2,1)} %get-tuple-element.30), channel_id=1, source_target_pairs={{0,2},{2,0},{4,6},{6,4},{8,10},{10,8},{12,14},{14,12},{16,18},{18,... | collective-permute-start | bytes 6291464 | tf_op jit(solution)/shard_map/ppermute | solution.py:615
  32.1 13.1 %all-to-all-start.1 = ((bf16[8,128,128]{2,1,0:T(8,128)(2,1)}), bf16[8,128,128]{2,1,0:T(8,128)(2,1)S(1)}, u32[]{:S(2)}, u32[]{:S(2)}) async-start(bf16[8,128,128]{2,1,0:T(8,128)(2,1)} %bitcast.20), calls=%async_computation.1 | async-start | bytes 524288 | tf_op jit(solution)/shard_map/all_to_all | solution.py:621
  37.6 32.0 %collective-permute-start.9 = (bf16[512,1024]{1,0:T(8,128)(2,1)}, bf16[512,1024]{1,0:T(8,128)(2,1)}, u32[]{:S(2)}, u32[]{:S(2)}) collective-permute-start(bf16[512,1024]{1,0:T(8,128)(2,1)} %collective-permute-done.2.refs_2_.refs_1_.refs_4_), channel_id=1, source_target_pairs={{0,1},{1,0},{2,3},{3,2},{4,5},{5,4},{6,7},{7,6},{8,9},{9,8},{10,11... | collective-permute-start | bytes 3145736 | tf_op jit(solution)/shard_map/ppermute | solution.py:618
  45.2 0.7 copy-start.4
  45.2 1.4 %copy-start.10 = (bf16[2048,512]{1,0:T(8,128)(2,1)}, bf16[2048,512]{1,0:T(8,128)(2,1)S(1)}, u32[]{:S(2)}) copy-start(bf16[2048,512]{1,0:T(8,128)(2,1)S(1)} %collective-permute-done.3.far_ref) | copy-start | bytes 6291460
  51.3 28.3 %collective-permute-start.6 = (bf16[4,2,128,512]{3,2,1,0:T(8,128)(2,1)}, bf16[4,2,128,512]{3,2,1,0:T(8,128)(2,1)}, u32[]{:S(2)}, u32[]{:S(2)}) collective-permute-start(bf16[4,2,128,512]{3,2,1,0:T(8,128)(2,1)} %get-tuple-element.31.refs_0_.after_ref), channel_id=1, source_target_pairs={{0,4},{2,6},{4,0},{6,2},{8,12},{10,14},{12,8},{14,10},{16,20},{18,... | collective-permute-start | bytes 3145736 | tf_op jit(solution)/shard_map/ppermute | solution.py:615
  52.5 7.7 %copy-start.5 = (bf16[8,128,128]{2,1,0:T(8,128)(2,1)S(1)}, bf16[8,128,128]{2,1,0:T(8,128)(2,1)}, u32[]{:S(2)}) copy-start(bf16[8,128,128]{2,1,0:T(8,128)(2,1)} %copy-done.4) | copy-start | bytes 786436
  52.5 7.7 %copy-start.8 = (bf16[1024,128]{1,0:T(8,128)(2,1)S(1)}, bf16[1024,128]{1,0:T(8,128)(2,1)}, u32[]{:S(2)}) copy-start(bf16[1024,128]{1,0:T(8,128)(2,1)} %get-tuple-element.24.own_ref) | copy-start | bytes 786436
  52.5 8.5 %copy-start.3 = (bf16[512,1024]{1,0:T(8,128)(2,1)S(1)}, bf16[512,1024]{1,0:T(8,128)(2,1)}, u32[]{:S(2)}) copy-start(bf16[512,1024]{1,0:T(8,128)(2,1)} %refs_0_.3) | copy-start | bytes 3145732
  59.0 9.8 %copy-start.2 = (bf16[512,1024]{1,0:T(8,128)(2,1)S(1)}, bf16[512,1024]{1,0:T(8,128)(2,1)}, u32[]{:S(2)}) copy-start(bf16[512,1024]{1,0:T(8,128)(2,1)} %copy-done.1) | copy-start | bytes 3145732
  59.0 2.5 %collective-permute-start.4 = (bf16[1024,128]{1,0:T(8,128)(2,1)}, bf16[1024,128]{1,0:T(8,128)(2,1)S(1)}, u32[]{:S(2)}, u32[]{:S(2)}) collective-permute-start(bf16[1024,128]{1,0:T(8,128)(2,1)} %get-tuple-element.35), channel_id=1, source_target_pairs={{0,2},{2,0},{4,6},{6,4},{8,10},{10,8},{12,14},{14,12},{16,18},{18,... | collective-permute-start | bytes 786440 | tf_op jit(solution)/shard_map/ppermute | solution.py:615
  61.0 7.8 %collective-permute-start.5 = (bf16[1024,128]{1,0:T(8,128)(2,1)}, bf16[1024,128]{1,0:T(8,128)(2,1)}, u32[]{:S(2)}, u32[]{:S(2)}) collective-permute-start(bf16[1024,128]{1,0:T(8,128)(2,1)} %fusion.2), channel_id=1, source_target_pairs={{0,2},{2,0},{4,6},{6,4},{8,10},{10,8},{12,14},{14,12},{16,18},{18,... | collective-permute-start | bytes 786440 | tf_op jit(solution)/shard_map/ppermute | solution.py:615
  61.0 21.0 %collective-permute-start.7 = (bf16[512,1024]{1,0:T(8,128)(2,1)S(1)}, bf16[512,1024]{1,0:T(8,128)(2,1)}, u32[]{:S(2)}, u32[]{:S(2)}) collective-permute-start(bf16[512,1024]{1,0:T(8,128)(2,1)S(1)} %copy-done.3), channel_id=1, source_target_pairs={{0,2},{2,0},{4,6},{6,4},{8,10},{10,8},{12,14},{14,12},{16,18},{18,... | collective-permute-start | bytes 3145736 | tf_op jit(solution)/shard_map/ppermute | solution.py:615
  61.5 0.7 copy-start.14
  61.5 20.5 %collective-permute-start.10 = (bf16[512,1024]{1,0:T(8,128)(2,1)}, bf16[512,1024]{1,0:T(8,128)(2,1)}, u32[]{:S(2)}, u32[]{:S(2)}) collective-permute-start(bf16[512,1024]{1,0:T(8,128)(2,1)} %collective-permute-done.2.refs_2_.refs_1_.refs_4_), channel_id=1, source_target_pairs={{0,2},{2,0},{4,6},{6,4},{8,10},{10,8},{12,14},{14,12},{16,18},{18,... | collective-permute-start | bytes 3145736 | tf_op jit(solution)/shard_map/ppermute | solution.py:615
  64.0 15.5 %all-to-all-start.2 = ((bf16[8,128,128]{2,1,0:T(8,128)(2,1)}), bf16[8,128,128]{2,1,0:T(8,128)(2,1)S(1)}, u32[]{:S(2)}, u32[]{:S(2)}) async-start(bf16[8,128,128]{2,1,0:T(8,128)(2,1)} %bitcast.16), calls=%async_computation.2 | async-start | bytes 524288 | tf_op jit(solution)/shard_map/all_to_all | solution.py:621
  68.8 13.2 %collective-permute-start.8 = (bf16[512,1024]{1,0:T(8,128)(2,1)S(1)}, bf16[512,1024]{1,0:T(8,128)(2,1)}, u32[]{:S(2)}, u32[]{:S(2)}) collective-permute-start(bf16[512,1024]{1,0:T(8,128)(2,1)S(1)} %copy-done.2), channel_id=1, source_target_pairs={{0,2},{2,0},{4,6},{6,4},{8,10},{10,8},{12,14},{14,12},{16,18},{18,... | collective-permute-start | bytes 3145736 | tf_op jit(solution)/shard_map/ppermute | solution.py:615
  69.6 12.4 %collective-permute-start.11 = (bf16[512,1024]{1,0:T(8,128)(2,1)}, bf16[512,1024]{1,0:T(8,128)(2,1)}, u32[]{:S(2)}, u32[]{:S(2)}) collective-permute-start(bf16[512,1024]{1,0:T(8,128)(2,1)} %collective-permute-done.9.refs_5_), channel_id=1, source_target_pairs={{0,2},{2,0},{4,6},{6,4},{8,10},{10,8},{12,14},{14,12},{16,18},{18,... | collective-permute-start | bytes 3145736 | tf_op jit(solution)/shard_map/ppermute | solution.py:615
  79.6 0.7 copy-start.13
  89.1 15.8 %collective-permute-start.14 = (bf16[128,2048]{1,0:T(8,128)(2,1)}, bf16[128,2048]{1,0:T(8,128)(2,1)S(1)}, u32[]{:S(2)}, u32[]{:S(2)}) collective-permute-start(bf16[128,2048]{1,0:T(8,128)(2,1)} %get-tuple-element.43), channel_id=1, source_target_pairs={{0,8},{2,10},{4,12},{6,14},{8,0},{10,2},{12,4},{14,6},{16,24},{18,... | collective-permute-start | bytes 1572872 | tf_op jit(solution)/shard_map/ppermute | solution.py:615
  89.5 17.8 %all-to-all-start.3 = ((bf16[8,128,128]{2,1,0:T(8,128)(2,1)}), bf16[8,128,128]{2,1,0:T(8,128)(2,1)S(1)}, u32[]{:S(2)}, u32[]{:S(2)}) async-start(bf16[8,128,128]{2,1,0:T(8,128)(2,1)} %bitcast.9), calls=%async_computation.3 | async-start | bytes 524288 | tf_op jit(solution)/shard_map/all_to_all | solution.py:621
  94.9 10.0 %copy-start.12 = (bf16[128,2048]{1,0:T(8,128)(2,1)S(1)}, bf16[128,2048]{1,0:T(8,128)(2,1)}, u32[]{:S(2)}) copy-start(bf16[128,2048]{1,0:T(8,128)(2,1)} %get-tuple-element.38.refs_8_) | copy-start | bytes 1572868
  94.9 12.4 %copy-start.6 = (bf16[1024,128]{1,0:T(8,128)(2,1)S(1)}, bf16[1024,128]{1,0:T(8,128)(2,1)}, u32[]{:S(2)}) copy-start(bf16[1024,128]{1,0:T(8,128)(2,1)} %get-tuple-element.34.a_ref) | copy-start | bytes 786436
  102.1 33.6 %collective-permute-start.13 = (bf16[128,2048]{1,0:T(8,128)(2,1)}, bf16[128,2048]{1,0:T(8,128)(2,1)S(1)}, u32[]{:S(2)}, u32[]{:S(2)}) collective-permute-start(bf16[128,2048]{1,0:T(8,128)(2,1)} %get-tuple-element.42), channel_id=1, source_target_pairs={{0,8},{2,10},{4,12},{6,14},{8,0},{10,2},{12,4},{14,6},{16,24},{18,... | collective-permute-start | bytes 1572872 | tf_op jit(solution)/shard_map/ppermute | solution.py:615
  105.1 30.7 %collective-permute-start.15 = (bf16[128,2048]{1,0:T(8,128)(2,1)S(1)}, bf16[128,2048]{1,0:T(8,128)(2,1)S(1)}, u32[]{:S(2)}, u32[]{:S(2)}) collective-permute-start(bf16[128,2048]{1,0:T(8,128)(2,1)S(1)} %add_convert_fusion), channel_id=1, source_target_pairs={{0,16},{2,18},{4,20},{6,22},{8,24},{10,26},{12,28},{14,30},{16,0},... | collective-permute-start | bytes 1572872 | tf_op jit(solution)/shard_map/ppermute | solution.py:615
  107.3 13.5 %copy-start.9 = (bf16[8,128,128]{2,1,0:T(8,128)(2,1)}, bf16[8,128,128]{2,1,0:T(8,128)(2,1)S(1)}, u32[]{:S(2)}) copy-start(bf16[8,128,128]{2,1,0:T(8,128)(2,1)S(1)} %all-to-all-done.3) | copy-start | bytes 786436
  107.4 13.4 %collective-permute-start.12 = (bf16[1024,128]{1,0:T(8,128)(2,1)S(1)}, bf16[1024,128]{1,0:T(8,128)(2,1)S(1)}, u32[]{:S(2)}, u32[]{:S(2)}) collective-permute-start(bf16[1024,128]{1,0:T(8,128)(2,1)S(1)} %add_convert_fusion.1), channel_id=1, source_target_pairs={{0,2},{2,0},{4,6},{6,4},{8,10},{10,8},{12,14},{14,12},{16,18},{18,... | collective-permute-start | bytes 786440 | tf_op jit(solution)/shard_map/ppermute | solution.py:615
  120.8 0.7 copy-start.16
  121.6 14.2 %copy-start.11 = (bf16[128,2048]{1,0:T(8,128)(2,1)S(1)}, bf16[128,2048]{1,0:T(8,128)(2,1)}, u32[]{:S(2)}) copy-start(bf16[128,2048]{1,0:T(8,128)(2,1)} %get-tuple-element.39.after_ref) | copy-start | bytes 1572868

commit v2 on v1

--- a/solution.py
+++ b/solution.py
@@ -318,29 +318,28 @@
     q_ref, k_ref, v_ref, mine_ref, send_ref = refs[waits:]
     core = me_ref[0] % 2
     half = q_ref.shape[0] // 2
-    mine, other = lanes(core, head), lanes(1 - core, head)
-    first, second = causal_apply(q_ref[:, other], k_ref[:, other], v_ref[:, other], False)
-    send_ref[head:, :half] = first.astype(BF).T
-    send_ref[head:, half:] = second.astype(BF).T
-    send_ref[:head, :] = q_ref[:, other].T
-    first, second = causal_apply(q_ref[:, mine], k_ref[:, mine], v_ref[:, mine], False)
-    mine_ref[:, :half] = first.astype(BF).T
-    mine_ref[:, half:] = second.astype(BF).T
+    for j in range(q_ref.shape[1] // (2 * head)):
+        for o_ref, side, base in ((send_ref, 1 - core, (2 * j + 1) * head), (mine_ref, core, j * head)):
+            pick = lanes(2 * j + side, head)
+            first, second = causal_apply(q_ref[:, pick], k_ref[:, pick], v_ref[:, pick], False)
+            o_ref[base : base + head, :half] = first.astype(BF).T
+            o_ref[base : base + head, half:] = second.astype(BF).T
+        send_ref[2 * j * head : (2 * j + 1) * head, :] = q_ref[:, lanes(2 * j + 1 - core, head)].T
 
 
 def pair_intra(me, after, q, k, v, head):
     tok, width = q.shape
-    steps = width // (2 * head)
-    spec = pl.BlockSpec((tok, 2 * head), lambda i, m: (0, i))
+    step = min(4 * head, width)
+    spec = pl.BlockSpec((tok, step), lambda i, m: (0, i))
     return pl.pallas_call(
         functools.partial(pair_intra_kernel, head, len(after)),
         grid_spec=pltpu.PrefetchScalarGridSpec(
             num_scalar_prefetch=1,
-            grid=(steps,),
+            grid=(width // step,),
             in_specs=[ANY] * len(after) + [spec] * 3,
             out_specs=[
-                pl.BlockSpec((head, tok), lambda i, m: (i, 0)),
-                pl.BlockSpec((2 * head, tok), lambda i, m: (i, 0)),
+                pl.BlockSpec((step // 2, tok), lambda i, m: (i, 0)),
+                pl.BlockSpec((step, tok), lambda i, m: (i, 0)),
             ],
         ),
         out_shape=[
@@ -353,10 +352,12 @@
     )(me, *after, q, k, v)
 
 
-def pair_attended_kernel(head, me_ref, after_ref, q0_ref, q1_ref, i_ref, far_ref, s_ref, own_ref, oth_ref, mine_ref, send_ref):
+def pair_attended_kernel(head, me_ref, after_ref, q0_ref, q1_ref, i_ref, far_ref, s_ref, own_ref, oth_ref,
+                         mine_ref, cross_ref, near_ref):
     core = (me_ref[0] % 2).astype(F32)
     south = (me_ref[0] // 2) % 2
-    for q_ref, side, o_ref in ((q0_ref, south, mine_ref), (q1_ref, 1 - south, send_ref)):
+
+    def fill(q_ref, side, o_ref):
         rows = lanes(side, head)
         state = s_ref[rows, :].astype(F32)
         near = (state + core * oth_ref[rows, :].astype(F32)).astype(BF)
@@ -367,17 +368,28 @@
         o_ref[0, 0] = here.astype(BF)
         o_ref[0, 1] = there.astype(BF)
 
+    fill(q0_ref, south, mine_ref)
+    crossing = pl.program_id(0) < pl.num_programs(0) // 2
+    pl.when(crossing)(lambda: fill(q1_ref, 1 - south, cross_ref))
+    pl.when(jnp.logical_not(crossing))(lambda: fill(q1_ref, 1 - south, near_ref))
+
 
 def pair_attended(me, after, q, inner, far, state, own, oth, head):
     tok, width = q.shape
     places = width // (4 * head)
+    half = places // 2
 
     def place(i, m):
-        return (m[0] // 4) ^ i
+        return (m[0] // 4) ^ i ^ half
 
     rows = pl.BlockSpec((2 * head, head), lambda i, m: (place(i, m), 0))
-    out = pl.BlockSpec((1, 2, head, tok), lambda i, m: (i, 0, 0, 0))
-    shape = jax.ShapeDtypeStruct((places, 2, head, tok), BF)
+
+    def out(index):
+        return pl.BlockSpec((1, 2, head, tok), lambda i, m: (index(i), 0, 0, 0))
+
+    def shape(count):
+        return jax.ShapeDtypeStruct((count, 2, head, tok), BF)
+
     return pl.pallas_call(
         functools.partial(pair_attended_kernel, head),
         grid_spec=pltpu.PrefetchScalarGridSpec(
@@ -391,9 +403,13 @@
                 pl.BlockSpec((4 * head, tok), lambda i, m: (place(i, m), 0)),
             ]
             + [rows] * 3,
-            out_specs=[out, out],
+            out_specs=[
+                out(lambda i: i ^ half),
+                out(lambda i: jnp.minimum(i, half - 1)),
+                out(lambda i: jnp.maximum(i - half, 0)),
+            ],
         ),
-        out_shape=[shape, shape],
+        out_shape=[shape(places), shape(half), shape(half)],
         compiler_params=params(),
         cost_estimate=cost(2 * tok * head * width, 10 * tok * width),
         name="pair_attended",
@@ -432,7 +448,7 @@
         grid_spec=pltpu.PrefetchScalarGridSpec(
             num_scalar_prefetch=1,
             grid=(2 * steps,),
-            in_specs=[whole, whole] + [own, other] * 4 + [ANY] * len(after),
+            in_specs=[whole, pl.BlockSpec(b.shape, lambda i, t: (0, 0, 0, 0))] + [own, other] * 4 + [ANY] * len(after),
             out_specs=[
                 pl.BlockSpec((head, step), lambda i, t: (0, (i + t[0] * steps) % (2 * steps)))
             ]
@@ -440,7 +456,7 @@
         ),
         out_shape=[jax.ShapeDtypeStruct((head, 2 * feat), BF)] * half,
         compiler_params=params(),
-        cost_estimate=cost(16 * tok * feat * half * head * far_side, 20 * feat * tok * far_side),
+        cost_estimate=cost(2e10, 0),
         name="quad_weight",
     )(tp, a, b, *cots, *after)
 
@@ -448,11 +464,11 @@
 def pair_query_kernel(head, me_ref, after_ref, g_ref, v_ref, k_ref, s_ref, kv_ref, t_ref, o_ref):
     core = me_ref[0] % 2
     half = g_ref.shape[0] // 2
-    near = (s_ref[...].astype(F32) + core.astype(F32) * kv_ref[...].astype(F32)).astype(BF)
-    for j in range(2):
-        at = slice(j * head, (j + 1) * head)
+    for j in range(g_ref.shape[1] // head):
+        at, row = slice(j * head, (j + 1) * head), slice(j // 2 * head, (j // 2 + 1) * head)
         g = g_ref[:, at]
-        state = jnp.where(core == j, near, t_ref[...])
+        near = s_ref[row, :].astype(F32) + core.astype(F32) * kv_ref[row, :].astype(F32)
+        state = jnp.where(core == j % 2, near.astype(BF), t_ref[row, :])
         first_half, second_half = causal_apply(g, v_ref[:, at], k_ref[:, at], False)
         over = dot(g, state, 1, 1)
         o_ref[:half, at] = (first_half + over[:half]).astype(BF)
@@ -461,13 +477,14 @@
 
 def pair_query_grad(me, after, g, v, k, state, kv, other, head):
     tok, width = g.shape
-    spec = pl.BlockSpec((tok, 2 * head), lambda i, m: (0, i))
-    rows = pl.BlockSpec((head, head), lambda i, m: (i, 0))
+    step = min(4 * head, width)
+    spec = pl.BlockSpec((tok, step), lambda i, m: (0, i))
+    rows = pl.BlockSpec((step // 2, head), lambda i, m: (i, 0))
     return pl.pallas_call(
         functools.partial(pair_query_kernel, head),
         grid_spec=pltpu.PrefetchScalarGridSpec(
             num_scalar_prefetch=1,
-            grid=(width // (2 * head),),
+            grid=(width // step,),
             in_specs=[ANY, spec, spec, spec, rows, rows, rows],
             out_specs=spec,
         ),
@@ -568,11 +585,11 @@
 def pair_key_value_kernel(head, me_ref, after_ref, q_ref, k_ref, v_ref, g_ref, s_ref, qd_ref, t_ref, ko_ref, vo_ref):
     core = me_ref[0] % 2
     half = g_ref.shape[0] // 2
-    near = (s_ref[...].astype(F32) + (1 - core).astype(F32) * qd_ref[...].astype(F32)).astype(BF)
-    for j in range(2):
-        at = slice(j * head, (j + 1) * head)
+    for j in range(g_ref.shape[1] // head):
+        at, row = slice(j * head, (j + 1) * head), slice(j // 2 * head, (j // 2 + 1) * head)
+        near = s_ref[row, :].astype(F32) + (1 - core).astype(F32) * qd_ref[row, :].astype(F32)
         q, k, v, g = q_ref[:, at], k_ref[:, at], v_ref[:, at], g_ref[:, at]
-        adj = jnp.where(core == j, near, t_ref[...])
+        adj = jnp.where(core == j % 2, near.astype(BF), t_ref[row, :])
         first, second = causal_apply(v, g, q, True)
         over = dot(v, adj, 1, 1)
         ko_ref[:half, at] = (first + over[:half]).astype(BF)
@@ -585,14 +602,15 @@
 
 def pair_key_value_grad(me, after, q, k, v, g, adjoint, qd, other, head):
     tok, width = g.shape
-    spec = pl.BlockSpec((tok, 2 * head), lambda i, m: (0, i))
-    rows = pl.BlockSpec((head, head), lambda i, m: (i, 0))
+    step = min(4 * head, width)
+    spec = pl.BlockSpec((tok, step), lambda i, m: (0, i))
+    rows = pl.BlockSpec((step // 2, head), lambda i, m: (i, 0))
     shape = jax.ShapeDtypeStruct((tok, width), BF)
     return pl.pallas_call(
         functools.partial(pair_key_value_kernel, head),
         grid_spec=pltpu.PrefetchScalarGridSpec(
             num_scalar_prefetch=1,
-            grid=(width // (2 * head),),
+            grid=(width // step,),
             in_specs=[ANY, spec, spec, spec, spec, rows, rows, rows],
             out_specs=[spec, spec],
         ),
@@ -635,10 +653,10 @@
 
     far_south = swap_tp(south)
     early = pair_grad(who, which, 0, (scanned, south), (), cotangent, far, out_weight, queries, head)
-    mine, send = pair_attended(
+    mine, send, send_near = pair_attended(
         who, early[0], queries, inner, swap(sent, 1), state, kv_mine, kv_other, head
     )
-    received = swap(send, 2)
+    received, received_near = swap(send, 2), swap(send_near, 2)
     state_other = swap(added(state, 1.0 - core, kv_mine), 1)
 
     grad, qd_mine, qd_send = pair_grad(
@@ -646,22 +664,22 @@
     )
     qd_other = swap(qd_send, 1)
     chip = add_after(send, qd_mine, qd_other)
-    query_g = pair_query_grad(who, chip, grad, values, keys, state, kv_other, state_other, head)
-    received = passed_after(received, (query_g,), 2e10)
-    scanned = scan_blocks(
-        across(chip), jnp.zeros_like(start), n // 2, True, (query_g, received)
-    )
-    after_chip = across(scanned)
     cots = [cotangent, far, swap(cotangent, 1), swap(far, 1)]
     cots += [south, far_south, swap(south, 1), swap(far_south, 1)]
 
-    crossing = quad_weight(which, (scanned,), mine, received, cots, 1)
-    crossed = swap(added(crossing[0], 1.0, swap(crossing[1], 4)), 8)
-    same = quad_weight(which, (crossing[0],), mine, received, cots, 0)
+    received = passed_after(received, (chip, state_other), 2e10)
+    crossing = quad_weight(which, (), mine, received, cots, 1)
+    summed = added(crossing[0], 1.0, swap(crossing[1], 4))
+    crossed = swap(summed, 8)
+    scanned = scan_blocks(across(chip), jnp.zeros_like(start), n // 2, True, (crossing[0],))
+    after_chip = across(scanned)
+    same = quad_weight(which, (scanned,), mine, received_near, cots, 0)
     neighbour = swap(same[1], 4)
+    query_g = pair_query_grad(who, summed, grad, values, keys, state, kv_other, state_other, head)
+    after_chip = passed_after(after_chip, (query_g,), 0)
     adjoint_other = swap(added(after_chip, core, qd_mine), 1)
     key_g, value_g = pair_key_value_grad(
-        who, same[0], queries, keys, values, grad, after_chip, qd_other, adjoint_other, head
+        who, query_g, queries, keys, values, grad, after_chip, qd_other, adjoint_other, head
     )
     total = same[0].astype(F32) + neighbour.astype(F32) + crossed.astype(F32)
     return query_g, key_g, value_g, total

time: 138 us -> 141 us (1.022)
  the two profiles are of different devices: /device:TPU:25 before, /device:TPU:0 now
where the time goes in v2:
time: 141 us; the launch traced here: 140 us
  Pallas kernels  73.4 us (52%)
  starting transfers between devices  34.5 us (24%)
  waiting for transfers between devices  18.8 us (13%)
  local copies, waits for them, and re-layouts  6.82 us (5%)
  other arithmetic  6.02 us (4%)
    all_to_all x4, starting transfers between devices, across(): return lax.all_to_all(x, 'ctx', 0, 0, axis_index_groups=groups, tiled=True)  18.4 us
    pallas_call x2, Pallas kernels, quad_weight(): pl.pallas_call(functools.partial(quad_weight_kernel, len(after)), grid_sp...  14.2 us
    pallas_call x1, Pallas kernels, pair_key_value_grad(): pl.pallas_call(functools.partial(pair_key_value_kernel, head), grid_spec=...  13.8 us
    pallas_call x2, Pallas kernels, pair_grad(): pl.pallas_call(functools.partial(pair_grad_kernel, head, len(after) + len...  12.9 us
    all_to_all x4, waiting for transfers between devices, across(): return lax.all_to_all(x, 'ctx', 0, 0, axis_index_groups=groups, tiled=True)  12.7 us
    ppermute x15, starting transfers between devices, swap(): return lax.ppermute(x, 'ctx', [(c, c ^ bit) for c in range(n)])  12.7 us
    pallas_call x1, Pallas kernels, pair_intra(): pl.pallas_call(functools.partial(pair_intra_kernel, head, len(after)), gr...  9.36 us
    pallas_call x1, Pallas kernels, pair_query_grad(): pl.pallas_call(functools.partial(pair_query_kernel, head), grid_spec=pltp...  8.23 us
  transfers between devices with their start and end apart: 21, of which 9 were waited for; matrix products, arithmetic and copies ran while one was open for 4% of the time, Pallas kernels for 51%

profile of v2, /device:TPU:0, one launch (start us, length us, event | category | flops | bytes accessed | tf_op | source)
XLA Modules:
  0.0 140.4 jit_solution(8322771429004741987)
XLA Ops:
  0.6 3.0 %collective-permute-start = (bf16[512,1024]{1,0:T(8,128)(2,1)}, bf16[512,1024]{1,0:T(8,128)(2,1)S(1)}, u32[]{:S(2)}, u32[]{:S(2)}) collective-permute-start(bf16[512,1024]{1,0:T(8,128)(2,1)} %refs_0_.3), channel_id=1, source_target_pairs={{0,1},{1,0},{2,3},{3,2},{4,5},{5,4},{6,7},{7,6},{8,9},{9,8},{10,11... | collective-permute-start | bytes 3145736 | tf_op jit(solution)/shard_map/ppermute | solution.py:636
  3.6 1.5 %collective-permute-start.2 = (bf16[512,1024]{1,0:T(8,128)(2,1)}, bf16[512,1024]{1,0:T(8,128)(2,1)}, u32[]{:S(2)}, u32[]{:S(2)}) collective-permute-start(bf16[512,1024]{1,0:T(8,128)(2,1)} %refs_0_.3), channel_id=1, source_target_pairs={{0,4},{2,6},{4,0},{6,2},{8,12},{10,14},{12,8},{14,10},{16,20},{18,... | collective-permute-start | bytes 3145736 | tf_op jit(solution)/shard_map/ppermute | solution.py:633
  5.2 4.4 %pair_sums.1 = (bf16[1024,128]{1,0:T(8,128)(2,1)}, bf16[1024,128]{1,0:T(8,128)(2,1)}) custom-call(s32[1]{0:T(128)} %bitcast.me_ref, bf16[512,2048]{1,0:T(8,128)(2,1)} %k_ref.3, bf16[512,2048]{1,0:T(8,128)(2,1)} %v_ref.3), custom_call_target="tpu_custom_call" | custom-call | flops 268435456 | bytes 4194304 | tf_op jit(solution)/shard_map/pair_sums/pallas_call | solution.py:302
  9.6 1.7 %collective-permute-done.1.oth_ref.kv_ref = bf16[1024,128]{1,0:T(8,128)(2,1)S(1)} collective-permute-done((bf16[1024,128]{1,0:T(8,128)(2,1)}, bf16[1024,128]{1,0:T(8,128)(2,1)S(1)}, u32[]{:S(2)}, u32[]{:S(2)}) %collective-permute-start.1) | collective-permute-done | bytes 262176 | tf_op jit(solution)/shard_map/ppermute | solution.py:633
  11.4 1.8 %fusion.refs_0_ = bf16[1024,128]{1,0:T(8,128)(2,1)} fusion(bf16[1024,128]{1,0:T(8,128)(2,1)} %get-tuple-element.25.own_ref, bf16[1024,128]{1,0:T(8,128)(2,1)S(1)} %collective-permute-done.1.oth_ref.kv_ref), kind=kLoop, calls=%fused_computation.4 | loop fusion | flops 524288 | bytes 786432 | tf_op jit(solution)/shard_map/convert_element_type | solution.py:642
  13.2 4.9 %all-to-all-start = ((bf16[8,128,128]{2,1,0:T(8,128)(2,1)}), bf16[8,128,128]{2,1,0:T(8,128)(2,1)S(1)}, u32[]{:S(2)}, u32[]{:S(2)}) async-start(bf16[8,128,128]{2,1,0:T(8,128)(2,1)} %bitcast.2), calls=%async_computation | async-start | bytes 524288 | tf_op jit(solution)/shard_map/all_to_all | solution.py:639
  18.1 0.6 dynamic-slice_bitcast_fusion.start_ref
  18.7 9.4 %pair_intra.1 = (bf16[1024,512]{1,0:T(8,128)(2,1)}, bf16[2048,512]{1,0:T(8,128)(2,1)}) custom-call(s32[1]{0:T(128)} %bitcast.me_ref, bf16[1024,128]{1,0:T(8,128)(2,1)} %fusion.refs_0_, bf16[512,2048]{1,0:T(8,128)(2,1)} %q_ref.5, bf16[512,2048]{1,0:T(8,128)(2,1)} %k_ref.3, bf16[512,2048]{1,0:T(8,128)(2,1)} %v_ref.3), custom_call_target="tpu_custom_call" | custom-call | flops 2147483648 | bytes 9437184 | tf_op jit(solution)/shard_map/pair_intra/pallas_call | solution.py:334
  28.1 3.2 %all-to-all-done = bf16[8,128,128]{2,1,0:T(8,128)(2,1)S(1)} async-done(((bf16[8,128,128]{2,1,0:T(8,128)(2,1)}), bf16[8,128,128]{2,1,0:T(8,128)(2,1)S(1)}, u32[]{:S(2)}, u32[]{:S(2)}) %all-to-all-start) | async-done | bytes 262176 | tf_op jit(solution)/shard_map/all_to_all | solution.py:639
  31.3 0.7 copy-done.15
  32.3 1.7 %scan_blocks.2 = (bf16[1024,128]{1,0:T(8,128)(2,1)}, bf16[2048,512]{1,0:T(8,128)(2,1)}) custom-call(bf16[1024,128]{1,0:T(8,128)(2,1)} %bitcast.18, f32[128,128]{1,0:T(8,128)} %dynamic-slice_bitcast_fusion.start_ref, bf16[1024,512]{1,0:T(8,128)(2,1)} %get-tuple-element.27.refs_0_.i_ref, bf16[512,1024]{1,0:T(8,128)(2,1)} %copy-done.1, ...), custom_call_target="tpu_custom_call", output_to_operand_aliasing={{1}: (5, {})} | custom-call | tf_op jit(solution)/shard_map/scan_blocks/pallas_call | solution.py:266
  34.0 0.4 collective-permute-start.9
  34.4 6.0 %all-to-all-start.1 = ((bf16[8,128,128]{2,1,0:T(8,128)(2,1)}), bf16[8,128,128]{2,1,0:T(8,128)(2,1)S(1)}, u32[]{:S(2)}, u32[]{:S(2)}) async-start(bf16[8,128,128]{2,1,0:T(8,128)(2,1)} %bitcast.19), calls=%async_computation.1 | async-start | bytes 524288 | tf_op jit(solution)/shard_map/all_to_all | solution.py:639
  40.4 6.4 %out_grad.2 = (bf16[512,2048]{1,0:T(8,128)(2,1)}, bf16[1024,128]{1,0:T(8,128)(2,1)}, bf16[1024,128]{1,0:T(8,128)(2,1)}) custom-call(s32[1]{0:T(128)} %bitcast.me_ref, s32[1]{0:T(128)} %bitcast.1.tp_ref, bf16[512,1024]{1,0:T(8,128)(2,1)} %refs_0_.3, bf16[512,1024]{1,0:T(8,128)(2,1)} %copy-done.1, bf16[2048,2048]{1,0:T(8,128)(2,1)} %w_ref.3, ...), custom_call_target="tpu_custom_call" | custom-call | flops 2147483648 | bytes 6291456 | tf_op jit(solution)/shard_map/out_grad/pallas_call | solution.py:528
  46.8 2.9 %all-to-all-done.1 = bf16[8,128,128]{2,1,0:T(8,128)(2,1)S(1)} async-done(((bf16[8,128,128]{2,1,0:T(8,128)(2,1)}), bf16[8,128,128]{2,1,0:T(8,128)(2,1)S(1)}, u32[]{:S(2)}, u32[]{:S(2)}) %all-to-all-start.1) | async-done | bytes 262176 | tf_op jit(solution)/shard_map/all_to_all | solution.py:639
  49.7 0.7 copy-done.3
  50.4 0.7 copy-done.10
  51.1 5.3 %pair_attended.1 = (bf16[4,2,128,512]{3,2,1,0:T(8,128)(2,1)}, bf16[2,2,128,512]{3,2,1,0:T(8,128)(2,1)}, bf16[2,2,128,512]{3,2,1,0:T(8,128)(2,1)}) custom-call(s32[1]{0:T(128)} %bitcast.me_ref, bf16[512,2048]{1,0:T(8,128)(2,1)} %get-tuple-element.30.after_ref.refs_1_, bf16[512,2048]{1,0:T(8,128)(2,1)} %q_ref.5, bf16[512,2048]{1,0:T(8,128)(2,1)} %q_ref.5, ...), custom_call_target="tpu_custom_call" | custom-call | flops 268435456 | bytes 10485760 | tf_op jit(solution)/shard_map/pair_attended/pallas_call | solution.py:393
  56.5 1.4 %collective-permute-start.4 = (bf16[2,2,128,512]{3,2,1,0:T(8,128)(2,1)}, bf16[2,2,128,512]{3,2,1,0:T(8,128)(2,1)}, u32[]{:S(2)}, u32[]{:S(2)}) collective-permute-start(bf16[2,2,128,512]{3,2,1,0:T(8,128)(2,1)} %get-tuple-element.33.refs_0_.after_ref), channel_id=1, source_target_pairs={{0,4},{2,6},{4,0},{6,2},{8,12},{10,14},{12,8},{14,10},{16,20},{18,... | collective-permute-start | bytes 1572872 | tf_op jit(solution)/shard_map/ppermute | solution.py:633
  57.9 6.5 %out_grad.3 = (bf16[512,2048]{1,0:T(8,128)(2,1)}, bf16[1024,128]{1,0:T(8,128)(2,1)}, bf16[1024,128]{1,0:T(8,128)(2,1)}) custom-call(s32[1]{0:T(128)} %bitcast.me_ref, s32[1]{0:T(128)} %bitcast.1.tp_ref, bf16[512,1024]{1,0:T(8,128)(2,1)} %refs_0_.3, bf16[512,1024]{1,0:T(8,128)(2,1)} %copy-done.1, ...), custom_call_target="tpu_custom_call", output_to_operand_aliasing={{0}: (7, {}), {1}: (8, {}), {2}: (9, {})} | custom-call | tf_op jit(solution)/shard_map/out_grad/pallas_call | solution.py:528
  64.5 0.8 fusion.2
  65.3 0.5 collective-permute-start.6
  65.8 0.4 collective-permute-done.5.b_ref.qd_ref
  66.3 0.6 copy-done.13
  66.9 1.8 %add_after.1.refs_1_ = bf16[1024,128]{1,0:T(8,128)(2,1)} custom-call(bf16[2,2,128,512]{3,2,1,0:T(8,128)(2,1)} %get-tuple-element.33.refs_0_.after_ref, bf16[1024,128]{1,0:T(8,128)(2,1)} %get-tuple-element.36.a_ref, bf16[1024,128]{1,0:T(8,128)(2,1)} %copy-done.13), custom_call_target="tpu_custom_call" | custom-call | tf_op jit(solution)/shard_map/add_after/pallas_call | solution.py:574
  68.7 3.4 %all-to-all-start.2 = ((bf16[8,128,128]{2,1,0:T(8,128)(2,1)}), bf16[8,128,128]{2,1,0:T(8,128)(2,1)S(1)}, u32[]{:S(2)}, u32[]{:S(2)}) async-start(bf16[8,128,128]{2,1,0:T(8,128)(2,1)} %bitcast.17), calls=%async_computation.2 | async-start | bytes 524288 | tf_op jit(solution)/shard_map/all_to_all | solution.py:639
  72.3 0.4 collective-permute-start.11
  72.7 1.9 %collective-permute-start.14 = (bf16[2,2,128,512]{3,2,1,0:T(8,128)(2,1)}, bf16[2,2,128,512]{3,2,1,0:T(8,128)(2,1)}, u32[]{:S(2)}, u32[]{:S(2)}) collective-permute-start(bf16[2,2,128,512]{3,2,1,0:T(8,128)(2,1)} %get-tuple-element.43), channel_id=1, source_target_pairs={{0,4},{2,6},{4,0},{6,2},{8,12},{10,14},{12,8},{14,10},{16,20},{18,... | collective-permute-start | bytes 1572872 | tf_op jit(solution)/shard_map/ppermute | solution.py:633
  74.9 1.6 %collective-permute-done.11.refs_7_ = bf16[512,1024]{1,0:T(8,128)(2,1)S(1)} collective-permute-done((bf16[512,1024]{1,0:T(8,128)(2,1)}, bf16[512,1024]{1,0:T(8,128)(2,1)S(1)}, u32[]{:S(2)}, u32[]{:S(2)}) %collective-permute-start.11) | collective-permute-done | bytes 1048608 | tf_op jit(solution)/shard_map/ppermute | solution.py:633
  76.5 1.0 copy-done.19
  77.5 7.1 %quad_weight.2 = (bf16[128,2048]{1,0:T(8,128)(2,1)}, bf16[128,2048]{1,0:T(8,128)(2,1)}) custom-call(s32[1]{0:T(128)} %bitcast.1.tp_ref, bf16[4,2,128,512]{3,2,1,0:T(8,128)(2,1)} %get-tuple-element.32.a_ref, bf16[2,2,128,512]{3,2,1,0:T(8,128)(2,1)} %passed_after.2.b_ref, bf16[512,1024]{1,0:T(8,128)(2,1)} %refs_0_.3, bf16[512,1024]{1,0:T(8,128)(2,1)} %copy-done.1, ...), custom_call_target="tpu_custom_call" | custom-call | flops 20000000000 | tf_op jit(solution)/shard_map/quad_weight/pallas_call | solution.py:446
  84.6 2.0 %collective-permute-start.12 = (bf16[128,2048]{1,0:T(8,128)(2,1)}, bf16[128,2048]{1,0:T(8,128)(2,1)}, u32[]{:S(2)}, u32[]{:S(2)}) collective-permute-start(bf16[128,2048]{1,0:T(8,128)(2,1)} %get-tuple-element.39), channel_id=1, source_target_pairs={{0,8},{2,10},{4,12},{6,14},{8,0},{10,2},{12,4},{14,6},{16,24},{18,... | collective-permute-start | bytes 1572872 | tf_op jit(solution)/shard_map/ppermute | solution.py:633
  86.6 0.7 broadcast_in_dim.3.start_ref
  87.4 1.7 %scan_blocks.3.refs_8_ = bf16[1024,128]{1,0:T(8,128)(2,1)} custom-call(bf16[1024,128]{1,0:T(8,128)(2,1)} %bitcast.16, f32[128,128]{1,0:T(8,128)} %broadcast_in_dim.3.start_ref, bf16[128,2048]{1,0:T(8,128)(2,1)} %get-tuple-element.38.refs_0_), custom_call_target="tpu_custom_call" | custom-call | tf_op jit(solution)/shard_map/scan_blocks/pallas_call | solution.py:266
  89.1 0.5 collective-permute-done.14.b_ref
  89.5 7.1 %quad_weight.3 = (bf16[128,2048]{1,0:T(8,128)(2,1)}, bf16[128,2048]{1,0:T(8,128)(2,1)}) custom-call(s32[1]{0:T(128)} %bitcast.1.tp_ref, bf16[4,2,128,512]{3,2,1,0:T(8,128)(2,1)} %get-tuple-element.32.a_ref, bf16[2,2,128,512]{3,2,1,0:T(8,128)(2,1)} %collective-permute-done.14.b_ref, bf16[512,1024]{1,0:T(8,128)(2,1)} %refs_0_.3, bf16[512,1024]{1,0:T(8,128)(2,1)} %copy-done.1, ...), custom_call_target="tpu_custom_call" | custom-call | flops 20000000000 | tf_op jit(solution)/shard_map/quad_weight/pallas_call | solution.py:446
  96.6 1.5 %collective-permute-start.15 = (bf16[128,2048]{1,0:T(8,128)(2,1)}, bf16[128,2048]{1,0:T(8,128)(2,1)S(1)}, u32[]{:S(2)}, u32[]{:S(2)}) collective-permute-start(bf16[128,2048]{1,0:T(8,128)(2,1)} %get-tuple-element.45), channel_id=1, source_target_pairs={{0,8},{2,10},{4,12},{6,14},{8,0},{10,2},{12,4},{14,6},{16,24},{18,... | collective-permute-start | bytes 1572872 | tf_op jit(solution)/shard_map/ppermute | solution.py:633
  98.2 4.1 %all-to-all-start.3 = ((bf16[8,128,128]{2,1,0:T(8,128)(2,1)}), bf16[8,128,128]{2,1,0:T(8,128)(2,1)S(1)}, u32[]{:S(2)}, u32[]{:S(2)}) async-start(bf16[8,128,128]{2,1,0:T(8,128)(2,1)} %bitcast.9), calls=%async_computation.3 | async-start | bytes 524288 | tf_op jit(solution)/shard_map/all_to_all | solution.py:639
  102.3 1.2 add_convert_fusion.after_ref
  103.5 3.0 %collective-permute-start.16 = (bf16[128,2048]{1,0:T(8,128)(2,1)S(1)}, bf16[128,2048]{1,0:T(8,128)(2,1)S(1)}, u32[]{:S(2)}, u32[]{:S(2)}) collective-permute-start(bf16[128,2048]{1,0:T(8,128)(2,1)S(1)} %add_convert_fusion.after_ref), channel_id=1, source_target_pairs={{0,16},{2,18},{4,20},{6,22},{8,24},{10,26},{12,28},{14,30},{16,0},... | collective-permute-start | bytes 1572872 | tf_op jit(solution)/shard_map/ppermute | solution.py:633
  106.5 8.2 %query_grad.1.refs_1_.after_ref = bf16[512,2048]{1,0:T(8,128)(2,1)} custom-call(s32[1]{0:T(128)} %bitcast.me_ref, bf16[128,2048]{1,0:T(8,128)(2,1)} %copy-done.11, bf16[512,2048]{1,0:T(8,128)(2,1)} %get-tuple-element.40.g_ref, bf16[512,2048]{1,0:T(8,128)(2,1)} %v_ref.3, bf16[512,2048]{1,0:T(8,128)(2,1)} %k_ref.3, bf16[1024,128]{1,0:T(8,128)(2,1)} %bitcast.14, ...), custom_call_target="tpu_custom_call" | custom-call | tf_op jit(solution)/shard_map/query_grad/pallas_call | solution.py:483
  114.7 6.6 %all-to-all-done.3 = bf16[8,128,128]{2,1,0:T(8,128)(2,1)S(1)} async-done(((bf16[8,128,128]{2,1,0:T(8,128)(2,1)}), bf16[8,128,128]{2,1,0:T(8,128)(2,1)S(1)}, u32[]{:S(2)}, u32[]{:S(2)}) %all-to-all-start.3) | async-done | bytes 262176 | tf_op jit(solution)/shard_map/all_to_all | solution.py:639
  121.3 0.7 copy-done.5
  122.0 1.0 add_convert_fusion.1
  123.1 1.5 %collective-permute-done.13.t_ref = bf16[1024,128]{1,0:T(8,128)(2,1)S(1)} collective-permute-done((bf16[1024,128]{1,0:T(8,128)(2,1)S(1)}, bf16[1024,128]{1,0:T(8,128)(2,1)S(1)}, u32[]{:S(2)}, u32[]{:S(2)}) %collective-permute-start.13) | collective-permute-done | bytes 262176 | tf_op jit(solution)/shard_map/ppermute | solution.py:633
  124.6 0.7 copy-done.17
  125.3 13.8 %key_value_grad.1 = (bf16[512,2048]{1,0:T(8,128)(2,1)}, bf16[512,2048]{1,0:T(8,128)(2,1)}) custom-call(s32[1]{0:T(128)} %bitcast.me_ref, bf16[512,2048]{1,0:T(8,128)(2,1)} %query_grad.1.refs_1_.after_ref, bf16[512,2048]{1,0:T(8,128)(2,1)} %q_ref.5, bf16[512,2048]{1,0:T(8,128)(2,1)} %k_ref.3, bf16[512,2048]{1,0:T(8,128)(2,1)} %v_ref.3, ...), custom_call_target="tpu_custom_call" | custom-call | tf_op jit(solution)/shard_map/key_value_grad/pallas_call | solution.py:609
  139.2 1.2 convert_add_fusion
  (55 shorter events, 1.4 us)
Async XLA Ops:
  0.6 17.4 %copy-start = (f32[16,128,128]{2,1,0:T(8,128)S(1)}, f32[16,128,128]{2,1,0:T(8,128)}, u32[]{:S(2)}) copy-start(f32[16,128,128]{2,1,0:T(8,128)} %param.11) | copy-start | bytes 3145732
  0.6 30.6 %collective-permute-start = (bf16[512,1024]{1,0:T(8,128)(2,1)}, bf16[512,1024]{1,0:T(8,128)(2,1)S(1)}, u32[]{:S(2)}, u32[]{:S(2)}) collective-permute-start(bf16[512,1024]{1,0:T(8,128)(2,1)} %refs_0_.3), channel_id=1, source_target_pairs={{0,1},{1,0},{2,3},{3,2},{4,5},{5,4},{6,7},{7,6},{8,9},{9,8},{10,11... | collective-permute-start | bytes 3145736 | tf_op jit(solution)/shard_map/ppermute | solution.py:636
  3.6 27.6 %collective-permute-start.2 = (bf16[512,1024]{1,0:T(8,128)(2,1)}, bf16[512,1024]{1,0:T(8,128)(2,1)}, u32[]{:S(2)}, u32[]{:S(2)}) collective-permute-start(bf16[512,1024]{1,0:T(8,128)(2,1)} %refs_0_.3), channel_id=1, source_target_pairs={{0,4},{2,6},{4,0},{6,2},{8,12},{10,14},{12,8},{14,10},{16,20},{18,... | collective-permute-start | bytes 3145736 | tf_op jit(solution)/shard_map/ppermute | solution.py:633
  9.6 1.7 %collective-permute-start.1 = (bf16[1024,128]{1,0:T(8,128)(2,1)}, bf16[1024,128]{1,0:T(8,128)(2,1)S(1)}, u32[]{:S(2)}, u32[]{:S(2)}) collective-permute-start(bf16[1024,128]{1,0:T(8,128)(2,1)} %get-tuple-element.26), channel_id=1, source_target_pairs={{0,2},{2,0},{4,6},{6,4},{8,10},{10,8},{12,14},{14,12},{16,18},{18,... | collective-permute-start | bytes 786440 | tf_op jit(solution)/shard_map/ppermute | solution.py:633
  11.4 16.7 %copy-start.8 = (bf16[1024,128]{1,0:T(8,128)(2,1)}, bf16[1024,128]{1,0:T(8,128)(2,1)S(1)}, u32[]{:S(2)}) copy-start(bf16[1024,128]{1,0:T(8,128)(2,1)S(1)} %collective-permute-done.1.oth_ref.kv_ref) | copy-start | bytes 786436
  13.2 18.1 %all-to-all-start = ((bf16[8,128,128]{2,1,0:T(8,128)(2,1)}), bf16[8,128,128]{2,1,0:T(8,128)(2,1)S(1)}, u32[]{:S(2)}, u32[]{:S(2)}) async-start(bf16[8,128,128]{2,1,0:T(8,128)(2,1)} %bitcast.2), calls=%async_computation | async-start | bytes 524288 | tf_op jit(solution)/shard_map/all_to_all | solution.py:639
  31.3 0.7 copy-start.15
  31.3 1.1 copy-start.1
  34.0 15.7 %collective-permute-start.3 = (bf16[2048,512]{1,0:T(8,128)(2,1)}, bf16[2048,512]{1,0:T(8,128)(2,1)S(1)}, u32[]{:S(2)}, u32[]{:S(2)}) collective-permute-start(bf16[2048,512]{1,0:T(8,128)(2,1)} %get-tuple-element.31), channel_id=1, source_target_pairs={{0,2},{2,0},{4,6},{6,4},{8,10},{10,8},{12,14},{14,12},{16,18},{18,... | collective-permute-start | bytes 6291464 | tf_op jit(solution)/shard_map/ppermute | solution.py:633
  34.0 38.3 %collective-permute-start.9 = (bf16[512,1024]{1,0:T(8,128)(2,1)}, bf16[512,1024]{1,0:T(8,128)(2,1)}, u32[]{:S(2)}, u32[]{:S(2)}) collective-permute-start(bf16[512,1024]{1,0:T(8,128)(2,1)} %collective-permute-done.2.refs_2_.refs_1_.refs_4_), channel_id=1, source_target_pairs={{0,1},{1,0},{2,3},{3,2},{4,5},{5,4},{6,7},{7,6},{8,9},{9,8},{10,11... | collective-permute-start | bytes 3145736 | tf_op jit(solution)/shard_map/ppermute | solution.py:636
  34.4 15.3 %all-to-all-start.1 = ((bf16[8,128,128]{2,1,0:T(8,128)(2,1)}), bf16[8,128,128]{2,1,0:T(8,128)(2,1)S(1)}, u32[]{:S(2)}, u32[]{:S(2)}) async-start(bf16[8,128,128]{2,1,0:T(8,128)(2,1)} %bitcast.19), calls=%async_computation.1 | async-start | bytes 524288 | tf_op jit(solution)/shard_map/all_to_all | solution.py:639
  49.7 0.7 copy-start.3
  49.7 1.4 copy-start.10
  56.5 16.2 %collective-permute-start.4 = (bf16[2,2,128,512]{3,2,1,0:T(8,128)(2,1)}, bf16[2,2,128,512]{3,2,1,0:T(8,128)(2,1)}, u32[]{:S(2)}, u32[]{:S(2)}) collective-permute-start(bf16[2,2,128,512]{3,2,1,0:T(8,128)(2,1)} %get-tuple-element.33.refs_0_.after_ref), channel_id=1, source_target_pairs={{0,4},{2,6},{4,0},{6,2},{8,12},{10,14},{12,8},{14,10},{16,20},{18,... | collective-permute-start | bytes 1572872 | tf_op jit(solution)/shard_map/ppermute | solution.py:633
  57.9 6.6 %copy-start.4 = (bf16[8,128,128]{2,1,0:T(8,128)(2,1)S(1)}, bf16[8,128,128]{2,1,0:T(8,128)(2,1)}, u32[]{:S(2)}) copy-start(bf16[8,128,128]{2,1,0:T(8,128)(2,1)} %copy-done.3) | copy-start | bytes 786436
  57.9 6.6 %copy-start.9 = (bf16[1024,128]{1,0:T(8,128)(2,1)S(1)}, bf16[1024,128]{1,0:T(8,128)(2,1)}, u32[]{:S(2)}) copy-start(bf16[1024,128]{1,0:T(8,128)(2,1)} %get-tuple-element.25.own_ref) | copy-start | bytes 786436
  57.9 7.9 %copy-start.6 = (bf16[512,1024]{1,0:T(8,128)(2,1)S(1)}, bf16[512,1024]{1,0:T(8,128)(2,1)}, u32[]{:S(2)}) copy-start(bf16[512,1024]{1,0:T(8,128)(2,1)} %refs_0_.3) | copy-start | bytes 3145732
  64.4 7.7 %copy-start.2 = (bf16[512,1024]{1,0:T(8,128)(2,1)S(1)}, bf16[512,1024]{1,0:T(8,128)(2,1)}, u32[]{:S(2)}) copy-start(bf16[512,1024]{1,0:T(8,128)(2,1)} %copy-done.1) | copy-start | bytes 3145732
  64.4 1.8 %collective-permute-start.5 = (bf16[1024,128]{1,0:T(8,128)(2,1)}, bf16[1024,128]{1,0:T(8,128)(2,1)S(1)}, u32[]{:S(2)}, u32[]{:S(2)}) collective-permute-start(bf16[1024,128]{1,0:T(8,128)(2,1)} %get-tuple-element.37), channel_id=1, source_target_pairs={{0,2},{2,0},{4,6},{6,4},{8,10},{10,8},{12,14},{14,12},{16,18},{18,... | collective-permute-start | bytes 786440 | tf_op jit(solution)/shard_map/ppermute | solution.py:633
  65.3 6.8 %collective-permute-start.6 = (bf16[1024,128]{1,0:T(8,128)(2,1)}, bf16[1024,128]{1,0:T(8,128)(2,1)}, u32[]{:S(2)}, u32[]{:S(2)}) collective-permute-start(bf16[1024,128]{1,0:T(8,128)(2,1)} %fusion.2), channel_id=1, source_target_pairs={{0,2},{2,0},{4,6},{6,4},{8,10},{10,8},{12,14},{14,12},{16,18},{18,... | collective-permute-start | bytes 786440 | tf_op jit(solution)/shard_map/ppermute | solution.py:633
  65.8 8.8 %collective-permute-start.7 = (bf16[512,1024]{1,0:T(8,128)(2,1)S(1)}, bf16[512,1024]{1,0:T(8,128)(2,1)}, u32[]{:S(2)}, u32[]{:S(2)}) collective-permute-start(bf16[512,1024]{1,0:T(8,128)(2,1)S(1)} %copy-done.6), channel_id=1, source_target_pairs={{0,2},{2,0},{4,6},{6,4},{8,10},{10,8},{12,14},{14,12},{16,18},{18,... | collective-permute-start | bytes 3145736 | tf_op jit(solution)/shard_map/ppermute | solution.py:633
  66.2 0.7 copy-start.13
  66.2 8.4 %collective-permute-start.10 = (bf16[512,1024]{1,0:T(8,128)(2,1)}, bf16[512,1024]{1,0:T(8,128)(2,1)}, u32[]{:S(2)}, u32[]{:S(2)}) collective-permute-start(bf16[512,1024]{1,0:T(8,128)(2,1)} %collective-permute-done.2.refs_2_.refs_1_.refs_4_), channel_id=1, source_target_pairs={{0,2},{2,0},{4,6},{6,4},{8,10},{10,8},{12,14},{14,12},{16,18},{18,... | collective-permute-start | bytes 3145736 | tf_op jit(solution)/shard_map/ppermute | solution.py:633
  68.7 17.9 %all-to-all-start.2 = ((bf16[8,128,128]{2,1,0:T(8,128)(2,1)}), bf16[8,128,128]{2,1,0:T(8,128)(2,1)S(1)}, u32[]{:S(2)}, u32[]{:S(2)}) async-start(bf16[8,128,128]{2,1,0:T(8,128)(2,1)} %bitcast.17), calls=%async_computation.2 | async-start | bytes 524288 | tf_op jit(solution)/shard_map/all_to_all | solution.py:639
  72.1 2.8 %collective-permute-start.8 = (bf16[512,1024]{1,0:T(8,128)(2,1)S(1)}, bf16[512,1024]{1,0:T(8,128)(2,1)S(1)}, u32[]{:S(2)}, u32[]{:S(2)}) collective-permute-start(bf16[512,1024]{1,0:T(8,128)(2,1)S(1)} %copy-done.2), channel_id=1, source_target_pairs={{0,2},{2,0},{4,6},{6,4},{8,10},{10,8},{12,14},{14,12},{16,18},{18,... | collective-permute-start | bytes 3145736 | tf_op jit(solution)/shard_map/ppermute | solution.py:633
  72.3 4.2 %collective-permute-start.11 = (bf16[512,1024]{1,0:T(8,128)(2,1)}, bf16[512,1024]{1,0:T(8,128)(2,1)S(1)}, u32[]{:S(2)}, u32[]{:S(2)}) collective-permute-start(bf16[512,1024]{1,0:T(8,128)(2,1)} %collective-permute-done.9.refs_5_), channel_id=1, source_target_pairs={{0,2},{2,0},{4,6},{6,4},{8,10},{10,8},{12,14},{14,12},{16,18},{18,... | collective-permute-start | bytes 3145736 | tf_op jit(solution)/shard_map/ppermute | solution.py:633
  72.7 16.9 %collective-permute-start.14 = (bf16[2,2,128,512]{3,2,1,0:T(8,128)(2,1)}, bf16[2,2,128,512]{3,2,1,0:T(8,128)(2,1)}, u32[]{:S(2)}, u32[]{:S(2)}) collective-permute-start(bf16[2,2,128,512]{3,2,1,0:T(8,128)(2,1)} %get-tuple-element.43), channel_id=1, source_target_pairs={{0,4},{2,6},{4,0},{6,2},{8,12},{10,14},{12,8},{14,10},{16,20},{18,... | collective-permute-start | bytes 1572872 | tf_op jit(solution)/shard_map/ppermute | solution.py:633
  74.9 1.6 %copy-start.18 = (bf16[512,1024]{1,0:T(8,128)(2,1)}, bf16[512,1024]{1,0:T(8,128)(2,1)S(1)}, u32[]{:S(2)}) copy-start(bf16[512,1024]{1,0:T(8,128)(2,1)S(1)} %collective-permute-done.8.refs_3_) | copy-start | bytes 3145732
  76.5 1.0 copy-start.19
  84.6 17.7 %collective-permute-start.12 = (bf16[128,2048]{1,0:T(8,128)(2,1)}, bf16[128,2048]{1,0:T(8,128)(2,1)}, u32[]{:S(2)}, u32[]{:S(2)}) collective-permute-start(bf16[128,2048]{1,0:T(8,128)(2,1)} %get-tuple-element.39), channel_id=1, source_target_pairs={{0,8},{2,10},{4,12},{6,14},{8,0},{10,2},{12,4},{14,6},{16,24},{18,... | collective-permute-start | bytes 1572872 | tf_op jit(solution)/shard_map/ppermute | solution.py:633
  86.6 0.8 copy-start.14
  89.1 13.2 %copy-start.12 = (bf16[128,2048]{1,0:T(8,128)(2,1)S(1)}, bf16[128,2048]{1,0:T(8,128)(2,1)}, u32[]{:S(2)}) copy-start(bf16[128,2048]{1,0:T(8,128)(2,1)} %get-tuple-element.38.refs_0_) | copy-start | bytes 1572868
  96.6 42.5 %collective-permute-start.15 = (bf16[128,2048]{1,0:T(8,128)(2,1)}, bf16[128,2048]{1,0:T(8,128)(2,1)S(1)}, u32[]{:S(2)}, u32[]{:S(2)}) collective-permute-start(bf16[128,2048]{1,0:T(8,128)(2,1)} %get-tuple-element.45), channel_id=1, source_target_pairs={{0,8},{2,10},{4,12},{6,14},{8,0},{10,2},{12,4},{14,6},{16,24},{18,... | collective-permute-start | bytes 1572872 | tf_op jit(solution)/shard_map/ppermute | solution.py:633
  98.2 23.1 %all-to-all-start.3 = ((bf16[8,128,128]{2,1,0:T(8,128)(2,1)}), bf16[8,128,128]{2,1,0:T(8,128)(2,1)S(1)}, u32[]{:S(2)}, u32[]{:S(2)}) async-start(bf16[8,128,128]{2,1,0:T(8,128)(2,1)} %bitcast.9), calls=%async_computation.3 | async-start | bytes 524288 | tf_op jit(solution)/shard_map/all_to_all | solution.py:639
  103.5 3.0 %copy-start.11 = (bf16[128,2048]{1,0:T(8,128)(2,1)}, bf16[128,2048]{1,0:T(8,128)(2,1)S(1)}, u32[]{:S(2)}) copy-start(bf16[128,2048]{1,0:T(8,128)(2,1)S(1)} %add_convert_fusion.after_ref) | copy-start | bytes 1572868
  103.5 35.6 %collective-permute-start.16 = (bf16[128,2048]{1,0:T(8,128)(2,1)S(1)}, bf16[128,2048]{1,0:T(8,128)(2,1)S(1)}, u32[]{:S(2)}, u32[]{:S(2)}) collective-permute-start(bf16[128,2048]{1,0:T(8,128)(2,1)S(1)} %add_convert_fusion.after_ref), channel_id=1, source_target_pairs={{0,16},{2,18},{4,20},{6,22},{8,24},{10,26},{12,28},{14,30},{16,0},... | collective-permute-start | bytes 1572872 | tf_op jit(solution)/shard_map/ppermute | solution.py:633
  114.7 7.3 %copy-start.7 = (bf16[1024,128]{1,0:T(8,128)(2,1)S(1)}, bf16[1024,128]{1,0:T(8,128)(2,1)}, u32[]{:S(2)}) copy-start(bf16[1024,128]{1,0:T(8,128)(2,1)} %get-tuple-element.36.a_ref) | copy-start | bytes 786436
  121.3 0.7 copy-start.5
  123.0 16.1 %copy-start.16 = (bf16[128,2048]{1,0:T(8,128)(2,1)S(1)}, bf16[128,2048]{1,0:T(8,128)(2,1)}, u32[]{:S(2)}) copy-start(bf16[128,2048]{1,0:T(8,128)(2,1)} %get-tuple-element.44) | copy-start | bytes 1572868
  123.0 1.6 %collective-permute-start.13 = (bf16[1024,128]{1,0:T(8,128)(2,1)S(1)}, bf16[1024,128]{1,0:T(8,128)(2,1)S(1)}, u32[]{:S(2)}, u32[]{:S(2)}) collective-permute-start(bf16[1024,128]{1,0:T(8,128)(2,1)S(1)} %add_convert_fusion.1), channel_id=1, source_target_pairs={{0,2},{2,0},{4,6},{6,4},{8,10},{10,8},{12,14},{14,12},{16,18},{18,... | collective-permute-start | bytes 786440 | tf_op jit(solution)/shard_map/ppermute | solution.py:633
  124.6 0.7 copy-start.17

commit v3 on v2

--- a/solution.py
+++ b/solution.py
@@ -9,6 +9,8 @@
 
 BF = jnp.bfloat16
 F32 = jnp.float32
+NEAR = 0
+SCAN = 2e10
 VMEM_LIMIT = 56 * 1024 * 1024
 
 
@@ -272,7 +274,7 @@
         + [jax.ShapeDtypeStruct(p.shape, p.dtype) for p in more],
         input_output_aliases={2 + len(after): 1} if more else {},
         compiler_params=params(),
-        cost_estimate=cost(0, 0),
+        cost_estimate=cost(SCAN, 0),
         name="scan_blocks",
     )(x, start, *after, *more)
     return out if more else out[0]
@@ -456,7 +458,7 @@
         ),
         out_shape=[jax.ShapeDtypeStruct((head, 2 * feat), BF)] * half,
         compiler_params=params(),
-        cost_estimate=cost(2e10, 0),
+        cost_estimate=cost(2e10 if far_side else NEAR, 0),
         name="quad_weight",
     )(tp, a, b, *cots, *after)
 
@@ -514,38 +516,34 @@
             o_ref[at, :] = dot(q_ref[:, pick], g_ref[:, pick], 0, 0).astype(BF)
 
 
-def pair_grad(me, tp, part, after, passed, own, far, w, q, head):
+def pair_grad(me, tp, after, own, far, w, q, head):
     tok, feat = own.shape
     width = q.shape[1]
-    step = min(4 * head, width // 2)
-    base = part * (width // 2 // step)
+    step = min(4 * head, width)
     whole = pl.BlockSpec((tok, feat), lambda i, m, t: (0, 0))
-    rows = pl.BlockSpec((step // 2, head), lambda i, m, t: (i + base, 0))
-    cols = pl.BlockSpec((tok, step), lambda i, m, t: (0, i + base))
+    rows = pl.BlockSpec((step // 2, head), lambda i, m, t: (i, 0))
+    cols = pl.BlockSpec((tok, step), lambda i, m, t: (0, i))
     sums = jax.ShapeDtypeStruct((width // 2, head), BF)
-    shapes = [jax.ShapeDtypeStruct((tok, width), BF), sums, sums]
-    shapes += [jax.ShapeDtypeStruct(p.shape, p.dtype) for p in passed[3:]]
-    return pl.pallas_call(
-        functools.partial(pair_grad_kernel, head, len(after) + len(passed)),
+    return pl.pallas_call(
+        functools.partial(pair_grad_kernel, head, len(after)),
         grid_spec=pltpu.PrefetchScalarGridSpec(
             num_scalar_prefetch=2,
-            grid=(width // 2 // step,),
+            grid=(width // step,),
             in_specs=[
                 whole,
                 whole,
-                pl.BlockSpec((step, 2 * feat), lambda i, m, t: (i + base, 0)),
+                pl.BlockSpec((step, 2 * feat), lambda i, m, t: (i, 0)),
                 cols,
             ]
-            + [ANY] * (len(after) + len(passed)),
-            out_specs=[cols, rows, rows] + [ANY] * len(passed[3:]),
+            + [ANY] * len(after),
+            out_specs=[cols, rows, rows],
             scratch_shapes=[pltpu.VMEM((tok, 2 * feat), BF)],
         ),
-        out_shape=shapes,
-        input_output_aliases={6 + len(after) + i: i for i in range(len(passed))},
-        compiler_params=params(),
-        cost_estimate=cost(2 * tok * feat * width * (1 - part), 3 * feat * width * (1 - part)),
+        out_shape=[jax.ShapeDtypeStruct((tok, width), BF), sums, sums],
+        compiler_params=params(),
+        cost_estimate=cost(4 * tok * feat * width, 4 * feat * width + 4 * tok * width),
         name="out_grad",
-    )(me, tp, own, far, w, q, *after, *passed)
+    )(me, tp, own, far, w, q, *after)
 
 
 def pass_kernel(*refs):
@@ -582,43 +580,65 @@
     )(after, a, b)
 
 
-def pair_key_value_kernel(head, me_ref, after_ref, q_ref, k_ref, v_ref, g_ref, s_ref, qd_ref, t_ref, ko_ref, vo_ref):
-    core = me_ref[0] % 2
+def key_value_inner_kernel(head, after_ref, q_ref, k_ref, v_ref, g_ref, ko_ref, vo_ref):
     half = g_ref.shape[0] // 2
     for j in range(g_ref.shape[1] // head):
+        at = slice(j * head, (j + 1) * head)
+        q, k, v, g = q_ref[:, at], k_ref[:, at], v_ref[:, at], g_ref[:, at]
+        first, second = causal_apply(v, g, q, True)
+        ko_ref[:half, at] = first.astype(BF)
+        ko_ref[half:, at] = second.astype(BF)
+        first, second = causal_apply(k, q, g, True)
+        vo_ref[:half, at] = first.astype(BF)
+        vo_ref[half:, at] = second.astype(BF)
+
+
+def key_value_inner(after, q, k, v, g, head):
+    tok, width = g.shape
+    step = min(4 * head, width)
+    spec = pl.BlockSpec((tok, step), lambda i: (0, i))
+    shape = jax.ShapeDtypeStruct((tok, width), BF)
+    return pl.pallas_call(
+        functools.partial(key_value_inner_kernel, head),
+        grid=(width // step,),
+        in_specs=[ANY, spec, spec, spec, spec],
+        out_specs=[spec, spec],
+        out_shape=[shape, shape],
+        compiler_params=params(),
+        cost_estimate=cost(0, 0),
+        name="key_value_inner",
+    )(after, q, k, v, g)
+
+
+def key_value_outer_kernel(head, me_ref, k_ref, v_ref, ki_ref, vi_ref, s_ref, qd_ref, t_ref, ko_ref, vo_ref):
+    core = me_ref[0] % 2
+    for j in range(k_ref.shape[1] // head):
         at, row = slice(j * head, (j + 1) * head), slice(j // 2 * head, (j // 2 + 1) * head)
         near = s_ref[row, :].astype(F32) + (1 - core).astype(F32) * qd_ref[row, :].astype(F32)
-        q, k, v, g = q_ref[:, at], k_ref[:, at], v_ref[:, at], g_ref[:, at]
         adj = jnp.where(core == j % 2, near.astype(BF), t_ref[row, :])
-        first, second = causal_apply(v, g, q, True)
-        over = dot(v, adj, 1, 1)
-        ko_ref[:half, at] = (first + over[:half]).astype(BF)
-        ko_ref[half:, at] = (second + over[half:]).astype(BF)
-        first, second = causal_apply(k, q, g, True)
-        over = dot(k, adj, 1, 0)
-        vo_ref[:half, at] = (first + over[:half]).astype(BF)
-        vo_ref[half:, at] = (second + over[half:]).astype(BF)
-
-
-def pair_key_value_grad(me, after, q, k, v, g, adjoint, qd, other, head):
-    tok, width = g.shape
+        ko_ref[:, at] = (dot(v_ref[:, at], adj, 1, 1) + ki_ref[:, at].astype(F32)).astype(BF)
+        vo_ref[:, at] = (dot(k_ref[:, at], adj, 1, 0) + vi_ref[:, at].astype(F32)).astype(BF)
+
+
+def key_value_outer(me, k, v, key_inner, value_inner, adjoint, qd, other, head):
+    tok, width = k.shape
     step = min(4 * head, width)
     spec = pl.BlockSpec((tok, step), lambda i, m: (0, i))
     rows = pl.BlockSpec((step // 2, head), lambda i, m: (i, 0))
     shape = jax.ShapeDtypeStruct((tok, width), BF)
     return pl.pallas_call(
-        functools.partial(pair_key_value_kernel, head),
+        functools.partial(key_value_outer_kernel, head),
         grid_spec=pltpu.PrefetchScalarGridSpec(
             num_scalar_prefetch=1,
             grid=(width // step,),
-            in_specs=[ANY, spec, spec, spec, spec, rows, rows, rows],
+            in_specs=[spec, spec, spec, spec, rows, rows, rows],
             out_specs=[spec, spec],
         ),
         out_shape=[shape, shape],
         compiler_params=params(),
         cost_estimate=cost(0, 0),
-        name="key_value_grad",
-    )(me, after, q, k, v, g, adjoint, qd, other)
+        name="key_value_outer",
+    )(me, k, v, key_inner, value_inner, adjoint, qd, other)
 
 
 def local_paired(queries, keys, values, cotangent, out_weight, memory):
@@ -652,22 +672,22 @@
     state = across(scanned)
 
     far_south = swap_tp(south)
-    early = pair_grad(who, which, 0, (scanned, south), (), cotangent, far, out_weight, queries, head)
+    grad, qd_mine, qd_send = pair_grad(
+        who, which, (scanned, south), cotangent, far, out_weight, queries, head
+    )
     mine, send, send_near = pair_attended(
-        who, early[0], queries, inner, swap(sent, 1), state, kv_mine, kv_other, head
+        who, grad, queries, inner, swap(sent, 1), state, kv_mine, kv_other, head
     )
     received, received_near = swap(send, 2), swap(send_near, 2)
     state_other = swap(added(state, 1.0 - core, kv_mine), 1)
 
-    grad, qd_mine, qd_send = pair_grad(
-        who, which, 1, (send,), early, cotangent, far, out_weight, queries, head
-    )
     qd_other = swap(qd_send, 1)
     chip = add_after(send, qd_mine, qd_other)
+    query_g = pair_query_grad(who, chip, grad, values, keys, state, kv_other, state_other, head)
     cots = [cotangent, far, swap(cotangent, 1), swap(far, 1)]
     cots += [south, far_south, swap(south, 1), swap(far_south, 1)]
 
-    received = passed_after(received, (chip, state_other), 2e10)
+    received = passed_after(received, (query_g,), 2e10)
     crossing = quad_weight(which, (), mine, received, cots, 1)
     summed = added(crossing[0], 1.0, swap(crossing[1], 4))
     crossed = swap(summed, 8)
@@ -675,11 +695,11 @@
     after_chip = across(scanned)
     same = quad_weight(which, (scanned,), mine, received_near, cots, 0)
     neighbour = swap(same[1], 4)
-    query_g = pair_query_grad(who, summed, grad, values, keys, state, kv_other, state_other, head)
-    after_chip = passed_after(after_chip, (query_g,), 0)
+    inners = key_value_inner(same[0], queries, keys, values, grad, head)
+    after_chip = passed_after(after_chip, (inners[0],), 0)
     adjoint_other = swap(added(after_chip, core, qd_mine), 1)
-    key_g, value_g = pair_key_value_grad(
-        who, query_g, queries, keys, values, grad, after_chip, qd_other, adjoint_other, head
+    key_g, value_g = key_value_outer(
+        who, keys, values, *inners, after_chip, qd_other, adjoint_other, head
     )
     total = same[0].astype(F32) + neighbour.astype(F32) + crossed.astype(F32)
     return query_g, key_g, value_g, total

time: 141 us -> 138 us (0.979)
  waiting for transfers between devices: 18.8 us -> 10.8 us
  starting transfers between devices: 34.5 us -> 38 us
    all_to_all x4, waiting for transfers between devices: 12.7 us -> 5.43 us  [across(): return lax.all_to_all(x, 'ctx', 0, 0, axis_index_groups=groups, tiled=True)]
    ppermute x15, starting transfers between devices: 12.7 us -> 15.1 us  [swap(): return lax.ppermute(x, 'ctx', [(c, c ^ bit) for c in range(n)])]
    unnamed x40 -> x36, local copies, waits for them, and re-layouts: 5.51 us -> 5.79 us
  transfers between devices with their start and end apart: 21 -> 21, of which waited for: 9 -> 6; matrix products, arithmetic and copies ran while one was open for 4% -> 5% of each run, Pallas kernels for 51% -> 52%
where the time goes in v3:
time: 138 us; the launch traced here: 137 us
  Pallas kernels  73.5 us (53%)
  starting transfers between devices  38 us (28%)
  waiting for transfers between devices  10.8 us (8%)
  local copies, waits for them, and re-layouts  7.06 us (5%)
  other arithmetic  6.7 us (5%)
    all_to_all x4, starting transfers between devices, across(): return lax.all_to_all(x, 'ctx', 0, 0, axis_index_groups=groups, tiled=True)  19.8 us
    ppermute x15, starting transfers between devices, swap(): return lax.ppermute(x, 'ctx', [(c, c ^ bit) for c in range(n)])  15.1 us
    pallas_call x2, Pallas kernels, quad_weight(): pl.pallas_call(functools.partial(quad_weight_kernel, len(after)), grid_sp...  14.3 us
    pallas_call x1, Pallas kernels, key_value_inner(): pl.pallas_call(functools.partial(key_value_inner_kernel, head), grid=(wid...  10.3 us
    pallas_call x1, Pallas kernels, pair_grad(): pl.pallas_call(functools.partial(pair_grad_kernel, head, len(after)), gri...  9.74 us
    pallas_call x1, Pallas kernels, pair_intra(): pl.pallas_call(functools.partial(pair_intra_kernel, head, len(after)), gr...  9.36 us
    pallas_call x1, Pallas kernels, pair_query_grad(): pl.pallas_call(functools.partial(pair_query_kernel, head), grid_spec=pltp...  8.22 us
    pallas_call x1, Pallas kernels, key_value_outer(): pl.pallas_call(functools.partial(key_value_outer_kernel, head), grid_spec...  6.54 us
  transfers between devices with their start and end apart: 21, of which 6 were waited for; matrix products, arithmetic and copies ran while one was open for 5% of the time, Pallas kernels for 52%

profile of v3, /device:TPU:0, one launch (start us, length us, event | category | flops | bytes accessed | tf_op | source)
XLA Modules:
  0.0 137.0 jit_solution(6839702220828312014)
XLA Ops:
  0.6 3.0 %collective-permute-start.2 = (bf16[512,1024]{1,0:T(8,128)(2,1)}, bf16[512,1024]{1,0:T(8,128)(2,1)S(1)}, u32[]{:S(2)}, u32[]{:S(2)}) collective-permute-start(bf16[512,1024]{1,0:T(8,128)(2,1)} %refs_0_.3), channel_id=1, source_target_pairs={{0,4},{2,6},{4,0},{6,2},{8,12},{10,14},{12,8},{14,10},{16,20},{18,... | collective-permute-start | bytes 3145736 | tf_op jit(solution)/shard_map/ppermute | solution.py:653
  3.7 1.5 %collective-permute-start = (bf16[512,1024]{1,0:T(8,128)(2,1)}, bf16[512,1024]{1,0:T(8,128)(2,1)S(1)}, u32[]{:S(2)}, u32[]{:S(2)}) collective-permute-start(bf16[512,1024]{1,0:T(8,128)(2,1)} %refs_0_.3), channel_id=1, source_target_pairs={{0,1},{1,0},{2,3},{3,2},{4,5},{5,4},{6,7},{7,6},{8,9},{9,8},{10,11... | collective-permute-start | bytes 3145736 | tf_op jit(solution)/shard_map/ppermute | solution.py:656
  5.2 4.4 %pair_sums.1 = (bf16[1024,128]{1,0:T(8,128)(2,1)}, bf16[1024,128]{1,0:T(8,128)(2,1)}) custom-call(s32[1]{0:T(128)} %bitcast.me_ref, bf16[512,2048]{1,0:T(8,128)(2,1)} %k_ref.5, bf16[512,2048]{1,0:T(8,128)(2,1)} %v_ref.5), custom_call_target="tpu_custom_call" | custom-call | flops 268435456 | bytes 4194304 | tf_op jit(solution)/shard_map/pair_sums/pallas_call | solution.py:304
  9.6 1.7 %collective-permute-done.1.oth_ref.kv_ref = bf16[1024,128]{1,0:T(8,128)(2,1)S(1)} collective-permute-done((bf16[1024,128]{1,0:T(8,128)(2,1)}, bf16[1024,128]{1,0:T(8,128)(2,1)S(1)}, u32[]{:S(2)}, u32[]{:S(2)}) %collective-permute-start.1) | collective-permute-done | bytes 262176 | tf_op jit(solution)/shard_map/ppermute | solution.py:653
  11.3 1.8 %fusion.refs_0_ = bf16[1024,128]{1,0:T(8,128)(2,1)} fusion(bf16[1024,128]{1,0:T(8,128)(2,1)} %get-tuple-element.24.own_ref, bf16[1024,128]{1,0:T(8,128)(2,1)S(1)} %collective-permute-done.1.oth_ref.kv_ref), kind=kLoop, calls=%fused_computation.4 | loop fusion | flops 524288 | bytes 786432 | tf_op jit(solution)/shard_map/convert_element_type | solution.py:662
  13.2 4.9 %all-to-all-start = ((bf16[8,128,128]{2,1,0:T(8,128)(2,1)}), bf16[8,128,128]{2,1,0:T(8,128)(2,1)}, u32[]{:S(2)}, u32[]{:S(2)}) async-start(bf16[8,128,128]{2,1,0:T(8,128)(2,1)} %bitcast.17), calls=%async_computation | async-start | bytes 524288 | tf_op jit(solution)/shard_map/all_to_all | solution.py:659
  18.0 0.6 dynamic-slice_bitcast_fusion.start_ref
  18.7 9.4 %pair_intra.1 = (bf16[1024,512]{1,0:T(8,128)(2,1)}, bf16[2048,512]{1,0:T(8,128)(2,1)}) custom-call(s32[1]{0:T(128)} %bitcast.me_ref, bf16[1024,128]{1,0:T(8,128)(2,1)} %fusion.refs_0_, bf16[512,2048]{1,0:T(8,128)(2,1)} %q_ref.3, bf16[512,2048]{1,0:T(8,128)(2,1)} %k_ref.5, bf16[512,2048]{1,0:T(8,128)(2,1)} %v_ref.5), custom_call_target="tpu_custom_call" | custom-call | flops 2147483648 | bytes 9437184 | tf_op jit(solution)/shard_map/pair_intra/pallas_call | solution.py:336
  28.0 1.9 %all-to-all-done = bf16[8,128,128]{2,1,0:T(8,128)(2,1)} async-done(((bf16[8,128,128]{2,1,0:T(8,128)(2,1)}), bf16[8,128,128]{2,1,0:T(8,128)(2,1)}, u32[]{:S(2)}, u32[]{:S(2)}) %all-to-all-start) | async-done | bytes 262176 | tf_op jit(solution)/shard_map/all_to_all | solution.py:659
  30.0 1.0 copy-done.8
  31.0 0.3 copy-done.9
  31.3 1.7 %scan_blocks.2 = (bf16[1024,128]{1,0:T(8,128)(2,1)}, bf16[2048,512]{1,0:T(8,128)(2,1)}) custom-call(bf16[1024,128]{1,0:T(8,128)(2,1)} %bitcast.3.x_ref, f32[128,128]{1,0:T(8,128)} %dynamic-slice_bitcast_fusion.start_ref, bf16[1024,512]{1,0:T(8,128)(2,1)} %get-tuple-element.26.refs_0_.i_ref, ...), custom_call_target="tpu_custom_call", output_to_operand_aliasing={{1}: (5, {})} | custom-call | flops 20000000000 | tf_op jit(solution)/shard_map/scan_blocks/pallas_call | solution.py:268
  33.0 1.7 %collective-permute-start.9 = (bf16[512,1024]{1,0:T(8,128)(2,1)}, bf16[512,1024]{1,0:T(8,128)(2,1)}, u32[]{:S(2)}, u32[]{:S(2)}) collective-permute-start(bf16[512,1024]{1,0:T(8,128)(2,1)} %copy-done.8), channel_id=1, source_target_pairs={{0,1},{1,0},{2,3},{3,2},{4,5},{5,4},{6,7},{7,6},{8,9},{9,8},{10,11... | collective-permute-start | bytes 3145736 | tf_op jit(solution)/shard_map/ppermute | solution.py:656
  34.7 5.8 %all-to-all-start.1 = ((bf16[8,128,128]{2,1,0:T(8,128)(2,1)}), bf16[8,128,128]{2,1,0:T(8,128)(2,1)S(1)}, u32[]{:S(2)}, u32[]{:S(2)}) async-start(bf16[8,128,128]{2,1,0:T(8,128)(2,1)} %bitcast.18), calls=%async_computation.1 | async-start | bytes 524288 | tf_op jit(solution)/shard_map/all_to_all | solution.py:659
  40.5 9.7 %out_grad.1 = (bf16[512,2048]{1,0:T(8,128)(2,1)}, bf16[1024,128]{1,0:T(8,128)(2,1)}, bf16[1024,128]{1,0:T(8,128)(2,1)}) custom-call(s32[1]{0:T(128)} %bitcast.me_ref, s32[1]{0:T(128)} %bitcast.1.tp_ref, bf16[512,1024]{1,0:T(8,128)(2,1)} %refs_0_.3, bf16[512,1024]{1,0:T(8,128)(2,1)} %copy-done.9, bf16[2048,2048]{1,0:T(8,128)(2,1)} %w_ref.1, ...), custom_call_target="tpu_custom_call" | custom-call | flops 4294967296 | bytes 12582912 | tf_op jit(solution)/shard_map/out_grad/pallas_call | solution.py:527
  50.3 1.3 copy-done.5
  51.7 5.5 %pair_attended.1 = (bf16[4,2,128,512]{3,2,1,0:T(8,128)(2,1)}, bf16[2,2,128,512]{3,2,1,0:T(8,128)(2,1)}, bf16[2,2,128,512]{3,2,1,0:T(8,128)(2,1)}) custom-call(s32[1]{0:T(128)} %bitcast.me_ref, bf16[512,2048]{1,0:T(8,128)(2,1)} %get-tuple-element.29.after_ref.g_ref, bf16[512,2048]{1,0:T(8,128)(2,1)} %q_ref.3, bf16[512,2048]{1,0:T(8,128)(2,1)} %q_ref.3, ...), custom_call_target="tpu_custom_call" | custom-call | flops 268435456 | bytes 10485760 | tf_op jit(solution)/shard_map/pair_attended/pallas_call | solution.py:395
  57.1 2.1 %collective-permute-start.12 = (bf16[2,2,128,512]{3,2,1,0:T(8,128)(2,1)}, bf16[2,2,128,512]{3,2,1,0:T(8,128)(2,1)}, u32[]{:S(2)}, u32[]{:S(2)}) collective-permute-start(bf16[2,2,128,512]{3,2,1,0:T(8,128)(2,1)} %get-tuple-element.31.after_ref), channel_id=1, source_target_pairs={{0,4},{2,6},{4,0},{6,2},{8,12},{10,14},{12,8},{14,10},{16,20},{18,... | collective-permute-start | bytes 1572872 | tf_op jit(solution)/shard_map/ppermute | solution.py:653
  59.2 1.7 %fusion.2 = bf16[1024,128]{1,0:T(8,128)(2,1)} fusion(bf16[1024,128]{1,0:T(8,128)(2,1)S(1)} %copy-done.4, f32[]{:T(128)S(6)} %sub.3, bf16[8,128,128]{2,1,0:T(8,128)(2,1)} %copy-done.1), kind=kLoop, calls=%fused_computation.6 | loop fusion | flops 655360 | bytes 786436 | tf_op jit(solution)/shard_map/convert_element_type | solution.py:662
  61.0 0.5 collective-permute-start.5
  61.5 0.5 collective-permute-start.10
  62.0 0.2 copy-done.13
  62.2 1.8 %add_after.1.after_ref = bf16[1024,128]{1,0:T(8,128)(2,1)} custom-call(bf16[2,2,128,512]{3,2,1,0:T(8,128)(2,1)} %get-tuple-element.31.after_ref, bf16[1024,128]{1,0:T(8,128)(2,1)} %get-tuple-element.32.a_ref, bf16[1024,128]{1,0:T(8,128)(2,1)} %copy-done.13), custom_call_target="tpu_custom_call" | custom-call | tf_op jit(solution)/shard_map/add_after/pallas_call | solution.py:572
  64.0 4.5 %all-to-all-start.2 = ((bf16[8,128,128]{2,1,0:T(8,128)(2,1)}), bf16[8,128,128]{2,1,0:T(8,128)(2,1)}, u32[]{:S(2)}, u32[]{:S(2)}) async-start(bf16[8,128,128]{2,1,0:T(8,128)(2,1)} %bitcast.16), calls=%async_computation.2 | async-start | bytes 524288 | tf_op jit(solution)/shard_map/all_to_all | solution.py:659
  68.6 0.3 collective-permute-start.8
  68.9 0.3 collective-permute-start.11
  69.3 8.2 %query_grad.1.refs_1_ = bf16[512,2048]{1,0:T(8,128)(2,1)} custom-call(s32[1]{0:T(128)} %bitcast.me_ref, bf16[1024,128]{1,0:T(8,128)(2,1)} %add_after.1.after_ref, bf16[512,2048]{1,0:T(8,128)(2,1)} %get-tuple-element.29.after_ref.g_ref, bf16[512,2048]{1,0:T(8,128)(2,1)} %v_ref.5, bf16[512,2048]{1,0:T(8,128)(2,1)} %k_ref.5, bf16[1024,128]{1,0:T(8,128)(2,1)} %bitcast.14, ...), custom_call_target="tpu_custom_call" | custom-call | tf_op jit(solution)/shard_map/query_grad/pallas_call | solution.py:485
  77.5 2.1 %collective-permute-start.6 = (bf16[2,2,128,512]{3,2,1,0:T(8,128)(2,1)}, bf16[2,2,128,512]{3,2,1,0:T(8,128)(2,1)}, u32[]{:S(2)}, u32[]{:S(2)}) collective-permute-start(bf16[2,2,128,512]{3,2,1,0:T(8,128)(2,1)} %get-tuple-element.35), channel_id=1, source_target_pairs={{0,4},{2,6},{4,0},{6,2},{8,12},{10,14},{12,8},{14,10},{16,20},{18,... | collective-permute-start | bytes 1572872 | tf_op jit(solution)/shard_map/ppermute | solution.py:653
  79.6 0.9 copy-done.11
  80.5 0.4 copy-done.12
  80.9 7.1 %quad_weight.2 = (bf16[128,2048]{1,0:T(8,128)(2,1)}, bf16[128,2048]{1,0:T(8,128)(2,1)}) custom-call(s32[1]{0:T(128)} %bitcast.1.tp_ref, bf16[4,2,128,512]{3,2,1,0:T(8,128)(2,1)} %get-tuple-element.34.a_ref, bf16[2,2,128,512]{3,2,1,0:T(8,128)(2,1)} %passed_after.2.b_ref, bf16[512,1024]{1,0:T(8,128)(2,1)} %refs_0_.3, bf16[512,1024]{1,0:T(8,128)(2,1)} %copy-done.9, ...), custom_call_target="tpu_custom_call" | custom-call | flops 20000000000 | tf_op jit(solution)/shard_map/quad_weight/pallas_call | solution.py:448
  88.0 1.5 %collective-permute-start.15 = (bf16[128,2048]{1,0:T(8,128)(2,1)}, bf16[128,2048]{1,0:T(8,128)(2,1)S(1)}, u32[]{:S(2)}, u32[]{:S(2)}) collective-permute-start(bf16[128,2048]{1,0:T(8,128)(2,1)} %get-tuple-element.43), channel_id=1, source_target_pairs={{0,8},{2,10},{4,12},{6,14},{8,0},{10,2},{12,4},{14,6},{16,24},{18,... | collective-permute-start | bytes 1572872 | tf_op jit(solution)/shard_map/ppermute | solution.py:653
  89.6 0.6 broadcast_in_dim.3.start_ref
  90.2 1.7 %scan_blocks.3.refs_8_ = bf16[1024,128]{1,0:T(8,128)(2,1)} custom-call(bf16[1024,128]{1,0:T(8,128)(2,1)} %bitcast.8.x_ref, f32[128,128]{1,0:T(8,128)} %broadcast_in_dim.3.start_ref, bf16[128,2048]{1,0:T(8,128)(2,1)} %get-tuple-element.36.refs_0_), custom_call_target="tpu_custom_call" | custom-call | flops 20000000000 | tf_op jit(solution)/shard_map/scan_blocks/pallas_call | solution.py:268
  91.9 7.1 %quad_weight.3 = (bf16[128,2048]{1,0:T(8,128)(2,1)}, bf16[128,2048]{1,0:T(8,128)(2,1)}) custom-call(s32[1]{0:T(128)} %bitcast.1.tp_ref, bf16[4,2,128,512]{3,2,1,0:T(8,128)(2,1)} %get-tuple-element.34.a_ref, bf16[2,2,128,512]{3,2,1,0:T(8,128)(2,1)} %collective-permute-done.6.b_ref, bf16[512,1024]{1,0:T(8,128)(2,1)} %refs_0_.3, bf16[512,1024]{1,0:T(8,128)(2,1)} %copy-done.9, ...), custom_call_target="tpu_custom_call" | custom-call | tf_op jit(solution)/shard_map/quad_weight/pallas_call | solution.py:448
  99.1 1.8 %collective-permute-start.14 = (bf16[128,2048]{1,0:T(8,128)(2,1)}, bf16[128,2048]{1,0:T(8,128)(2,1)S(1)}, u32[]{:S(2)}, u32[]{:S(2)}) collective-permute-start(bf16[128,2048]{1,0:T(8,128)(2,1)} %get-tuple-element.42), channel_id=1, source_target_pairs={{0,8},{2,10},{4,12},{6,14},{8,0},{10,2},{12,4},{14,6},{16,24},{18,... | collective-permute-start | bytes 1572872 | tf_op jit(solution)/shard_map/ppermute | solution.py:653
  100.8 4.5 %all-to-all-start.3 = ((bf16[8,128,128]{2,1,0:T(8,128)(2,1)}), bf16[8,128,128]{2,1,0:T(8,128)(2,1)S(1)}, u32[]{:S(2)}, u32[]{:S(2)}) async-start(bf16[8,128,128]{2,1,0:T(8,128)(2,1)} %bitcast.9), calls=%async_computation.3 | async-start | bytes 524288 | tf_op jit(solution)/shard_map/all_to_all | solution.py:659
  105.4 0.9 add_convert_fusion
  106.3 2.9 %collective-permute-start.16 = (bf16[128,2048]{1,0:T(8,128)(2,1)}, bf16[128,2048]{1,0:T(8,128)(2,1)S(1)}, u32[]{:S(2)}, u32[]{:S(2)}) collective-permute-start(bf16[128,2048]{1,0:T(8,128)(2,1)} %add_convert_fusion), channel_id=1, source_target_pairs={{0,16},{2,18},{4,20},{6,22},{8,24},{10,26},{12,28},{14,30},{16,0},... | collective-permute-start | bytes 1572872 | tf_op jit(solution)/shard_map/ppermute | solution.py:653
  109.2 10.3 %key_value_inner.1 = (bf16[512,2048]{1,0:T(8,128)(2,1)}, bf16[512,2048]{1,0:T(8,128)(2,1)}) custom-call(bf16[128,2048]{1,0:T(8,128)(2,1)} %get-tuple-element.37.after_ref, bf16[512,2048]{1,0:T(8,128)(2,1)} %q_ref.3, bf16[512,2048]{1,0:T(8,128)(2,1)} %k_ref.5, bf16[512,2048]{1,0:T(8,128)(2,1)} %v_ref.5, bf16[512,2048]{1,0:T(8,128)(2,1)} %get-tuple-element.29.after_ref.g_ref), custom_call_target="tpu_custom_call" | custom-call | tf_op jit(solution)/shard_map/key_value_inner/pallas_call | solution.py:601
  119.6 3.5 %all-to-all-done.3 = bf16[8,128,128]{2,1,0:T(8,128)(2,1)S(1)} async-done(((bf16[8,128,128]{2,1,0:T(8,128)(2,1)}), bf16[8,128,128]{2,1,0:T(8,128)(2,1)S(1)}, u32[]{:S(2)}, u32[]{:S(2)}) %all-to-all-start.3) | async-done | bytes 262176 | tf_op jit(solution)/shard_map/all_to_all | solution.py:659
  123.1 0.7 copy-done.2
  123.8 1.0 add_convert_fusion.1
  124.9 1.5 %collective-permute-done.13.t_ref = bf16[1024,128]{1,0:T(8,128)(2,1)S(1)} collective-permute-done((bf16[1024,128]{1,0:T(8,128)(2,1)S(1)}, bf16[1024,128]{1,0:T(8,128)(2,1)S(1)}, u32[]{:S(2)}, u32[]{:S(2)}) %collective-permute-start.13) | collective-permute-done | bytes 262176 | tf_op jit(solution)/shard_map/ppermute | solution.py:653
  126.4 0.7 copy-done.17
  127.2 6.5 %key_value_outer.1 = (bf16[512,2048]{1,0:T(8,128)(2,1)}, bf16[512,2048]{1,0:T(8,128)(2,1)}) custom-call(s32[1]{0:T(128)} %bitcast.me_ref, bf16[512,2048]{1,0:T(8,128)(2,1)} %k_ref.5, bf16[512,2048]{1,0:T(8,128)(2,1)} %v_ref.5, bf16[512,2048]{1,0:T(8,128)(2,1)} %get-tuple-element.38.refs_1_.ki_ref, bf16[512,2048]{1,0:T(8,128)(2,1)} %get-tuple-element.39.vi_ref, ...), custom_call_target="tpu_custom_call" | custom-call | tf_op jit(solution)/shard_map/key_value_outer/pallas_call | solution.py:629
  133.7 2.0 %collective-permute-done.16 = bf16[128,2048]{1,0:T(8,128)(2,1)S(1)} collective-permute-done((bf16[128,2048]{1,0:T(8,128)(2,1)}, bf16[128,2048]{1,0:T(8,128)(2,1)S(1)}, u32[]{:S(2)}, u32[]{:S(2)}) %collective-permute-start.16) | collective-permute-done | bytes 524320 | tf_op jit(solution)/shard_map/ppermute | solution.py:653
  135.8 1.2 convert_add_fusion
  (51 shorter events, 0.4 us)
Async XLA Ops:
  0.6 17.4 %copy-start = (f32[16,128,128]{2,1,0:T(8,128)S(1)}, f32[16,128,128]{2,1,0:T(8,128)}, u32[]{:S(2)}) copy-start(f32[16,128,128]{2,1,0:T(8,128)} %param.11) | copy-start | bytes 3145732
  0.6 29.3 %collective-permute-start.2 = (bf16[512,1024]{1,0:T(8,128)(2,1)}, bf16[512,1024]{1,0:T(8,128)(2,1)S(1)}, u32[]{:S(2)}, u32[]{:S(2)}) collective-permute-start(bf16[512,1024]{1,0:T(8,128)(2,1)} %refs_0_.3), channel_id=1, source_target_pairs={{0,4},{2,6},{4,0},{6,2},{8,12},{10,14},{12,8},{14,10},{16,20},{18,... | collective-permute-start | bytes 3145736 | tf_op jit(solution)/shard_map/ppermute | solution.py:653
  3.7 26.3 %collective-permute-start = (bf16[512,1024]{1,0:T(8,128)(2,1)}, bf16[512,1024]{1,0:T(8,128)(2,1)S(1)}, u32[]{:S(2)}, u32[]{:S(2)}) collective-permute-start(bf16[512,1024]{1,0:T(8,128)(2,1)} %refs_0_.3), channel_id=1, source_target_pairs={{0,1},{1,0},{2,3},{3,2},{4,5},{5,4},{6,7},{7,6},{8,9},{9,8},{10,11... | collective-permute-start | bytes 3145736 | tf_op jit(solution)/shard_map/ppermute | solution.py:656
  9.6 1.7 %collective-permute-start.1 = (bf16[1024,128]{1,0:T(8,128)(2,1)}, bf16[1024,128]{1,0:T(8,128)(2,1)S(1)}, u32[]{:S(2)}, u32[]{:S(2)}) collective-permute-start(bf16[1024,128]{1,0:T(8,128)(2,1)} %get-tuple-element.25), channel_id=1, source_target_pairs={{0,2},{2,0},{4,6},{6,4},{8,10},{10,8},{12,14},{14,12},{16,18},{18,... | collective-permute-start | bytes 786440 | tf_op jit(solution)/shard_map/ppermute | solution.py:653
  11.3 16.7 %copy-start.3 = (bf16[1024,128]{1,0:T(8,128)(2,1)}, bf16[1024,128]{1,0:T(8,128)(2,1)S(1)}, u32[]{:S(2)}) copy-start(bf16[1024,128]{1,0:T(8,128)(2,1)S(1)} %collective-permute-done.1.oth_ref.kv_ref) | copy-start | bytes 786436
  13.2 16.8 %all-to-all-start = ((bf16[8,128,128]{2,1,0:T(8,128)(2,1)}), bf16[8,128,128]{2,1,0:T(8,128)(2,1)}, u32[]{:S(2)}, u32[]{:S(2)}) async-start(bf16[8,128,128]{2,1,0:T(8,128)(2,1)} %bitcast.17), calls=%async_computation | async-start | bytes 524288 | tf_op jit(solution)/shard_map/all_to_all | solution.py:659
  30.0 1.0 copy-start.8
  30.0 1.3 copy-start.9
  33.0 17.3 %collective-permute-start.3 = (bf16[2048,512]{1,0:T(8,128)(2,1)}, bf16[2048,512]{1,0:T(8,128)(2,1)S(1)}, u32[]{:S(2)}, u32[]{:S(2)}) collective-permute-start(bf16[2048,512]{1,0:T(8,128)(2,1)} %get-tuple-element.30), channel_id=1, source_target_pairs={{0,2},{2,0},{4,6},{6,4},{8,10},{10,8},{12,14},{14,12},{16,18},{18,... | collective-permute-start | bytes 6291464 | tf_op jit(solution)/shard_map/ppermute | solution.py:653
  33.0 35.9 %collective-permute-start.9 = (bf16[512,1024]{1,0:T(8,128)(2,1)}, bf16[512,1024]{1,0:T(8,128)(2,1)}, u32[]{:S(2)}, u32[]{:S(2)}) collective-permute-start(bf16[512,1024]{1,0:T(8,128)(2,1)} %copy-done.8), channel_id=1, source_target_pairs={{0,1},{1,0},{2,3},{3,2},{4,5},{5,4},{6,7},{7,6},{8,9},{9,8},{10,11... | collective-permute-start | bytes 3145736 | tf_op jit(solution)/shard_map/ppermute | solution.py:656
  34.7 15.6 %all-to-all-start.1 = ((bf16[8,128,128]{2,1,0:T(8,128)(2,1)}), bf16[8,128,128]{2,1,0:T(8,128)(2,1)S(1)}, u32[]{:S(2)}, u32[]{:S(2)}) async-start(bf16[8,128,128]{2,1,0:T(8,128)(2,1)} %bitcast.18), calls=%async_computation.1 | async-start | bytes 524288 | tf_op jit(solution)/shard_map/all_to_all | solution.py:659
  50.3 1.4 %copy-start.1 = (bf16[8,128,128]{2,1,0:T(8,128)(2,1)}, bf16[8,128,128]{2,1,0:T(8,128)(2,1)S(1)}, u32[]{:S(2)}) copy-start(bf16[8,128,128]{2,1,0:T(8,128)(2,1)S(1)} %all-to-all-done.1) | copy-start | bytes 786436
  50.3 1.4 copy-start.5
  51.7 7.6 %copy-start.4 = (bf16[1024,128]{1,0:T(8,128)(2,1)S(1)}, bf16[1024,128]{1,0:T(8,128)(2,1)}, u32[]{:S(2)}) copy-start(bf16[1024,128]{1,0:T(8,128)(2,1)} %get-tuple-element.24.own_ref) | copy-start | bytes 786436
  51.7 9.8 %copy-start.7 = (bf16[512,1024]{1,0:T(8,128)(2,1)S(1)}, bf16[512,1024]{1,0:T(8,128)(2,1)}, u32[]{:S(2)}) copy-start(bf16[512,1024]{1,0:T(8,128)(2,1)} %refs_0_.3) | copy-start | bytes 3145732
  57.1 11.4 %copy-start.10 = (bf16[512,1024]{1,0:T(8,128)(2,1)S(1)}, bf16[512,1024]{1,0:T(8,128)(2,1)}, u32[]{:S(2)}) copy-start(bf16[512,1024]{1,0:T(8,128)(2,1)} %copy-done.9) | copy-start | bytes 3145732
  57.1 20.3 %collective-permute-start.12 = (bf16[2,2,128,512]{3,2,1,0:T(8,128)(2,1)}, bf16[2,2,128,512]{3,2,1,0:T(8,128)(2,1)}, u32[]{:S(2)}, u32[]{:S(2)}) collective-permute-start(bf16[2,2,128,512]{3,2,1,0:T(8,128)(2,1)} %get-tuple-element.31.after_ref), channel_id=1, source_target_pairs={{0,4},{2,6},{4,0},{6,2},{8,12},{10,14},{12,8},{14,10},{16,20},{18,... | collective-permute-start | bytes 1572872 | tf_op jit(solution)/shard_map/ppermute | solution.py:653
  59.2 2.3 %collective-permute-start.4 = (bf16[1024,128]{1,0:T(8,128)(2,1)}, bf16[1024,128]{1,0:T(8,128)(2,1)S(1)}, u32[]{:S(2)}, u32[]{:S(2)}) collective-permute-start(bf16[1024,128]{1,0:T(8,128)(2,1)} %get-tuple-element.33), channel_id=1, source_target_pairs={{0,2},{2,0},{4,6},{6,4},{8,10},{10,8},{12,14},{14,12},{16,18},{18,... | collective-permute-start | bytes 786440 | tf_op jit(solution)/shard_map/ppermute | solution.py:653
  61.0 7.6 %collective-permute-start.5 = (bf16[1024,128]{1,0:T(8,128)(2,1)}, bf16[1024,128]{1,0:T(8,128)(2,1)S(1)}, u32[]{:S(2)}, u32[]{:S(2)}) collective-permute-start(bf16[1024,128]{1,0:T(8,128)(2,1)} %fusion.2), channel_id=1, source_target_pairs={{0,2},{2,0},{4,6},{6,4},{8,10},{10,8},{12,14},{14,12},{16,18},{18,... | collective-permute-start | bytes 786440 | tf_op jit(solution)/shard_map/ppermute | solution.py:653
  61.5 18.1 %collective-permute-start.7 = (bf16[512,1024]{1,0:T(8,128)(2,1)S(1)}, bf16[512,1024]{1,0:T(8,128)(2,1)}, u32[]{:S(2)}, u32[]{:S(2)}) collective-permute-start(bf16[512,1024]{1,0:T(8,128)(2,1)S(1)} %copy-done.7), channel_id=1, source_target_pairs={{0,2},{2,0},{4,6},{6,4},{8,10},{10,8},{12,14},{14,12},{16,18},{18,... | collective-permute-start | bytes 3145736 | tf_op jit(solution)/shard_map/ppermute | solution.py:653
  61.5 0.7 copy-start.13
  61.5 18.1 %collective-permute-start.10 = (bf16[512,1024]{1,0:T(8,128)(2,1)}, bf16[512,1024]{1,0:T(8,128)(2,1)}, u32[]{:S(2)}, u32[]{:S(2)}) collective-permute-start(bf16[512,1024]{1,0:T(8,128)(2,1)} %copy-done.8), channel_id=1, source_target_pairs={{0,2},{2,0},{4,6},{6,4},{8,10},{10,8},{12,14},{14,12},{16,18},{18,... | collective-permute-start | bytes 3145736 | tf_op jit(solution)/shard_map/ppermute | solution.py:653
  64.0 25.6 %all-to-all-start.2 = ((bf16[8,128,128]{2,1,0:T(8,128)(2,1)}), bf16[8,128,128]{2,1,0:T(8,128)(2,1)}, u32[]{:S(2)}, u32[]{:S(2)}) async-start(bf16[8,128,128]{2,1,0:T(8,128)(2,1)} %bitcast.16), calls=%async_computation.2 | async-start | bytes 524288 | tf_op jit(solution)/shard_map/all_to_all | solution.py:659
  68.5 0.7 copy-start.16
  68.6 11.0 %collective-permute-start.8 = (bf16[512,1024]{1,0:T(8,128)(2,1)S(1)}, bf16[512,1024]{1,0:T(8,128)(2,1)S(1)}, u32[]{:S(2)}, u32[]{:S(2)}) collective-permute-start(bf16[512,1024]{1,0:T(8,128)(2,1)S(1)} %copy-done.10), channel_id=1, source_target_pairs={{0,2},{2,0},{4,6},{6,4},{8,10},{10,8},{12,14},{14,12},{16,18},{18,... | collective-permute-start | bytes 3145736 | tf_op jit(solution)/shard_map/ppermute | solution.py:653
  68.9 10.7 %collective-permute-start.11 = (bf16[512,1024]{1,0:T(8,128)(2,1)}, bf16[512,1024]{1,0:T(8,128)(2,1)S(1)}, u32[]{:S(2)}, u32[]{:S(2)}) collective-permute-start(bf16[512,1024]{1,0:T(8,128)(2,1)} %collective-permute-done.9.refs_5_), channel_id=1, source_target_pairs={{0,2},{2,0},{4,6},{6,4},{8,10},{10,8},{12,14},{14,12},{16,18},{18,... | collective-permute-start | bytes 3145736 | tf_op jit(solution)/shard_map/ppermute | solution.py:653
  77.5 14.5 %collective-permute-start.6 = (bf16[2,2,128,512]{3,2,1,0:T(8,128)(2,1)}, bf16[2,2,128,512]{3,2,1,0:T(8,128)(2,1)}, u32[]{:S(2)}, u32[]{:S(2)}) collective-permute-start(bf16[2,2,128,512]{3,2,1,0:T(8,128)(2,1)} %get-tuple-element.35), channel_id=1, source_target_pairs={{0,4},{2,6},{4,0},{6,2},{8,12},{10,14},{12,8},{14,10},{16,20},{18,... | collective-permute-start | bytes 1572872 | tf_op jit(solution)/shard_map/ppermute | solution.py:653
  79.6 1.0 copy-start.11
  79.6 1.3 copy-start.12
  88.0 17.3 %collective-permute-start.15 = (bf16[128,2048]{1,0:T(8,128)(2,1)}, bf16[128,2048]{1,0:T(8,128)(2,1)S(1)}, u32[]{:S(2)}, u32[]{:S(2)}) collective-permute-start(bf16[128,2048]{1,0:T(8,128)(2,1)} %get-tuple-element.43), channel_id=1, source_target_pairs={{0,8},{2,10},{4,12},{6,14},{8,0},{10,2},{12,4},{14,6},{16,24},{18,... | collective-permute-start | bytes 1572872 | tf_op jit(solution)/shard_map/ppermute | solution.py:653
  91.9 13.5 %copy-start.15 = (bf16[128,2048]{1,0:T(8,128)(2,1)S(1)}, bf16[128,2048]{1,0:T(8,128)(2,1)}, u32[]{:S(2)}) copy-start(bf16[128,2048]{1,0:T(8,128)(2,1)} %get-tuple-element.36.refs_0_) | copy-start | bytes 1572868
  99.1 34.7 %collective-permute-start.14 = (bf16[128,2048]{1,0:T(8,128)(2,1)}, bf16[128,2048]{1,0:T(8,128)(2,1)S(1)}, u32[]{:S(2)}, u32[]{:S(2)}) collective-permute-start(bf16[128,2048]{1,0:T(8,128)(2,1)} %get-tuple-element.42), channel_id=1, source_target_pairs={{0,8},{2,10},{4,12},{6,14},{8,0},{10,2},{12,4},{14,6},{16,24},{18,... | collective-permute-start | bytes 1572872 | tf_op jit(solution)/shard_map/ppermute | solution.py:653
  100.8 22.2 %all-to-all-start.3 = ((bf16[8,128,128]{2,1,0:T(8,128)(2,1)}), bf16[8,128,128]{2,1,0:T(8,128)(2,1)S(1)}, u32[]{:S(2)}, u32[]{:S(2)}) async-start(bf16[8,128,128]{2,1,0:T(8,128)(2,1)} %bitcast.9), calls=%async_computation.3 | async-start | bytes 524288 | tf_op jit(solution)/shard_map/all_to_all | solution.py:659
  106.3 29.5 %collective-permute-start.16 = (bf16[128,2048]{1,0:T(8,128)(2,1)}, bf16[128,2048]{1,0:T(8,128)(2,1)S(1)}, u32[]{:S(2)}, u32[]{:S(2)}) collective-permute-start(bf16[128,2048]{1,0:T(8,128)(2,1)} %add_convert_fusion), channel_id=1, source_target_pairs={{0,16},{2,18},{4,20},{6,22},{8,24},{10,26},{12,28},{14,30},{16,0},... | collective-permute-start | bytes 1572872 | tf_op jit(solution)/shard_map/ppermute | solution.py:653
  119.6 4.2 %copy-start.14 = (bf16[1024,128]{1,0:T(8,128)(2,1)S(1)}, bf16[1024,128]{1,0:T(8,128)(2,1)}, u32[]{:S(2)}) copy-start(bf16[1024,128]{1,0:T(8,128)(2,1)} %get-tuple-element.32.a_ref) | copy-start | bytes 786436
  123.1 0.7 copy-start.2
  124.8 1.6 %collective-permute-start.13 = (bf16[1024,128]{1,0:T(8,128)(2,1)S(1)}, bf16[1024,128]{1,0:T(8,128)(2,1)S(1)}, u32[]{:S(2)}, u32[]{:S(2)}) collective-permute-start(bf16[1024,128]{1,0:T(8,128)(2,1)S(1)} %add_convert_fusion.1), channel_id=1, source_target_pairs={{0,2},{2,0},{4,6},{6,4},{8,10},{10,8},{12,14},{14,12},{16,18},{18,... | collective-permute-start | bytes 786440 | tf_op jit(solution)/shard_map/ppermute | solution.py:653
  126.4 0.7 copy-start.17
  127.2 8.6 %copy-start.6 = (bf16[128,2048]{1,0:T(8,128)(2,1)S(1)}, bf16[128,2048]{1,0:T(8,128)(2,1)}, u32[]{:S(2)}) copy-start(bf16[128,2048]{1,0:T(8,128)(2,1)} %get-tuple-element.37.after_ref) | copy-start | bytes 1572868

commit v4 on v3

--- a/solution.py
+++ b/solution.py
@@ -252,10 +252,10 @@
 ANY = pl.BlockSpec(memory_space=pl.ANY)
 
 
-def scan_kernel(n, reverse, waits, x_ref, start_ref, *refs):
+def scan_kernel(n, reverse, waits, x_ref, *refs):
     o_ref = refs[waits]
-    rows = start_ref.shape[0]
-    total = start_ref[...]
+    rows = x_ref.shape[0] // n
+    total = jnp.zeros((rows, x_ref.shape[1]), F32) if reverse else refs[0][...]
     for i in range(n):
         c = n - 1 - i if reverse else i
         at = slice(c * rows, (c + 1) * rows)
@@ -265,18 +265,19 @@
 
 def scan_blocks(x, start, n, reverse, after=(), passed=None):
     more = () if passed is None else (passed,)
+    first = () if reverse else (start,)
     out = pl.pallas_call(
-        functools.partial(scan_kernel, n, reverse, len(after) + len(more)),
-        in_specs=[pl.BlockSpec(x.shape, lambda: (0, 0)), pl.BlockSpec(start.shape, lambda: (0, 0))]
+        functools.partial(scan_kernel, n, reverse, len(first) + len(after) + len(more)),
+        in_specs=[pl.BlockSpec(y.shape, lambda: (0, 0)) for y in (x, *first)]
         + [ANY] * (len(after) + len(more)),
         out_specs=[pl.BlockSpec(x.shape, lambda: (0, 0))] + [ANY] * len(more),
         out_shape=[jax.ShapeDtypeStruct(x.shape, BF)]
         + [jax.ShapeDtypeStruct(p.shape, p.dtype) for p in more],
-        input_output_aliases={2 + len(after): 1} if more else {},
+        input_output_aliases={1 + len(first) + len(after): 1} if more else {},
         compiler_params=params(),
         cost_estimate=cost(SCAN, 0),
         name="scan_blocks",
-    )(x, start, *after, *more)
+    )(x, *first, *after, *more)
     return out if more else out[0]
 
 
@@ -355,7 +356,7 @@
 
 
 def pair_attended_kernel(head, me_ref, after_ref, q0_ref, q1_ref, i_ref, far_ref, s_ref, own_ref, oth_ref,
-                         mine_ref, cross_ref, near_ref):
+                         mine_ref, cross_ref, near_ref, away_ref):
     core = (me_ref[0] % 2).astype(F32)
     south = (me_ref[0] // 2) % 2
 
@@ -364,6 +365,7 @@
         state = s_ref[rows, :].astype(F32)
         near = (state + core * oth_ref[rows, :].astype(F32)).astype(BF)
         away = (state + (1.0 - core) * own_ref[rows, :].astype(F32)).astype(BF)
+        away_ref[rows, :] = away
         here = dot(near, q_ref[...], 0, 1) + i_ref[rows, :].astype(F32)
         there = dot(away, far_ref[lanes(2 * side, head), :], 0, 0)
         there = there + far_ref[lanes(2 * side + 1, head), :].astype(F32)
@@ -409,9 +411,15 @@
                 out(lambda i: i ^ half),
                 out(lambda i: jnp.minimum(i, half - 1)),
                 out(lambda i: jnp.maximum(i - half, 0)),
+                rows,
             ],
         ),
-        out_shape=[shape(places), shape(half), shape(half)],
+        out_shape=[
+            shape(places),
+            shape(half),
+            shape(half),
+            jax.ShapeDtypeStruct((width // 2, head), BF),
+        ],
         compiler_params=params(),
         cost_estimate=cost(2 * tok * head * width, 10 * tok * width),
         name="pair_attended",
@@ -675,27 +683,27 @@
     grad, qd_mine, qd_send = pair_grad(
         who, which, (scanned, south), cotangent, far, out_weight, queries, head
     )
-    mine, send, send_near = pair_attended(
+    mine, send, send_near, away = pair_attended(
         who, grad, queries, inner, swap(sent, 1), state, kv_mine, kv_other, head
     )
     received, received_near = swap(send, 2), swap(send_near, 2)
-    state_other = swap(added(state, 1.0 - core, kv_mine), 1)
+    state_other = swap(away, 1)
 
     qd_other = swap(qd_send, 1)
     chip = add_after(send, qd_mine, qd_other)
-    query_g = pair_query_grad(who, chip, grad, values, keys, state, kv_other, state_other, head)
     cots = [cotangent, far, swap(cotangent, 1), swap(far, 1)]
     cots += [south, far_south, swap(south, 1), swap(far_south, 1)]
 
-    received = passed_after(received, (query_g,), 2e10)
+    received = passed_after(received, (chip, state_other), 2e10)
     crossing = quad_weight(which, (), mine, received, cots, 1)
     summed = added(crossing[0], 1.0, swap(crossing[1], 4))
     crossed = swap(summed, 8)
-    scanned = scan_blocks(across(chip), jnp.zeros_like(start), n // 2, True, (crossing[0],))
+    scanned = scan_blocks(across(chip), None, n // 2, True, (crossing[0],))
     after_chip = across(scanned)
     same = quad_weight(which, (scanned,), mine, received_near, cots, 0)
     neighbour = swap(same[1], 4)
-    inners = key_value_inner(same[0], queries, keys, values, grad, head)
+    query_g = pair_query_grad(who, summed, grad, values, keys, state, kv_other, state_other, head)
+    inners = key_value_inner(query_g, queries, keys, values, grad, head)
     after_chip = passed_after(after_chip, (inners[0],), 0)
     adjoint_other = swap(added(after_chip, core, qd_mine), 1)
     key_g, value_g = key_value_outer(
@@ -719,7 +727,7 @@
     state = carried(kv, start, "ctx", False)
     inner = intra(queries, keys, values, head)
     grad, qd = out_grad_and_sums(tp.reshape(1), cotangent, far, out_weight, queries, head)
-    adjoint = carried(qd, jnp.zeros_like(start), "ctx", True)
+    adjoint = carried(qd, None, "ctx", True)
     attended = attended_of(queries, state, inner, head)
     term = weight_term(attended, cotangent, far)
     total = lax.psum_scatter(term, "ctx", scatter_dimension=0, tiled=True)

time: 138 us -> 134 us (0.971)
  other arithmetic: 6.7 us -> 5.21 us
  waiting for transfers between devices: 10.8 us -> 9.36 us
    all_to_all x4, waiting for transfers between devices: 5.43 us -> 1.83 us  [across(): return lax.all_to_all(x, 'ctx', 0, 0, axis_index_groups=groups, tiled=True)]
    ppermute x15, waiting for transfers between devices: 5.39 us -> 7.52 us  [swap(): return lax.ppermute(x, 'ctx', [(c, c ^ bit) for c in range(n)])]
    convert_element_type x4 -> x3, other arithmetic: 5.52 us -> 4.02 us  [added(): return (x.astype(F32) + factor * y.astype(F32)).astype(BF)]
  transfers between devices with their start and end apart: 21 -> 21, of which waited for: 6 -> 5; matrix products, arithmetic and copies ran while one was open for 5% -> 3% of each run, Pallas kernels for 52% -> 54%
where the time goes in v4:
time: 134 us; the launch traced here: 133 us
  Pallas kernels  73.7 us (55%)
  starting transfers between devices  38 us (28%)
  waiting for transfers between devices  9.36 us (7%)
  local copies, waits for them, and re-layouts  6.02 us (4%)
  other arithmetic  5.21 us (4%)
    all_to_all x4, starting transfers between devices, across(): return lax.all_to_all(x, 'ctx', 0, 0, axis_index_groups=groups, tiled=True)  19.9 us
    ppermute x15, starting transfers between devices, swap(): return lax.ppermute(x, 'ctx', [(c, c ^ bit) for c in range(n)])  14.9 us
    pallas_call x2, Pallas kernels, quad_weight(): pl.pallas_call(functools.partial(quad_weight_kernel, len(after)), grid_sp...  14.3 us
    pallas_call x1, Pallas kernels, key_value_inner(): pl.pallas_call(functools.partial(key_value_inner_kernel, head), grid=(wid...  10.3 us
    pallas_call x1, Pallas kernels, pair_grad(): pl.pallas_call(functools.partial(pair_grad_kernel, head, len(after)), gri...  9.74 us
    pallas_call x1, Pallas kernels, pair_intra(): pl.pallas_call(functools.partial(pair_intra_kernel, head, len(after)), gr...  9.36 us
    pallas_call x1, Pallas kernels, pair_query_grad(): pl.pallas_call(functools.partial(pair_query_kernel, head), grid_spec=pltp...  8.23 us
    ppermute x15, waiting for transfers between devices, swap(): return lax.ppermute(x, 'ctx', [(c, c ^ bit) for c in range(n)])  7.52 us
  transfers between devices with their start and end apart: 21, of which 5 were waited for; matrix products, arithmetic and copies ran while one was open for 3% of the time, Pallas kernels for 54%

profile of v4, /device:TPU:0, one launch (start us, length us, event | category | flops | bytes accessed | tf_op | source)
XLA Modules:
  0.0 133.1 jit_solution(12613746601932165373)
XLA Ops:
  0.6 3.0 %collective-permute-start.2 = (bf16[512,1024]{1,0:T(8,128)(2,1)}, bf16[512,1024]{1,0:T(8,128)(2,1)}, u32[]{:S(2)}, u32[]{:S(2)}) collective-permute-start(bf16[512,1024]{1,0:T(8,128)(2,1)} %refs_0_.3), channel_id=1, source_target_pairs={{0,4},{2,6},{4,0},{6,2},{8,12},{10,14},{12,8},{14,10},{16,20},{18,... | collective-permute-start | bytes 3145736 | tf_op jit(solution)/shard_map/ppermute | solution.py:661
  3.7 1.5 %collective-permute-start = (bf16[512,1024]{1,0:T(8,128)(2,1)}, bf16[512,1024]{1,0:T(8,128)(2,1)S(1)}, u32[]{:S(2)}, u32[]{:S(2)}) collective-permute-start(bf16[512,1024]{1,0:T(8,128)(2,1)} %refs_0_.3), channel_id=1, source_target_pairs={{0,1},{1,0},{2,3},{3,2},{4,5},{5,4},{6,7},{7,6},{8,9},{9,8},{10,11... | collective-permute-start | bytes 3145736 | tf_op jit(solution)/shard_map/ppermute | solution.py:664
  5.2 4.4 %pair_sums.1 = (bf16[1024,128]{1,0:T(8,128)(2,1)}, bf16[1024,128]{1,0:T(8,128)(2,1)}) custom-call(s32[1]{0:T(128)} %bitcast.me_ref, bf16[512,2048]{1,0:T(8,128)(2,1)} %k_ref.5, bf16[512,2048]{1,0:T(8,128)(2,1)} %v_ref.5), custom_call_target="tpu_custom_call" | custom-call | flops 268435456 | bytes 4194304 | tf_op jit(solution)/shard_map/pair_sums/pallas_call | solution.py:305
  9.6 1.7 %collective-permute-done.1.oth_ref.kv_ref = bf16[1024,128]{1,0:T(8,128)(2,1)S(1)} collective-permute-done((bf16[1024,128]{1,0:T(8,128)(2,1)}, bf16[1024,128]{1,0:T(8,128)(2,1)S(1)}, u32[]{:S(2)}, u32[]{:S(2)}) %collective-permute-start.1) | collective-permute-done | bytes 262176 | tf_op jit(solution)/shard_map/ppermute | solution.py:661
  11.3 1.8 %add_convert_fusion.2.refs_0_ = bf16[1024,128]{1,0:T(8,128)(2,1)} fusion(bf16[1024,128]{1,0:T(8,128)(2,1)S(1)} %collective-permute-done.1.oth_ref.kv_ref, bf16[1024,128]{1,0:T(8,128)(2,1)} %get-tuple-element.25.own_ref), kind=kLoop, calls=%fused_computation.3 | loop fusion | flops 524288 | bytes 786432 | tf_op jit(solution)/shard_map/convert_element_type | solution.py:670
  13.2 4.9 %all-to-all-start = ((bf16[8,128,128]{2,1,0:T(8,128)(2,1)}), bf16[8,128,128]{2,1,0:T(8,128)(2,1)S(1)}, u32[]{:S(2)}, u32[]{:S(2)}) async-start(bf16[8,128,128]{2,1,0:T(8,128)(2,1)} %bitcast.2), calls=%async_computation | async-start | bytes 524288 | tf_op jit(solution)/shard_map/all_to_all | solution.py:667
  18.0 0.6 dynamic-slice_bitcast_fusion.refs_0_
  18.7 9.4 %pair_intra.1 = (bf16[1024,512]{1,0:T(8,128)(2,1)}, bf16[2048,512]{1,0:T(8,128)(2,1)}) custom-call(s32[1]{0:T(128)} %bitcast.me_ref, bf16[1024,128]{1,0:T(8,128)(2,1)} %add_convert_fusion.2.refs_0_, bf16[512,2048]{1,0:T(8,128)(2,1)} %q_ref.3, bf16[512,2048]{1,0:T(8,128)(2,1)} %k_ref.5, bf16[512,2048]{1,0:T(8,128)(2,1)} %v_ref.5), custom_call_target="tpu_custom_call" | custom-call | flops 2147483648 | bytes 9437184 | tf_op jit(solution)/shard_map/pair_intra/pallas_call | solution.py:337
  28.0 1.8 %all-to-all-done = bf16[8,128,128]{2,1,0:T(8,128)(2,1)S(1)} async-done(((bf16[8,128,128]{2,1,0:T(8,128)(2,1)}), bf16[8,128,128]{2,1,0:T(8,128)(2,1)S(1)}, u32[]{:S(2)}, u32[]{:S(2)}) %all-to-all-start) | async-done | bytes 262176 | tf_op jit(solution)/shard_map/all_to_all | solution.py:667
  29.9 0.7 copy-done.16
  30.6 0.4 copy-done.6
  30.9 1.7 %scan_blocks.2 = (bf16[1024,128]{1,0:T(8,128)(2,1)}, bf16[2048,512]{1,0:T(8,128)(2,1)}) custom-call(bf16[1024,128]{1,0:T(8,128)(2,1)} %bitcast.16, f32[128,128]{1,0:T(8,128)} %dynamic-slice_bitcast_fusion.refs_0_, bf16[1024,512]{1,0:T(8,128)(2,1)} %get-tuple-element.27.refs_1_.i_ref, bf16[512,1024]{1,0:T(8,128)(2,1)} %copy-done.6, ...), custom_call_target="tpu_custom_call", output_to_operand_aliasing={{1}: (5, {})} | custom-call | flops 20000000000 | tf_op jit(solution)/shard_map/scan_blocks/pallas_call | solution.py:269
  32.6 1.7 %collective-permute-start.9 = (bf16[512,1024]{1,0:T(8,128)(2,1)}, bf16[512,1024]{1,0:T(8,128)(2,1)}, u32[]{:S(2)}, u32[]{:S(2)}) collective-permute-start(bf16[512,1024]{1,0:T(8,128)(2,1)} %collective-permute-done.2.refs_3_.refs_1_.refs_4_), channel_id=1, source_target_pairs={{0,1},{1,0},{2,3},{3,2},{4,5},{5,4},{6,7},{7,6},{8,9},{9,8},{10,11... | collective-permute-start | bytes 3145736 | tf_op jit(solution)/shard_map/ppermute | solution.py:664
  34.3 5.8 %all-to-all-start.1 = ((bf16[8,128,128]{2,1,0:T(8,128)(2,1)}), bf16[8,128,128]{2,1,0:T(8,128)(2,1)S(1)}, u32[]{:S(2)}, u32[]{:S(2)}) async-start(bf16[8,128,128]{2,1,0:T(8,128)(2,1)} %bitcast.17), calls=%async_computation.1 | async-start | bytes 524288 | tf_op jit(solution)/shard_map/all_to_all | solution.py:667
  40.2 9.7 %out_grad.1 = (bf16[512,2048]{1,0:T(8,128)(2,1)}, bf16[1024,128]{1,0:T(8,128)(2,1)}, bf16[1024,128]{1,0:T(8,128)(2,1)}) custom-call(s32[1]{0:T(128)} %bitcast.me_ref, s32[1]{0:T(128)} %bitcast.1.tp_ref, bf16[512,1024]{1,0:T(8,128)(2,1)} %refs_0_.3, bf16[512,1024]{1,0:T(8,128)(2,1)} %copy-done.6, bf16[2048,2048]{1,0:T(8,128)(2,1)} %w_ref.1, ...), custom_call_target="tpu_custom_call" | custom-call | flops 4294967296 | bytes 12582912 | tf_op jit(solution)/shard_map/out_grad/pallas_call | solution.py:535
  49.9 0.7 copy-done.3
  50.6 5.6 %pair_attended.1 = (bf16[4,2,128,512]{3,2,1,0:T(8,128)(2,1)}, bf16[2,2,128,512]{3,2,1,0:T(8,128)(2,1)}, bf16[2,2,128,512]{3,2,1,0:T(8,128)(2,1)}, bf16[1024,128]{1,0:T(8,128)(2,1)}) custom-call(s32[1]{0:T(128)} %bitcast.me_ref, bf16[512,2048]{1,0:T(8,128)(2,1)} %get-tuple-element.30.after_ref.g_ref, bf16[512,2048]{1,0:T(8,128)(2,1)} %q_ref.3, ...), custom_call_target="tpu_custom_call" | custom-call | flops 268435456 | bytes 10485760 | tf_op jit(solution)/shard_map/pair_attended/pallas_call | solution.py:397
  56.2 2.1 %collective-permute-start.4 = (bf16[2,2,128,512]{3,2,1,0:T(8,128)(2,1)}, bf16[2,2,128,512]{3,2,1,0:T(8,128)(2,1)}, u32[]{:S(2)}, u32[]{:S(2)}) collective-permute-start(bf16[2,2,128,512]{3,2,1,0:T(8,128)(2,1)} %get-tuple-element.33.after_ref), channel_id=1, source_target_pairs={{0,4},{2,6},{4,0},{6,2},{8,12},{10,14},{12,8},{14,10},{16,20},{18,... | collective-permute-start | bytes 1572872 | tf_op jit(solution)/shard_map/ppermute | solution.py:661
  58.3 0.5 collective-permute-start.6
  58.8 1.4 %collective-permute-done.5.b_ref.qd_ref = bf16[1024,128]{1,0:T(8,128)(2,1)S(1)} collective-permute-done((bf16[1024,128]{1,0:T(8,128)(2,1)S(1)}, bf16[1024,128]{1,0:T(8,128)(2,1)S(1)}, u32[]{:S(2)}, u32[]{:S(2)}) %collective-permute-start.5) | collective-permute-done | bytes 262176 | tf_op jit(solution)/shard_map/ppermute | solution.py:661
  60.2 0.1 collective-permute-start.10
  60.3 0.6 copy-done.10
  60.9 1.8 %add_after.1.refs_1_ = bf16[1024,128]{1,0:T(8,128)(2,1)} custom-call(bf16[2,2,128,512]{3,2,1,0:T(8,128)(2,1)} %get-tuple-element.33.after_ref, bf16[1024,128]{1,0:T(8,128)(2,1)} %get-tuple-element.34.a_ref, bf16[1024,128]{1,0:T(8,128)(2,1)} %copy-done.10), custom_call_target="tpu_custom_call" | custom-call | tf_op jit(solution)/shard_map/add_after/pallas_call | solution.py:580
  62.7 4.5 %all-to-all-start.2 = ((bf16[8,128,128]{2,1,0:T(8,128)(2,1)}), bf16[8,128,128]{2,1,0:T(8,128)(2,1)}, u32[]{:S(2)}, u32[]{:S(2)}) async-start(bf16[8,128,128]{2,1,0:T(8,128)(2,1)} %bitcast.15), calls=%async_computation.2 | async-start | bytes 524288 | tf_op jit(solution)/shard_map/all_to_all | solution.py:667
  67.2 0.1 collective-permute-start.8
  67.3 0.5 collective-permute-start.11
  67.8 2.9 %collective-permute-done.4.refs_0_ = bf16[2,2,128,512]{3,2,1,0:T(8,128)(2,1)} collective-permute-done((bf16[2,2,128,512]{3,2,1,0:T(8,128)(2,1)}, bf16[2,2,128,512]{3,2,1,0:T(8,128)(2,1)}, u32[]{:S(2)}, u32[]{:S(2)}) %collective-permute-start.4) | collective-permute-done | bytes 524320 | tf_op jit(solution)/shard_map/ppermute | solution.py:661
  70.7 2.6 %collective-permute-start.14 = (bf16[2,2,128,512]{3,2,1,0:T(8,128)(2,1)}, bf16[2,2,128,512]{3,2,1,0:T(8,128)(2,1)}, u32[]{:S(2)}, u32[]{:S(2)}) collective-permute-start(bf16[2,2,128,512]{3,2,1,0:T(8,128)(2,1)} %get-tuple-element.43), channel_id=1, source_target_pairs={{0,4},{2,6},{4,0},{6,2},{8,12},{10,14},{12,8},{14,10},{16,20},{18,... | collective-permute-start | bytes 1572872 | tf_op jit(solution)/shard_map/ppermute | solution.py:661
  73.3 0.9 copy-done.8
  74.3 0.4 copy-done.9
  74.7 7.1 %quad_weight.2 = (bf16[128,2048]{1,0:T(8,128)(2,1)}, bf16[128,2048]{1,0:T(8,128)(2,1)}) custom-call(s32[1]{0:T(128)} %bitcast.1.tp_ref, bf16[4,2,128,512]{3,2,1,0:T(8,128)(2,1)} %get-tuple-element.32.a_ref, bf16[2,2,128,512]{3,2,1,0:T(8,128)(2,1)} %passed_after.2.b_ref, bf16[512,1024]{1,0:T(8,128)(2,1)} %refs_0_.3, bf16[512,1024]{1,0:T(8,128)(2,1)} %copy-done.6, ...), custom_call_target="tpu_custom_call" | custom-call | flops 20000000000 | tf_op jit(solution)/shard_map/quad_weight/pallas_call | solution.py:456
  81.7 2.1 %collective-permute-start.12 = (bf16[128,2048]{1,0:T(8,128)(2,1)}, bf16[128,2048]{1,0:T(8,128)(2,1)}, u32[]{:S(2)}, u32[]{:S(2)}) collective-permute-start(bf16[128,2048]{1,0:T(8,128)(2,1)} %get-tuple-element.38), channel_id=1, source_target_pairs={{0,8},{2,10},{4,12},{6,14},{8,0},{10,2},{12,4},{14,6},{16,24},{18,... | collective-permute-start | bytes 1572872 | tf_op jit(solution)/shard_map/ppermute | solution.py:661
  83.9 1.7 %scan_blocks.3.refs_8_ = bf16[1024,128]{1,0:T(8,128)(2,1)} custom-call(bf16[1024,128]{1,0:T(8,128)(2,1)} %bitcast.8.x_ref, bf16[128,2048]{1,0:T(8,128)(2,1)} %get-tuple-element.37.refs_0_), custom_call_target="tpu_custom_call" | custom-call | flops 20000000000 | tf_op jit(solution)/shard_map/scan_blocks/pallas_call | solution.py:269
  85.6 7.2 %quad_weight.3 = (bf16[128,2048]{1,0:T(8,128)(2,1)}, bf16[128,2048]{1,0:T(8,128)(2,1)}) custom-call(s32[1]{0:T(128)} %bitcast.1.tp_ref, bf16[4,2,128,512]{3,2,1,0:T(8,128)(2,1)} %get-tuple-element.32.a_ref, bf16[2,2,128,512]{3,2,1,0:T(8,128)(2,1)} %collective-permute-done.14.b_ref, bf16[512,1024]{1,0:T(8,128)(2,1)} %refs_0_.3, bf16[512,1024]{1,0:T(8,128)(2,1)} %copy-done.6, ...), custom_call_target="tpu_custom_call" | custom-call | tf_op jit(solution)/shard_map/quad_weight/pallas_call | solution.py:456
  92.7 0.8 collective-permute-start.15
  93.6 4.6 %all-to-all-start.3 = ((bf16[8,128,128]{2,1,0:T(8,128)(2,1)}), bf16[8,128,128]{2,1,0:T(8,128)(2,1)S(1)}, u32[]{:S(2)}, u32[]{:S(2)}) async-start(bf16[8,128,128]{2,1,0:T(8,128)(2,1)} %bitcast.9), calls=%async_computation.3 | async-start | bytes 524288 | tf_op jit(solution)/shard_map/all_to_all | solution.py:667
  98.2 1.2 add_convert_fusion.after_ref
  99.4 3.0 %collective-permute-start.16 = (bf16[128,2048]{1,0:T(8,128)(2,1)S(1)}, bf16[128,2048]{1,0:T(8,128)(2,1)S(1)}, u32[]{:S(2)}, u32[]{:S(2)}) collective-permute-start(bf16[128,2048]{1,0:T(8,128)(2,1)S(1)} %add_convert_fusion.after_ref), channel_id=1, source_target_pairs={{0,16},{2,18},{4,20},{6,22},{8,24},{10,26},{12,28},{14,30},{16,0},... | collective-permute-start | bytes 1572872 | tf_op jit(solution)/shard_map/ppermute | solution.py:661
  102.4 8.2 %query_grad.1.after_ref = bf16[512,2048]{1,0:T(8,128)(2,1)} custom-call(s32[1]{0:T(128)} %bitcast.me_ref, bf16[128,2048]{1,0:T(8,128)(2,1)} %copy-done.4, bf16[512,2048]{1,0:T(8,128)(2,1)} %get-tuple-element.30.after_ref.g_ref, bf16[512,2048]{1,0:T(8,128)(2,1)} %v_ref.5, bf16[512,2048]{1,0:T(8,128)(2,1)} %k_ref.5, bf16[1024,128]{1,0:T(8,128)(2,1)} %bitcast.14, ...), custom_call_target="tpu_custom_call" | custom-call | tf_op jit(solution)/shard_map/query_grad/pallas_call | solution.py:493
  110.6 10.3 %key_value_inner.1 = (bf16[512,2048]{1,0:T(8,128)(2,1)}, bf16[512,2048]{1,0:T(8,128)(2,1)}) custom-call(bf16[512,2048]{1,0:T(8,128)(2,1)} %query_grad.1.after_ref, bf16[512,2048]{1,0:T(8,128)(2,1)} %q_ref.3, bf16[512,2048]{1,0:T(8,128)(2,1)} %k_ref.5, bf16[512,2048]{1,0:T(8,128)(2,1)} %v_ref.5, bf16[512,2048]{1,0:T(8,128)(2,1)} %get-tuple-element.30.after_ref.g_ref), custom_call_target="tpu_custom_call" | custom-call | tf_op jit(solution)/shard_map/key_value_inner/pallas_call | solution.py:609
  121.0 0.7 copy-done.1
  121.7 0.3 copy-done.11
  122.0 1.0 add_convert_fusion.1
  123.1 0.1 collective-permute-start.13
  123.1 1.5 %collective-permute-done.13.t_ref = bf16[1024,128]{1,0:T(8,128)(2,1)S(1)} collective-permute-done((bf16[1024,128]{1,0:T(8,128)(2,1)S(1)}, bf16[1024,128]{1,0:T(8,128)(2,1)S(1)}, u32[]{:S(2)}, u32[]{:S(2)}) %collective-permute-start.13) | collective-permute-done | bytes 262176 | tf_op jit(solution)/shard_map/ppermute | solution.py:661
  124.7 0.7 copy-done.15
  125.4 6.5 %key_value_outer.1 = (bf16[512,2048]{1,0:T(8,128)(2,1)}, bf16[512,2048]{1,0:T(8,128)(2,1)}) custom-call(s32[1]{0:T(128)} %bitcast.me_ref, bf16[512,2048]{1,0:T(8,128)(2,1)} %k_ref.5, bf16[512,2048]{1,0:T(8,128)(2,1)} %v_ref.5, bf16[512,2048]{1,0:T(8,128)(2,1)} %get-tuple-element.39.refs_1_.ki_ref, bf16[512,2048]{1,0:T(8,128)(2,1)} %get-tuple-element.40.vi_ref, ...), custom_call_target="tpu_custom_call" | custom-call | tf_op jit(solution)/shard_map/key_value_outer/pallas_call | solution.py:637
  132.0 1.2 convert_add_fusion
  (49 shorter events, 0.1 us)
Async XLA Ops:
  0.6 17.4 %copy-start = (f32[16,128,128]{2,1,0:T(8,128)S(1)}, f32[16,128,128]{2,1,0:T(8,128)}, u32[]{:S(2)}) copy-start(f32[16,128,128]{2,1,0:T(8,128)} %param.11) | copy-start | bytes 3145732
  0.6 29.2 %collective-permute-start.2 = (bf16[512,1024]{1,0:T(8,128)(2,1)}, bf16[512,1024]{1,0:T(8,128)(2,1)}, u32[]{:S(2)}, u32[]{:S(2)}) collective-permute-start(bf16[512,1024]{1,0:T(8,128)(2,1)} %refs_0_.3), channel_id=1, source_target_pairs={{0,4},{2,6},{4,0},{6,2},{8,12},{10,14},{12,8},{14,10},{16,20},{18,... | collective-permute-start | bytes 3145736 | tf_op jit(solution)/shard_map/ppermute | solution.py:661
  3.7 26.2 %collective-permute-start = (bf16[512,1024]{1,0:T(8,128)(2,1)}, bf16[512,1024]{1,0:T(8,128)(2,1)S(1)}, u32[]{:S(2)}, u32[]{:S(2)}) collective-permute-start(bf16[512,1024]{1,0:T(8,128)(2,1)} %refs_0_.3), channel_id=1, source_target_pairs={{0,1},{1,0},{2,3},{3,2},{4,5},{5,4},{6,7},{7,6},{8,9},{9,8},{10,11... | collective-permute-start | bytes 3145736 | tf_op jit(solution)/shard_map/ppermute | solution.py:664
  9.6 1.7 %collective-permute-start.1 = (bf16[1024,128]{1,0:T(8,128)(2,1)}, bf16[1024,128]{1,0:T(8,128)(2,1)S(1)}, u32[]{:S(2)}, u32[]{:S(2)}) collective-permute-start(bf16[1024,128]{1,0:T(8,128)(2,1)} %get-tuple-element.26), channel_id=1, source_target_pairs={{0,2},{2,0},{4,6},{6,4},{8,10},{10,8},{12,14},{14,12},{16,18},{18,... | collective-permute-start | bytes 786440 | tf_op jit(solution)/shard_map/ppermute | solution.py:661
  11.3 16.7 %copy-start.2 = (bf16[1024,128]{1,0:T(8,128)(2,1)}, bf16[1024,128]{1,0:T(8,128)(2,1)S(1)}, u32[]{:S(2)}) copy-start(bf16[1024,128]{1,0:T(8,128)(2,1)S(1)} %collective-permute-done.1.oth_ref.kv_ref) | copy-start | bytes 786436
  13.2 16.7 %all-to-all-start = ((bf16[8,128,128]{2,1,0:T(8,128)(2,1)}), bf16[8,128,128]{2,1,0:T(8,128)(2,1)S(1)}, u32[]{:S(2)}, u32[]{:S(2)}) async-start(bf16[8,128,128]{2,1,0:T(8,128)(2,1)} %bitcast.2), calls=%async_computation | async-start | bytes 524288 | tf_op jit(solution)/shard_map/all_to_all | solution.py:667
  29.9 0.7 copy-start.16
  29.9 1.0 copy-start.6
  32.6 17.3 %collective-permute-start.3 = (bf16[2048,512]{1,0:T(8,128)(2,1)}, bf16[2048,512]{1,0:T(8,128)(2,1)}, u32[]{:S(2)}, u32[]{:S(2)}) collective-permute-start(bf16[2048,512]{1,0:T(8,128)(2,1)} %get-tuple-element.31), channel_id=1, source_target_pairs={{0,2},{2,0},{4,6},{6,4},{8,10},{10,8},{12,14},{14,12},{16,18},{18,... | collective-permute-start | bytes 6291464 | tf_op jit(solution)/shard_map/ppermute | solution.py:661
  32.6 34.6 %collective-permute-start.9 = (bf16[512,1024]{1,0:T(8,128)(2,1)}, bf16[512,1024]{1,0:T(8,128)(2,1)}, u32[]{:S(2)}, u32[]{:S(2)}) collective-permute-start(bf16[512,1024]{1,0:T(8,128)(2,1)} %collective-permute-done.2.refs_3_.refs_1_.refs_4_), channel_id=1, source_target_pairs={{0,1},{1,0},{2,3},{3,2},{4,5},{5,4},{6,7},{7,6},{8,9},{9,8},{10,11... | collective-permute-start | bytes 3145736 | tf_op jit(solution)/shard_map/ppermute | solution.py:664
  34.3 15.6 %all-to-all-start.1 = ((bf16[8,128,128]{2,1,0:T(8,128)(2,1)}), bf16[8,128,128]{2,1,0:T(8,128)(2,1)S(1)}, u32[]{:S(2)}, u32[]{:S(2)}) async-start(bf16[8,128,128]{2,1,0:T(8,128)(2,1)} %bitcast.17), calls=%async_computation.1 | async-start | bytes 524288 | tf_op jit(solution)/shard_map/all_to_all | solution.py:667
  49.9 0.7 copy-start.3
  50.6 7.7 %copy-start.17 = (bf16[1024,128]{1,0:T(8,128)(2,1)S(1)}, bf16[1024,128]{1,0:T(8,128)(2,1)}, u32[]{:S(2)}) copy-start(bf16[1024,128]{1,0:T(8,128)(2,1)} %get-tuple-element.35) | copy-start | bytes 786436
  50.6 8.2 %copy-start.5 = (bf16[512,1024]{1,0:T(8,128)(2,1)S(1)}, bf16[512,1024]{1,0:T(8,128)(2,1)}, u32[]{:S(2)}) copy-start(bf16[512,1024]{1,0:T(8,128)(2,1)} %refs_0_.3) | copy-start | bytes 3145732
  50.6 16.6 %copy-start.7 = (bf16[512,1024]{1,0:T(8,128)(2,1)S(1)}, bf16[512,1024]{1,0:T(8,128)(2,1)}, u32[]{:S(2)}) copy-start(bf16[512,1024]{1,0:T(8,128)(2,1)} %copy-done.6) | copy-start | bytes 3145732
  56.2 14.5 %collective-permute-start.4 = (bf16[2,2,128,512]{3,2,1,0:T(8,128)(2,1)}, bf16[2,2,128,512]{3,2,1,0:T(8,128)(2,1)}, u32[]{:S(2)}, u32[]{:S(2)}) collective-permute-start(bf16[2,2,128,512]{3,2,1,0:T(8,128)(2,1)} %get-tuple-element.33.after_ref), channel_id=1, source_target_pairs={{0,4},{2,6},{4,0},{6,2},{8,12},{10,14},{12,8},{14,10},{16,20},{18,... | collective-permute-start | bytes 1572872 | tf_op jit(solution)/shard_map/ppermute | solution.py:661
  58.3 1.9 %collective-permute-start.5 = (bf16[1024,128]{1,0:T(8,128)(2,1)S(1)}, bf16[1024,128]{1,0:T(8,128)(2,1)S(1)}, u32[]{:S(2)}, u32[]{:S(2)}) collective-permute-start(bf16[1024,128]{1,0:T(8,128)(2,1)S(1)} %copy-done.17), channel_id=1, source_target_pairs={{0,2},{2,0},{4,6},{6,4},{8,10},{10,8},{12,14},{14,12},{16,18},{18,... | collective-permute-start | bytes 786440 | tf_op jit(solution)/shard_map/ppermute | solution.py:661
  58.3 9.0 %collective-permute-start.6 = (bf16[1024,128]{1,0:T(8,128)(2,1)}, bf16[1024,128]{1,0:T(8,128)(2,1)S(1)}, u32[]{:S(2)}, u32[]{:S(2)}) collective-permute-start(bf16[1024,128]{1,0:T(8,128)(2,1)} %get-tuple-element.36), channel_id=1, source_target_pairs={{0,2},{2,0},{4,6},{6,4},{8,10},{10,8},{12,14},{14,12},{16,18},{18,... | collective-permute-start | bytes 786440 | tf_op jit(solution)/shard_map/ppermute | solution.py:661
  58.8 14.5 %collective-permute-start.7 = (bf16[512,1024]{1,0:T(8,128)(2,1)S(1)}, bf16[512,1024]{1,0:T(8,128)(2,1)}, u32[]{:S(2)}, u32[]{:S(2)}) collective-permute-start(bf16[512,1024]{1,0:T(8,128)(2,1)S(1)} %copy-done.5), channel_id=1, source_target_pairs={{0,2},{2,0},{4,6},{6,4},{8,10},{10,8},{12,14},{14,12},{16,18},{18,... | collective-permute-start | bytes 3145736 | tf_op jit(solution)/shard_map/ppermute | solution.py:661
  60.2 0.7 copy-start.10
  60.2 13.1 %collective-permute-start.10 = (bf16[512,1024]{1,0:T(8,128)(2,1)}, bf16[512,1024]{1,0:T(8,128)(2,1)}, u32[]{:S(2)}, u32[]{:S(2)}) collective-permute-start(bf16[512,1024]{1,0:T(8,128)(2,1)} %collective-permute-done.2.refs_3_.refs_1_.refs_4_), channel_id=1, source_target_pairs={{0,2},{2,0},{4,6},{6,4},{8,10},{10,8},{12,14},{14,12},{16,18},{18,... | collective-permute-start | bytes 3145736 | tf_op jit(solution)/shard_map/ppermute | solution.py:661
  62.7 21.2 %all-to-all-start.2 = ((bf16[8,128,128]{2,1,0:T(8,128)(2,1)}), bf16[8,128,128]{2,1,0:T(8,128)(2,1)}, u32[]{:S(2)}, u32[]{:S(2)}) async-start(bf16[8,128,128]{2,1,0:T(8,128)(2,1)} %bitcast.15), calls=%async_computation.2 | async-start | bytes 524288 | tf_op jit(solution)/shard_map/all_to_all | solution.py:667
  67.2 6.1 %collective-permute-start.8 = (bf16[512,1024]{1,0:T(8,128)(2,1)S(1)}, bf16[512,1024]{1,0:T(8,128)(2,1)S(1)}, u32[]{:S(2)}, u32[]{:S(2)}) collective-permute-start(bf16[512,1024]{1,0:T(8,128)(2,1)S(1)} %copy-done.7), channel_id=1, source_target_pairs={{0,2},{2,0},{4,6},{6,4},{8,10},{10,8},{12,14},{14,12},{16,18},{18,... | collective-permute-start | bytes 3145736 | tf_op jit(solution)/shard_map/ppermute | solution.py:661
  67.3 5.9 %copy-start.14 = (bf16[1024,128]{1,0:T(8,128)(2,1)}, bf16[1024,128]{1,0:T(8,128)(2,1)S(1)}, u32[]{:S(2)}) copy-start(bf16[1024,128]{1,0:T(8,128)(2,1)S(1)} %collective-permute-done.6.refs_2_.t_ref) | copy-start | bytes 786436
  67.3 6.0 %collective-permute-start.11 = (bf16[512,1024]{1,0:T(8,128)(2,1)}, bf16[512,1024]{1,0:T(8,128)(2,1)S(1)}, u32[]{:S(2)}, u32[]{:S(2)}) collective-permute-start(bf16[512,1024]{1,0:T(8,128)(2,1)} %collective-permute-done.9.refs_5_), channel_id=1, source_target_pairs={{0,2},{2,0},{4,6},{6,4},{8,10},{10,8},{12,14},{14,12},{16,18},{18,... | collective-permute-start | bytes 3145736 | tf_op jit(solution)/shard_map/ppermute | solution.py:661
  70.7 14.9 %collective-permute-start.14 = (bf16[2,2,128,512]{3,2,1,0:T(8,128)(2,1)}, bf16[2,2,128,512]{3,2,1,0:T(8,128)(2,1)}, u32[]{:S(2)}, u32[]{:S(2)}) collective-permute-start(bf16[2,2,128,512]{3,2,1,0:T(8,128)(2,1)} %get-tuple-element.43), channel_id=1, source_target_pairs={{0,4},{2,6},{4,0},{6,2},{8,12},{10,14},{12,8},{14,10},{16,20},{18,... | collective-permute-start | bytes 1572872 | tf_op jit(solution)/shard_map/ppermute | solution.py:661
  73.3 1.0 copy-start.8
  73.3 1.3 copy-start.9
  81.7 16.5 %collective-permute-start.12 = (bf16[128,2048]{1,0:T(8,128)(2,1)}, bf16[128,2048]{1,0:T(8,128)(2,1)}, u32[]{:S(2)}, u32[]{:S(2)}) collective-permute-start(bf16[128,2048]{1,0:T(8,128)(2,1)} %get-tuple-element.38), channel_id=1, source_target_pairs={{0,8},{2,10},{4,12},{6,14},{8,0},{10,2},{12,4},{14,6},{16,24},{18,... | collective-permute-start | bytes 1572872 | tf_op jit(solution)/shard_map/ppermute | solution.py:661
  85.6 12.7 %copy-start.13 = (bf16[128,2048]{1,0:T(8,128)(2,1)S(1)}, bf16[128,2048]{1,0:T(8,128)(2,1)}, u32[]{:S(2)}) copy-start(bf16[128,2048]{1,0:T(8,128)(2,1)} %get-tuple-element.37.refs_0_) | copy-start | bytes 1572868
  92.7 39.2 %collective-permute-start.15 = (bf16[128,2048]{1,0:T(8,128)(2,1)}, bf16[128,2048]{1,0:T(8,128)(2,1)S(1)}, u32[]{:S(2)}, u32[]{:S(2)}) collective-permute-start(bf16[128,2048]{1,0:T(8,128)(2,1)} %get-tuple-element.45), channel_id=1, source_target_pairs={{0,8},{2,10},{4,12},{6,14},{8,0},{10,2},{12,4},{14,6},{16,24},{18,... | collective-permute-start | bytes 1572872 | tf_op jit(solution)/shard_map/ppermute | solution.py:661
  93.6 27.4 %all-to-all-start.3 = ((bf16[8,128,128]{2,1,0:T(8,128)(2,1)}), bf16[8,128,128]{2,1,0:T(8,128)(2,1)S(1)}, u32[]{:S(2)}, u32[]{:S(2)}) async-start(bf16[8,128,128]{2,1,0:T(8,128)(2,1)} %bitcast.9), calls=%async_computation.3 | async-start | bytes 524288 | tf_op jit(solution)/shard_map/all_to_all | solution.py:667
  99.4 3.0 %copy-start.4 = (bf16[128,2048]{1,0:T(8,128)(2,1)}, bf16[128,2048]{1,0:T(8,128)(2,1)S(1)}, u32[]{:S(2)}) copy-start(bf16[128,2048]{1,0:T(8,128)(2,1)S(1)} %add_convert_fusion.after_ref) | copy-start | bytes 1572868
  99.4 32.5 %collective-permute-start.16 = (bf16[128,2048]{1,0:T(8,128)(2,1)S(1)}, bf16[128,2048]{1,0:T(8,128)(2,1)S(1)}, u32[]{:S(2)}, u32[]{:S(2)}) collective-permute-start(bf16[128,2048]{1,0:T(8,128)(2,1)S(1)} %add_convert_fusion.after_ref), channel_id=1, source_target_pairs={{0,16},{2,18},{4,20},{6,22},{8,24},{10,26},{12,28},{14,30},{16,0},... | collective-permute-start | bytes 1572872 | tf_op jit(solution)/shard_map/ppermute | solution.py:661
  121.0 1.0 copy-start.11
  121.0 0.7 copy-start.1
  123.1 1.6 %collective-permute-start.13 = (bf16[1024,128]{1,0:T(8,128)(2,1)S(1)}, bf16[1024,128]{1,0:T(8,128)(2,1)S(1)}, u32[]{:S(2)}, u32[]{:S(2)}) collective-permute-start(bf16[1024,128]{1,0:T(8,128)(2,1)S(1)} %add_convert_fusion.1), channel_id=1, source_target_pairs={{0,2},{2,0},{4,6},{6,4},{8,10},{10,8},{12,14},{14,12},{16,18},{18,... | collective-permute-start | bytes 786440 | tf_op jit(solution)/shard_map/ppermute | solution.py:661
  124.7 0.7 copy-start.15
  125.4 6.6 %copy-start.12 = (bf16[128,2048]{1,0:T(8,128)(2,1)S(1)}, bf16[128,2048]{1,0:T(8,128)(2,1)}, u32[]{:S(2)}) copy-start(bf16[128,2048]{1,0:T(8,128)(2,1)} %get-tuple-element.44) | copy-start | bytes 1572868

commit v5 on v4

--- a/solution.py
+++ b/solution.py
@@ -428,14 +428,18 @@
 
 def quad_weight_kernel(waits, tp_ref, a_ref, b_ref, *refs):
     half, _, head, tok = a_ref.shape
-    ins, outs = refs[:8], refs[8 + waits :]
+    ins, outs, a_all, c_all = refs[:8], refs[8 + waits : -2], refs[-2], refs[-1]
+
+    @pl.when(pl.program_id(0) == 0)
+    def _():
+        for k in range(4):
+            block = (a_ref if k < 2 else b_ref)[:, k % 2]
+            a_all[:, k * tok : (k + 1) * tok] = block.reshape(half * head, tok)
 
     def product(part):
-        total = None
         for k in range(4):
-            block = (a_ref if k < 2 else b_ref)[:, k % 2].reshape(half * head, tok)
-            term = dot(block, ins[2 * k + part][...], 1, 0)
-            total = term if total is None else total + term
+            c_all[k * tok : (k + 1) * tok, :] = ins[2 * k + part][...]
+        total = dot(a_all[...], c_all[...], 1, 0)
         for i, o_ref in enumerate(outs):
             o_ref[...] = total[i * head : (i + 1) * head].astype(BF)
 
@@ -463,6 +467,10 @@
                 pl.BlockSpec((head, step), lambda i, t: (0, (i + t[0] * steps) % (2 * steps)))
             ]
             * half,
+            scratch_shapes=[
+                pltpu.VMEM((half * head, 4 * tok), BF),
+                pltpu.VMEM((4 * tok, step), BF),
+            ],
         ),
         out_shape=[jax.ShapeDtypeStruct((head, 2 * feat), BF)] * half,
         compiler_params=params(),
@@ -471,7 +479,7 @@
     )(tp, a, b, *cots, *after)
 
 
-def pair_query_kernel(head, me_ref, after_ref, g_ref, v_ref, k_ref, s_ref, kv_ref, t_ref, o_ref):
+def pair_query_kernel(head, me_ref, after_ref, so_far_ref, g_ref, v_ref, k_ref, s_ref, kv_ref, t_ref, o_ref):
     core = me_ref[0] % 2
     half = g_ref.shape[0] // 2
     for j in range(g_ref.shape[1] // head):
@@ -485,24 +493,26 @@
         o_ref[half:, at] = (second_half + over[half:]).astype(BF)
 
 
-def pair_query_grad(me, after, g, v, k, state, kv, other, head):
+def pair_query_grad(me, part, after, so_far, g, v, k, state, kv, other, head):
     tok, width = g.shape
-    step = min(4 * head, width)
-    spec = pl.BlockSpec((tok, step), lambda i, m: (0, i))
-    rows = pl.BlockSpec((step // 2, head), lambda i, m: (i, 0))
+    step = min(4 * head, width // 2)
+    steps = width // 2 // step
+    spec = pl.BlockSpec((tok, step), lambda i, m: (0, i + part * steps))
+    rows = pl.BlockSpec((step // 2, head), lambda i, m: (i + part * steps, 0))
     return pl.pallas_call(
         functools.partial(pair_query_kernel, head),
         grid_spec=pltpu.PrefetchScalarGridSpec(
             num_scalar_prefetch=1,
-            grid=(width // step,),
-            in_specs=[ANY, spec, spec, spec, rows, rows, rows],
+            grid=(steps,),
+            in_specs=[ANY, ANY, spec, spec, spec, rows, rows, rows],
             out_specs=spec,
         ),
         out_shape=jax.ShapeDtypeStruct((tok, width), BF),
+        input_output_aliases={2: 0} if part else {},
         compiler_params=params(),
         cost_estimate=cost(0, 0),
         name="query_grad",
-    )(me, after, g, v, k, state, kv, other)
+    )(me, after, so_far, g, v, k, state, kv, other)
 
 
 def pair_grad_kernel(head, waits, me_ref, tp_ref, own_ref, far_ref, w_ref, q_ref, *refs):
@@ -694,7 +704,9 @@
     cots = [cotangent, far, swap(cotangent, 1), swap(far, 1)]
     cots += [south, far_south, swap(south, 1), swap(far_south, 1)]
 
-    received = passed_after(received, (chip, state_other), 2e10)
+    query_args = (grad, values, keys, state, kv_other, state_other, head)
+    query_g = pair_query_grad(who, 0, chip, grad, *query_args)
+    received = passed_after(received, (query_g,), 2e10)
     crossing = quad_weight(which, (), mine, received, cots, 1)
     summed = added(crossing[0], 1.0, swap(crossing[1], 4))
     crossed = swap(summed, 8)
@@ -702,7 +714,7 @@
     after_chip = across(scanned)
     same = quad_weight(which, (scanned,), mine, received_near, cots, 0)
     neighbour = swap(same[1], 4)
-    query_g = pair_query_grad(who, summed, grad, values, keys, state, kv_other, state_other, head)
+    query_g = pair_query_grad(who, 1, summed, query_g, *query_args)
     inners = key_value_inner(query_g, queries, keys, values, grad, head)
     after_chip = passed_after(after_chip, (inners[0],), 0)
     adjoint_other = swap(added(after_chip, core, qd_mine), 1)

time: 134 us -> 134 us (level)
  waiting for transfers between devices: 9.36 us -> 6.46 us
  local copies, waits for them, and re-layouts: 6.02 us -> 8.76 us
  Pallas kernels: 73.7 us -> 76 us
    ppermute x15, waiting for transfers between devices: 7.52 us -> 4.65 us  [swap(): return lax.ppermute(x, 'ctx', [(c, c ^ bit) for c in range(n)])]
    unnamed x36 -> x42, local copies, waits for them, and re-layouts: 5.4 us -> 8.12 us
    pallas_call x1 -> x2, Pallas kernels: 8.23 us -> 10.3 us  [pair_query_grad(): pl.pallas_call(functools.partial(pair_query_kernel, head), grid_spec=pltp...]
  transfers between devices with their start and end apart: 21 -> 21, of which waited for: 5 -> 4; matrix products, arithmetic and copies ran while one was open for 3% -> 3% of each run, Pallas kernels for 54% -> 56%
where the time goes in v5:
time: 134 us; the launch traced here: 133 us
  Pallas kernels  76 us (57%)
  starting transfers between devices  36.7 us (27%)
  local copies, waits for them, and re-layouts  8.76 us (7%)
  waiting for transfers between devices  6.46 us (5%)
  other arithmetic  4.17 us (3%)
    all_to_all x4, starting transfers between devices, across(): return lax.all_to_all(x, 'ctx', 0, 0, axis_index_groups=groups, tiled=True)  19.1 us
    pallas_call x2, Pallas kernels, quad_weight(): pl.pallas_call(functools.partial(quad_weight_kernel, len(after)), grid_sp...  14.5 us
    ppermute x15, starting transfers between devices, swap(): return lax.ppermute(x, 'ctx', [(c, c ^ bit) for c in range(n)])  14.4 us
    pallas_call x1, Pallas kernels, key_value_inner(): pl.pallas_call(functools.partial(key_value_inner_kernel, head), grid=(wid...  10.4 us
    pallas_call x2, Pallas kernels, pair_query_grad(): pl.pallas_call(functools.partial(pair_query_kernel, head), grid_spec=pltp...  10.3 us
    pallas_call x1, Pallas kernels, pair_grad(): pl.pallas_call(functools.partial(pair_grad_kernel, head, len(after)), gri...  9.73 us
    pallas_call x1, Pallas kernels, pair_intra(): pl.pallas_call(functools.partial(pair_intra_kernel, head, len(after)), gr...  9.36 us
    unnamed x42, local copies, waits for them, and re-layouts  8.12 us
  transfers between devices with their start and end apart: 21, of which 4 were waited for; matrix products, arithmetic and copies ran while one was open for 3% of the time, Pallas kernels for 56%

profile of v5, /device:TPU:0, one launch (start us, length us, event | category | flops | bytes accessed | tf_op | source)
XLA Modules:
  0.0 132.9 jit_solution(12678601840691725617)
XLA Ops:
  0.6 3.0 %collective-permute-start.2 = (bf16[512,1024]{1,0:T(8,128)(2,1)}, bf16[512,1024]{1,0:T(8,128)(2,1)}, u32[]{:S(2)}, u32[]{:S(2)}) collective-permute-start(bf16[512,1024]{1,0:T(8,128)(2,1)} %refs_0_.3), channel_id=1, source_target_pairs={{0,4},{2,6},{4,0},{6,2},{8,12},{10,14},{12,8},{14,10},{16,20},{18,... | collective-permute-start | bytes 3145736 | tf_op jit(solution)/shard_map/ppermute | solution.py:671
  3.7 1.5 %collective-permute-start = (bf16[512,1024]{1,0:T(8,128)(2,1)}, bf16[512,1024]{1,0:T(8,128)(2,1)S(1)}, u32[]{:S(2)}, u32[]{:S(2)}) collective-permute-start(bf16[512,1024]{1,0:T(8,128)(2,1)} %refs_0_.3), channel_id=1, source_target_pairs={{0,1},{1,0},{2,3},{3,2},{4,5},{5,4},{6,7},{7,6},{8,9},{9,8},{10,11... | collective-permute-start | bytes 3145736 | tf_op jit(solution)/shard_map/ppermute | solution.py:674
  5.2 4.4 %pair_sums.1 = (bf16[1024,128]{1,0:T(8,128)(2,1)}, bf16[1024,128]{1,0:T(8,128)(2,1)}) custom-call(s32[1]{0:T(128)} %bitcast.me_ref, bf16[512,2048]{1,0:T(8,128)(2,1)} %k_ref.7, bf16[512,2048]{1,0:T(8,128)(2,1)} %v_ref.7), custom_call_target="tpu_custom_call" | custom-call | flops 268435456 | bytes 4194304 | tf_op jit(solution)/shard_map/pair_sums/pallas_call | solution.py:305
  9.6 1.7 %collective-permute-done.1.oth_ref.kv_ref = bf16[1024,128]{1,0:T(8,128)(2,1)S(1)} collective-permute-done((bf16[1024,128]{1,0:T(8,128)(2,1)}, bf16[1024,128]{1,0:T(8,128)(2,1)S(1)}, u32[]{:S(2)}, u32[]{:S(2)}) %collective-permute-start.1) | collective-permute-done | bytes 262176 | tf_op jit(solution)/shard_map/ppermute | solution.py:671
  11.4 1.8 %add_convert_fusion.2.refs_0_ = bf16[1024,128]{1,0:T(8,128)(2,1)} fusion(bf16[1024,128]{1,0:T(8,128)(2,1)S(1)} %collective-permute-done.1.oth_ref.kv_ref, bf16[1024,128]{1,0:T(8,128)(2,1)} %get-tuple-element.25.own_ref), kind=kLoop, calls=%fused_computation.3 | loop fusion | flops 524288 | bytes 786432 | tf_op jit(solution)/shard_map/convert_element_type | solution.py:680
  13.2 4.9 %all-to-all-start = ((bf16[8,128,128]{2,1,0:T(8,128)(2,1)}), bf16[8,128,128]{2,1,0:T(8,128)(2,1)S(1)}, u32[]{:S(2)}, u32[]{:S(2)}) async-start(bf16[8,128,128]{2,1,0:T(8,128)(2,1)} %bitcast.2), calls=%async_computation | async-start | bytes 524288 | tf_op jit(solution)/shard_map/all_to_all | solution.py:677
  18.1 0.6 dynamic-slice_bitcast_fusion.refs_0_
  18.7 9.4 %pair_intra.1 = (bf16[1024,512]{1,0:T(8,128)(2,1)}, bf16[2048,512]{1,0:T(8,128)(2,1)}) custom-call(s32[1]{0:T(128)} %bitcast.me_ref, bf16[1024,128]{1,0:T(8,128)(2,1)} %add_convert_fusion.2.refs_0_, bf16[512,2048]{1,0:T(8,128)(2,1)} %q_ref.3, bf16[512,2048]{1,0:T(8,128)(2,1)} %k_ref.7, bf16[512,2048]{1,0:T(8,128)(2,1)} %v_ref.7), custom_call_target="tpu_custom_call" | custom-call | flops 2147483648 | bytes 9437184 | tf_op jit(solution)/shard_map/pair_intra/pallas_call | solution.py:337
  28.1 1.8 %all-to-all-done = bf16[8,128,128]{2,1,0:T(8,128)(2,1)S(1)} async-done(((bf16[8,128,128]{2,1,0:T(8,128)(2,1)}), bf16[8,128,128]{2,1,0:T(8,128)(2,1)S(1)}, u32[]{:S(2)}, u32[]{:S(2)}) %all-to-all-start) | async-done | bytes 262176 | tf_op jit(solution)/shard_map/all_to_all | solution.py:677
  29.9 0.7 copy-done.18
  30.6 0.4 copy-done.6
  30.9 1.7 %scan_blocks.2 = (bf16[1024,128]{1,0:T(8,128)(2,1)}, bf16[2048,512]{1,0:T(8,128)(2,1)}) custom-call(bf16[1024,128]{1,0:T(8,128)(2,1)} %bitcast.19, f32[128,128]{1,0:T(8,128)} %dynamic-slice_bitcast_fusion.refs_0_, bf16[1024,512]{1,0:T(8,128)(2,1)} %get-tuple-element.27.refs_1_.i_ref, bf16[512,1024]{1,0:T(8,128)(2,1)} %copy-done.6, ...), custom_call_target="tpu_custom_call", output_to_operand_aliasing={{1}: (5, {})} | custom-call | flops 20000000000 | tf_op jit(solution)/shard_map/scan_blocks/pallas_call | solution.py:269
  32.6 1.7 %collective-permute-start.9 = (bf16[512,1024]{1,0:T(8,128)(2,1)}, bf16[512,1024]{1,0:T(8,128)(2,1)}, u32[]{:S(2)}, u32[]{:S(2)}) collective-permute-start(bf16[512,1024]{1,0:T(8,128)(2,1)} %collective-permute-done.2.refs_3_.refs_1_.refs_4_), channel_id=1, source_target_pairs={{0,1},{1,0},{2,3},{3,2},{4,5},{5,4},{6,7},{7,6},{8,9},{9,8},{10,11... | collective-permute-start | bytes 3145736 | tf_op jit(solution)/shard_map/ppermute | solution.py:674
  34.3 5.8 %all-to-all-start.1 = ((bf16[8,128,128]{2,1,0:T(8,128)(2,1)}), bf16[8,128,128]{2,1,0:T(8,128)(2,1)S(1)}, u32[]{:S(2)}, u32[]{:S(2)}) async-start(bf16[8,128,128]{2,1,0:T(8,128)(2,1)} %bitcast.20), calls=%async_computation.1 | async-start | bytes 524288 | tf_op jit(solution)/shard_map/all_to_all | solution.py:677
  40.2 9.7 %out_grad.1 = (bf16[512,2048]{1,0:T(8,128)(2,1)}, bf16[1024,128]{1,0:T(8,128)(2,1)}, bf16[1024,128]{1,0:T(8,128)(2,1)}) custom-call(s32[1]{0:T(128)} %bitcast.me_ref, s32[1]{0:T(128)} %bitcast.1.tp_ref, bf16[512,1024]{1,0:T(8,128)(2,1)} %refs_0_.3, bf16[512,1024]{1,0:T(8,128)(2,1)} %copy-done.6, bf16[2048,2048]{1,0:T(8,128)(2,1)} %w_ref.1, ...), custom_call_target="tpu_custom_call" | custom-call | flops 4294967296 | bytes 12582912 | tf_op jit(solution)/shard_map/out_grad/pallas_call | solution.py:545
  49.9 0.7 copy-done.2
  50.6 0.7 copy-done.4
  51.3 5.5 %pair_attended.1 = (bf16[4,2,128,512]{3,2,1,0:T(8,128)(2,1)}, bf16[2,2,128,512]{3,2,1,0:T(8,128)(2,1)}, bf16[2,2,128,512]{3,2,1,0:T(8,128)(2,1)}, bf16[1024,128]{1,0:T(8,128)(2,1)}) custom-call(s32[1]{0:T(128)} %bitcast.me_ref, bf16[512,2048]{1,0:T(8,128)(2,1)} %get-tuple-element.30.after_ref.so_far_ref.g_ref, bf16[512,2048]{1,0:T(8,128)(2,1)} %q_ref.3, ...), custom_call_target="tpu_custom_call" | custom-call | flops 268435456 | bytes 10485760 | tf_op jit(solution)/shard_map/pair_attended/pallas_call | solution.py:397
  56.8 2.1 %collective-permute-start.4 = (bf16[2,2,128,512]{3,2,1,0:T(8,128)(2,1)}, bf16[2,2,128,512]{3,2,1,0:T(8,128)(2,1)S(1)}, u32[]{:S(2)}, u32[]{:S(2)}) collective-permute-start(bf16[2,2,128,512]{3,2,1,0:T(8,128)(2,1)} %get-tuple-element.33.after_ref), channel_id=1, source_target_pairs={{0,4},{2,6},{4,0},{6,2},{8,12},{10,14},{12,8},{14,10},{16,20},{18,... | collective-permute-start | bytes 1572872 | tf_op jit(solution)/shard_map/ppermute | solution.py:671
  58.9 0.5 collective-permute-start.6
  59.4 1.4 %collective-permute-done.5.b_ref.qd_ref = bf16[1024,128]{1,0:T(8,128)(2,1)S(1)} collective-permute-done((bf16[1024,128]{1,0:T(8,128)(2,1)S(1)}, bf16[1024,128]{1,0:T(8,128)(2,1)S(1)}, u32[]{:S(2)}, u32[]{:S(2)}) %collective-permute-start.5) | collective-permute-done | bytes 262176 | tf_op jit(solution)/shard_map/ppermute | solution.py:671
  60.9 0.6 copy-done.10
  61.5 1.8 %add_after.1.after_ref = bf16[1024,128]{1,0:T(8,128)(2,1)} custom-call(bf16[2,2,128,512]{3,2,1,0:T(8,128)(2,1)} %get-tuple-element.33.after_ref, bf16[1024,128]{1,0:T(8,128)(2,1)} %get-tuple-element.34.a_ref, bf16[1024,128]{1,0:T(8,128)(2,1)} %copy-done.10), custom_call_target="tpu_custom_call" | custom-call | tf_op jit(solution)/shard_map/add_after/pallas_call | solution.py:590
  63.3 4.5 %all-to-all-start.2 = ((bf16[8,128,128]{2,1,0:T(8,128)(2,1)}), bf16[8,128,128]{2,1,0:T(8,128)(2,1)S(1)}, u32[]{:S(2)}, u32[]{:S(2)}) async-start(bf16[8,128,128]{2,1,0:T(8,128)(2,1)} %bitcast.16), calls=%async_computation.2 | async-start | bytes 524288 | tf_op jit(solution)/shard_map/all_to_all | solution.py:677
  67.9 0.5 collective-permute-start.11
  68.6 5.1 %query_grad.2.refs_1_.so_far_ref = bf16[512,2048]{1,0:T(8,128)(2,1)} custom-call(s32[1]{0:T(128)} %bitcast.me_ref, bf16[1024,128]{1,0:T(8,128)(2,1)} %add_after.1.after_ref, bf16[512,2048]{1,0:T(8,128)(2,1)} %get-tuple-element.30.after_ref.so_far_ref.g_ref, bf16[512,2048]{1,0:T(8,128)(2,1)} %get-tuple-element.30.after_ref.so_far_ref.g_ref, ...), custom_call_target="tpu_custom_call" | custom-call | tf_op jit(solution)/shard_map/query_grad/pallas_call | solution.py:502
  73.8 2.0 %collective-permute-start.14 = (bf16[2,2,128,512]{3,2,1,0:T(8,128)(2,1)}, bf16[2,2,128,512]{3,2,1,0:T(8,128)(2,1)S(1)}, u32[]{:S(2)}, u32[]{:S(2)}) collective-permute-start(bf16[2,2,128,512]{3,2,1,0:T(8,128)(2,1)} %get-tuple-element.43), channel_id=1, source_target_pairs={{0,4},{2,6},{4,0},{6,2},{8,12},{10,14},{12,8},{14,10},{16,20},{18,... | collective-permute-start | bytes 1572872 | tf_op jit(solution)/shard_map/ppermute | solution.py:671
  75.9 0.9 copy-done.7
  76.8 0.4 copy-done.8
  77.2 0.4 copy-done.9
  77.5 7.2 %quad_weight.2 = (bf16[128,2048]{1,0:T(8,128)(2,1)}, bf16[128,2048]{1,0:T(8,128)(2,1)}) custom-call(s32[1]{0:T(128)} %bitcast.1.tp_ref, bf16[4,2,128,512]{3,2,1,0:T(8,128)(2,1)} %get-tuple-element.32.a_ref, bf16[2,2,128,512]{3,2,1,0:T(8,128)(2,1)} %passed_after.2.b_ref, bf16[512,1024]{1,0:T(8,128)(2,1)} %refs_0_.3, bf16[512,1024]{1,0:T(8,128)(2,1)} %copy-done.6, ...), custom_call_target="tpu_custom_call" | custom-call | flops 20000000000 | tf_op jit(solution)/shard_map/quad_weight/pallas_call | solution.py:460
  84.7 1.5 %collective-permute-start.12 = (bf16[128,2048]{1,0:T(8,128)(2,1)}, bf16[128,2048]{1,0:T(8,128)(2,1)S(1)}, u32[]{:S(2)}, u32[]{:S(2)}) collective-permute-start(bf16[128,2048]{1,0:T(8,128)(2,1)} %get-tuple-element.38), channel_id=1, source_target_pairs={{0,8},{2,10},{4,12},{6,14},{8,0},{10,2},{12,4},{14,6},{16,24},{18,... | collective-permute-start | bytes 1572872 | tf_op jit(solution)/shard_map/ppermute | solution.py:671
  86.2 0.7 copy-done.17
  86.9 1.7 %scan_blocks.3.refs_8_ = bf16[1024,128]{1,0:T(8,128)(2,1)} custom-call(bf16[1024,128]{1,0:T(8,128)(2,1)} %bitcast.18, bf16[128,2048]{1,0:T(8,128)(2,1)} %get-tuple-element.37.refs_0_), custom_call_target="tpu_custom_call" | custom-call | flops 20000000000 | tf_op jit(solution)/shard_map/scan_blocks/pallas_call | solution.py:269
  88.6 3.8 %all-to-all-start.3 = ((bf16[8,128,128]{2,1,0:T(8,128)(2,1)}), bf16[8,128,128]{2,1,0:T(8,128)(2,1)S(1)}, u32[]{:S(2)}, u32[]{:S(2)}) async-start(bf16[8,128,128]{2,1,0:T(8,128)(2,1)} %bitcast.17), calls=%async_computation.3 | async-start | bytes 524288 | tf_op jit(solution)/shard_map/all_to_all | solution.py:677
  92.4 0.8 copy-done.14
  93.2 7.4 %quad_weight.3 = (bf16[128,2048]{1,0:T(8,128)(2,1)}, bf16[128,2048]{1,0:T(8,128)(2,1)}) custom-call(s32[1]{0:T(128)} %bitcast.1.tp_ref, bf16[4,2,128,512]{3,2,1,0:T(8,128)(2,1)} %get-tuple-element.32.a_ref, bf16[2,2,128,512]{3,2,1,0:T(8,128)(2,1)} %copy-done.14, bf16[512,1024]{1,0:T(8,128)(2,1)} %refs_0_.3, bf16[512,1024]{1,0:T(8,128)(2,1)} %copy-done.6, ...), custom_call_target="tpu_custom_call" | custom-call | tf_op jit(solution)/shard_map/quad_weight/pallas_call | solution.py:460
  100.6 2.1 %collective-permute-start.15 = (bf16[128,2048]{1,0:T(8,128)(2,1)}, bf16[128,2048]{1,0:T(8,128)(2,1)S(1)}, u32[]{:S(2)}, u32[]{:S(2)}) collective-permute-start(bf16[128,2048]{1,0:T(8,128)(2,1)} %get-tuple-element.45), channel_id=1, source_target_pairs={{0,8},{2,10},{4,12},{6,14},{8,0},{10,2},{12,4},{14,6},{16,24},{18,... | collective-permute-start | bytes 1572872 | tf_op jit(solution)/shard_map/ppermute | solution.py:671
  102.8 2.4 %collective-permute-start.16 = (bf16[128,2048]{1,0:T(8,128)(2,1)S(1)}, bf16[128,2048]{1,0:T(8,128)(2,1)S(1)}, u32[]{:S(2)}, u32[]{:S(2)}) collective-permute-start(bf16[128,2048]{1,0:T(8,128)(2,1)S(1)} %add_convert_fusion.after_ref), channel_id=1, source_target_pairs={{0,16},{2,18},{4,20},{6,22},{8,24},{10,26},{12,28},{14,30},{16,0},... | collective-permute-start | bytes 1572872 | tf_op jit(solution)/shard_map/ppermute | solution.py:671
  105.2 5.2 %query_grad.3.after_ref = bf16[512,2048]{1,0:T(8,128)(2,1)} custom-call(s32[1]{0:T(128)} %bitcast.me_ref, bf16[128,2048]{1,0:T(8,128)(2,1)} %copy-done.5, bf16[512,2048]{1,0:T(8,128)(2,1)} %query_grad.2.refs_1_.so_far_ref, bf16[512,2048]{1,0:T(8,128)(2,1)} %get-tuple-element.30.after_ref.so_far_ref.g_ref, ...), custom_call_target="tpu_custom_call", output_to_operand_aliasing={{}: (2, {})} | custom-call | tf_op jit(solution)/shard_map/query_grad/pallas_call | solution.py:502
  110.4 10.4 %key_value_inner.1 = (bf16[512,2048]{1,0:T(8,128)(2,1)}, bf16[512,2048]{1,0:T(8,128)(2,1)}) custom-call(bf16[512,2048]{1,0:T(8,128)(2,1)} %query_grad.3.after_ref, bf16[512,2048]{1,0:T(8,128)(2,1)} %q_ref.3, bf16[512,2048]{1,0:T(8,128)(2,1)} %k_ref.7, bf16[512,2048]{1,0:T(8,128)(2,1)} %v_ref.7, bf16[512,2048]{1,0:T(8,128)(2,1)} %get-tuple-element.30.after_ref.so_far_ref.g_ref), custom_call_target="tpu_custom_call" | custom-call | tf_op jit(solution)/shard_map/key_value_inner/pallas_call | solution.py:619
  120.8 0.7 copy-done.3
  121.5 0.3 copy-done.12
  121.8 1.0 add_convert_fusion.1
  122.9 1.5 %collective-permute-done.13.t_ref = bf16[1024,128]{1,0:T(8,128)(2,1)S(1)} collective-permute-done((bf16[1024,128]{1,0:T(8,128)(2,1)S(1)}, bf16[1024,128]{1,0:T(8,128)(2,1)S(1)}, u32[]{:S(2)}, u32[]{:S(2)}) %collective-permute-start.13) | collective-permute-done | bytes 262176 | tf_op jit(solution)/shard_map/ppermute | solution.py:671
  124.5 0.7 copy-done.16
  125.2 6.5 %key_value_outer.1 = (bf16[512,2048]{1,0:T(8,128)(2,1)}, bf16[512,2048]{1,0:T(8,128)(2,1)}) custom-call(s32[1]{0:T(128)} %bitcast.me_ref, bf16[512,2048]{1,0:T(8,128)(2,1)} %k_ref.7, bf16[512,2048]{1,0:T(8,128)(2,1)} %v_ref.7, bf16[512,2048]{1,0:T(8,128)(2,1)} %get-tuple-element.39.refs_1_.ki_ref, bf16[512,2048]{1,0:T(8,128)(2,1)} %get-tuple-element.40.vi_ref, ...), custom_call_target="tpu_custom_call" | custom-call | tf_op jit(solution)/shard_map/key_value_outer/pallas_call | solution.py:647
  131.7 1.2 convert_add_fusion
  (56 shorter events, 0.7 us)
Async XLA Ops:
  0.6 17.4 %copy-start = (f32[16,128,128]{2,1,0:T(8,128)S(1)}, f32[16,128,128]{2,1,0:T(8,128)}, u32[]{:S(2)}) copy-start(f32[16,128,128]{2,1,0:T(8,128)} %param.11) | copy-start | bytes 3145732
  0.6 29.2 %collective-permute-start.2 = (bf16[512,1024]{1,0:T(8,128)(2,1)}, bf16[512,1024]{1,0:T(8,128)(2,1)}, u32[]{:S(2)}, u32[]{:S(2)}) collective-permute-start(bf16[512,1024]{1,0:T(8,128)(2,1)} %refs_0_.3), channel_id=1, source_target_pairs={{0,4},{2,6},{4,0},{6,2},{8,12},{10,14},{12,8},{14,10},{16,20},{18,... | collective-permute-start | bytes 3145736 | tf_op jit(solution)/shard_map/ppermute | solution.py:671
  3.7 26.2 %collective-permute-start = (bf16[512,1024]{1,0:T(8,128)(2,1)}, bf16[512,1024]{1,0:T(8,128)(2,1)S(1)}, u32[]{:S(2)}, u32[]{:S(2)}) collective-permute-start(bf16[512,1024]{1,0:T(8,128)(2,1)} %refs_0_.3), channel_id=1, source_target_pairs={{0,1},{1,0},{2,3},{3,2},{4,5},{5,4},{6,7},{7,6},{8,9},{9,8},{10,11... | collective-permute-start | bytes 3145736 | tf_op jit(solution)/shard_map/ppermute | solution.py:674
  9.6 1.7 %collective-permute-start.1 = (bf16[1024,128]{1,0:T(8,128)(2,1)}, bf16[1024,128]{1,0:T(8,128)(2,1)S(1)}, u32[]{:S(2)}, u32[]{:S(2)}) collective-permute-start(bf16[1024,128]{1,0:T(8,128)(2,1)} %get-tuple-element.26), channel_id=1, source_target_pairs={{0,2},{2,0},{4,6},{6,4},{8,10},{10,8},{12,14},{14,12},{16,18},{18,... | collective-permute-start | bytes 786440 | tf_op jit(solution)/shard_map/ppermute | solution.py:671
  11.4 16.7 %copy-start.1 = (bf16[1024,128]{1,0:T(8,128)(2,1)}, bf16[1024,128]{1,0:T(8,128)(2,1)S(1)}, u32[]{:S(2)}) copy-start(bf16[1024,128]{1,0:T(8,128)(2,1)S(1)} %collective-permute-done.1.oth_ref.kv_ref) | copy-start | bytes 786436
  13.2 16.7 %all-to-all-start = ((bf16[8,128,128]{2,1,0:T(8,128)(2,1)}), bf16[8,128,128]{2,1,0:T(8,128)(2,1)S(1)}, u32[]{:S(2)}, u32[]{:S(2)}) async-start(bf16[8,128,128]{2,1,0:T(8,128)(2,1)} %bitcast.2), calls=%async_computation | async-start | bytes 524288 | tf_op jit(solution)/shard_map/all_to_all | solution.py:677
  29.9 0.7 copy-start.18
  29.9 1.0 copy-start.6
  32.6 17.3 %collective-permute-start.3 = (bf16[2048,512]{1,0:T(8,128)(2,1)}, bf16[2048,512]{1,0:T(8,128)(2,1)S(1)}, u32[]{:S(2)}, u32[]{:S(2)}) collective-permute-start(bf16[2048,512]{1,0:T(8,128)(2,1)} %get-tuple-element.31), channel_id=1, source_target_pairs={{0,2},{2,0},{4,6},{6,4},{8,10},{10,8},{12,14},{14,12},{16,18},{18,... | collective-permute-start | bytes 6291464 | tf_op jit(solution)/shard_map/ppermute | solution.py:671
  32.6 35.2 %collective-permute-start.9 = (bf16[512,1024]{1,0:T(8,128)(2,1)}, bf16[512,1024]{1,0:T(8,128)(2,1)}, u32[]{:S(2)}, u32[]{:S(2)}) collective-permute-start(bf16[512,1024]{1,0:T(8,128)(2,1)} %collective-permute-done.2.refs_3_.refs_1_.refs_4_), channel_id=1, source_target_pairs={{0,1},{1,0},{2,3},{3,2},{4,5},{5,4},{6,7},{7,6},{8,9},{9,8},{10,11... | collective-permute-start | bytes 3145736 | tf_op jit(solution)/shard_map/ppermute | solution.py:674
  34.3 15.6 %all-to-all-start.1 = ((bf16[8,128,128]{2,1,0:T(8,128)(2,1)}), bf16[8,128,128]{2,1,0:T(8,128)(2,1)S(1)}, u32[]{:S(2)}, u32[]{:S(2)}) async-start(bf16[8,128,128]{2,1,0:T(8,128)(2,1)} %bitcast.20), calls=%async_computation.1 | async-start | bytes 524288 | tf_op jit(solution)/shard_map/all_to_all | solution.py:677
  49.9 0.7 copy-start.2
  49.9 1.4 %copy-start.4 = (bf16[2048,512]{1,0:T(8,128)(2,1)}, bf16[2048,512]{1,0:T(8,128)(2,1)S(1)}, u32[]{:S(2)}) copy-start(bf16[2048,512]{1,0:T(8,128)(2,1)S(1)} %collective-permute-done.3.far_ref) | copy-start | bytes 6291460
  51.3 7.6 %copy-start.20 = (bf16[1024,128]{1,0:T(8,128)(2,1)S(1)}, bf16[1024,128]{1,0:T(8,128)(2,1)}, u32[]{:S(2)}) copy-start(bf16[1024,128]{1,0:T(8,128)(2,1)} %get-tuple-element.35) | copy-start | bytes 786436
  56.8 17.0 %collective-permute-start.4 = (bf16[2,2,128,512]{3,2,1,0:T(8,128)(2,1)}, bf16[2,2,128,512]{3,2,1,0:T(8,128)(2,1)S(1)}, u32[]{:S(2)}, u32[]{:S(2)}) collective-permute-start(bf16[2,2,128,512]{3,2,1,0:T(8,128)(2,1)} %get-tuple-element.33.after_ref), channel_id=1, source_target_pairs={{0,4},{2,6},{4,0},{6,2},{8,12},{10,14},{12,8},{14,10},{16,20},{18,... | collective-permute-start | bytes 1572872 | tf_op jit(solution)/shard_map/ppermute | solution.py:671
  58.9 1.9 %collective-permute-start.5 = (bf16[1024,128]{1,0:T(8,128)(2,1)S(1)}, bf16[1024,128]{1,0:T(8,128)(2,1)S(1)}, u32[]{:S(2)}, u32[]{:S(2)}) collective-permute-start(bf16[1024,128]{1,0:T(8,128)(2,1)S(1)} %copy-done.20), channel_id=1, source_target_pairs={{0,2},{2,0},{4,6},{6,4},{8,10},{10,8},{12,14},{14,12},{16,18},{18,... | collective-permute-start | bytes 786440 | tf_op jit(solution)/shard_map/ppermute | solution.py:671
  58.9 9.0 %collective-permute-start.6 = (bf16[1024,128]{1,0:T(8,128)(2,1)}, bf16[1024,128]{1,0:T(8,128)(2,1)S(1)}, u32[]{:S(2)}, u32[]{:S(2)}) collective-permute-start(bf16[1024,128]{1,0:T(8,128)(2,1)} %get-tuple-element.36), channel_id=1, source_target_pairs={{0,2},{2,0},{4,6},{6,4},{8,10},{10,8},{12,14},{14,12},{16,18},{18,... | collective-permute-start | bytes 786440 | tf_op jit(solution)/shard_map/ppermute | solution.py:671
  59.4 16.4 %collective-permute-start.7 = (bf16[512,1024]{1,0:T(8,128)(2,1)}, bf16[512,1024]{1,0:T(8,128)(2,1)S(1)}, u32[]{:S(2)}, u32[]{:S(2)}) collective-permute-start(bf16[512,1024]{1,0:T(8,128)(2,1)} %refs_0_.3), channel_id=1, source_target_pairs={{0,2},{2,0},{4,6},{6,4},{8,10},{10,8},{12,14},{14,12},{16,18},{18,... | collective-permute-start | bytes 3145736 | tf_op jit(solution)/shard_map/ppermute | solution.py:671
  60.8 0.7 copy-start.10
  60.8 15.1 %collective-permute-start.10 = (bf16[512,1024]{1,0:T(8,128)(2,1)}, bf16[512,1024]{1,0:T(8,128)(2,1)}, u32[]{:S(2)}, u32[]{:S(2)}) collective-permute-start(bf16[512,1024]{1,0:T(8,128)(2,1)} %collective-permute-done.2.refs_3_.refs_1_.refs_4_), channel_id=1, source_target_pairs={{0,2},{2,0},{4,6},{6,4},{8,10},{10,8},{12,14},{14,12},{16,18},{18,... | collective-permute-start | bytes 3145736 | tf_op jit(solution)/shard_map/ppermute | solution.py:671
  63.3 22.9 %all-to-all-start.2 = ((bf16[8,128,128]{2,1,0:T(8,128)(2,1)}), bf16[8,128,128]{2,1,0:T(8,128)(2,1)S(1)}, u32[]{:S(2)}, u32[]{:S(2)}) async-start(bf16[8,128,128]{2,1,0:T(8,128)(2,1)} %bitcast.16), calls=%async_computation.2 | async-start | bytes 524288 | tf_op jit(solution)/shard_map/all_to_all | solution.py:677
  67.8 8.0 %collective-permute-start.8 = (bf16[512,1024]{1,0:T(8,128)(2,1)}, bf16[512,1024]{1,0:T(8,128)(2,1)S(1)}, u32[]{:S(2)}, u32[]{:S(2)}) collective-permute-start(bf16[512,1024]{1,0:T(8,128)(2,1)} %copy-done.6), channel_id=1, source_target_pairs={{0,2},{2,0},{4,6},{6,4},{8,10},{10,8},{12,14},{14,12},{16,18},{18,... | collective-permute-start | bytes 3145736 | tf_op jit(solution)/shard_map/ppermute | solution.py:671
  67.9 0.7 copy-start.11
  67.9 7.9 %collective-permute-start.11 = (bf16[512,1024]{1,0:T(8,128)(2,1)}, bf16[512,1024]{1,0:T(8,128)(2,1)S(1)}, u32[]{:S(2)}, u32[]{:S(2)}) collective-permute-start(bf16[512,1024]{1,0:T(8,128)(2,1)} %collective-permute-done.9.refs_5_), channel_id=1, source_target_pairs={{0,2},{2,0},{4,6},{6,4},{8,10},{10,8},{12,14},{14,12},{16,18},{18,... | collective-permute-start | bytes 3145736 | tf_op jit(solution)/shard_map/ppermute | solution.py:671
  73.8 2.0 %copy-start.19 = (bf16[2,2,128,512]{3,2,1,0:T(8,128)(2,1)}, bf16[2,2,128,512]{3,2,1,0:T(8,128)(2,1)S(1)}, u32[]{:S(2)}) copy-start(bf16[2,2,128,512]{3,2,1,0:T(8,128)(2,1)S(1)} %collective-permute-done.4.refs_0_) | copy-start | bytes 1572868
  73.8 18.6 %collective-permute-start.14 = (bf16[2,2,128,512]{3,2,1,0:T(8,128)(2,1)}, bf16[2,2,128,512]{3,2,1,0:T(8,128)(2,1)S(1)}, u32[]{:S(2)}, u32[]{:S(2)}) collective-permute-start(bf16[2,2,128,512]{3,2,1,0:T(8,128)(2,1)} %get-tuple-element.43), channel_id=1, source_target_pairs={{0,4},{2,6},{4,0},{6,2},{8,12},{10,14},{12,8},{14,10},{16,20},{18,... | collective-permute-start | bytes 1572872 | tf_op jit(solution)/shard_map/ppermute | solution.py:671
  75.8 1.0 copy-start.7
  75.8 1.3 copy-start.8
  75.9 1.6 %copy-start.9 = (bf16[512,1024]{1,0:T(8,128)(2,1)}, bf16[512,1024]{1,0:T(8,128)(2,1)S(1)}, u32[]{:S(2)}) copy-start(bf16[512,1024]{1,0:T(8,128)(2,1)S(1)} %collective-permute-done.11.refs_7_) | copy-start | bytes 3145732
  84.7 18.0 %collective-permute-start.12 = (bf16[128,2048]{1,0:T(8,128)(2,1)}, bf16[128,2048]{1,0:T(8,128)(2,1)S(1)}, u32[]{:S(2)}, u32[]{:S(2)}) collective-permute-start(bf16[128,2048]{1,0:T(8,128)(2,1)} %get-tuple-element.38), channel_id=1, source_target_pairs={{0,8},{2,10},{4,12},{6,14},{8,0},{10,2},{12,4},{14,6},{16,24},{18,... | collective-permute-start | bytes 1572872 | tf_op jit(solution)/shard_map/ppermute | solution.py:671
  86.2 0.7 copy-start.17
  88.6 32.2 %all-to-all-start.3 = ((bf16[8,128,128]{2,1,0:T(8,128)(2,1)}), bf16[8,128,128]{2,1,0:T(8,128)(2,1)S(1)}, u32[]{:S(2)}, u32[]{:S(2)}) async-start(bf16[8,128,128]{2,1,0:T(8,128)(2,1)} %bitcast.17), calls=%async_computation.3 | async-start | bytes 524288 | tf_op jit(solution)/shard_map/all_to_all | solution.py:677
  92.4 10.3 %copy-start.15 = (bf16[128,2048]{1,0:T(8,128)(2,1)S(1)}, bf16[128,2048]{1,0:T(8,128)(2,1)}, u32[]{:S(2)}) copy-start(bf16[128,2048]{1,0:T(8,128)(2,1)} %get-tuple-element.37.refs_0_) | copy-start | bytes 1572868
  92.4 0.8 copy-start.14
  100.6 31.1 %collective-permute-start.15 = (bf16[128,2048]{1,0:T(8,128)(2,1)}, bf16[128,2048]{1,0:T(8,128)(2,1)S(1)}, u32[]{:S(2)}, u32[]{:S(2)}) collective-permute-start(bf16[128,2048]{1,0:T(8,128)(2,1)} %get-tuple-element.45), channel_id=1, source_target_pairs={{0,8},{2,10},{4,12},{6,14},{8,0},{10,2},{12,4},{14,6},{16,24},{18,... | collective-permute-start | bytes 1572872 | tf_op jit(solution)/shard_map/ppermute | solution.py:671
  102.8 2.4 %copy-start.5 = (bf16[128,2048]{1,0:T(8,128)(2,1)}, bf16[128,2048]{1,0:T(8,128)(2,1)S(1)}, u32[]{:S(2)}) copy-start(bf16[128,2048]{1,0:T(8,128)(2,1)S(1)} %add_convert_fusion.after_ref) | copy-start | bytes 1572868
  102.8 28.9 %collective-permute-start.16 = (bf16[128,2048]{1,0:T(8,128)(2,1)S(1)}, bf16[128,2048]{1,0:T(8,128)(2,1)S(1)}, u32[]{:S(2)}, u32[]{:S(2)}) collective-permute-start(bf16[128,2048]{1,0:T(8,128)(2,1)S(1)} %add_convert_fusion.after_ref), channel_id=1, source_target_pairs={{0,16},{2,18},{4,20},{6,22},{8,24},{10,26},{12,28},{14,30},{16,0},... | collective-permute-start | bytes 1572872 | tf_op jit(solution)/shard_map/ppermute | solution.py:671
  120.8 1.0 copy-start.12
  120.8 0.7 copy-start.3
  122.9 1.6 %collective-permute-start.13 = (bf16[1024,128]{1,0:T(8,128)(2,1)S(1)}, bf16[1024,128]{1,0:T(8,128)(2,1)S(1)}, u32[]{:S(2)}, u32[]{:S(2)}) collective-permute-start(bf16[1024,128]{1,0:T(8,128)(2,1)S(1)} %add_convert_fusion.1), channel_id=1, source_target_pairs={{0,2},{2,0},{4,6},{6,4},{8,10},{10,8},{12,14},{14,12},{16,18},{18,... | collective-permute-start | bytes 786440 | tf_op jit(solution)/shard_map/ppermute | solution.py:671
  124.5 0.7 copy-start.16
  125.2 6.6 %copy-start.13 = (bf16[128,2048]{1,0:T(8,128)(2,1)S(1)}, bf16[128,2048]{1,0:T(8,128)(2,1)}, u32[]{:S(2)}) copy-start(bf16[128,2048]{1,0:T(8,128)(2,1)} %get-tuple-element.44) | copy-start | bytes 1572868

commit v6 on v5

--- a/solution.py
+++ b/solution.py
@@ -598,65 +598,43 @@
     )(after, a, b)
 
 
-def key_value_inner_kernel(head, after_ref, q_ref, k_ref, v_ref, g_ref, ko_ref, vo_ref):
+def pair_key_value_kernel(head, me_ref, after_ref, q_ref, k_ref, v_ref, g_ref, s_ref, qd_ref, t_ref, ko_ref, vo_ref):
+    core = me_ref[0] % 2
     half = g_ref.shape[0] // 2
     for j in range(g_ref.shape[1] // head):
-        at = slice(j * head, (j + 1) * head)
-        q, k, v, g = q_ref[:, at], k_ref[:, at], v_ref[:, at], g_ref[:, at]
-        first, second = causal_apply(v, g, q, True)
-        ko_ref[:half, at] = first.astype(BF)
-        ko_ref[half:, at] = second.astype(BF)
-        first, second = causal_apply(k, q, g, True)
-        vo_ref[:half, at] = first.astype(BF)
-        vo_ref[half:, at] = second.astype(BF)
-
-
-def key_value_inner(after, q, k, v, g, head):
-    tok, width = g.shape
-    step = min(4 * head, width)
-    spec = pl.BlockSpec((tok, step), lambda i: (0, i))
-    shape = jax.ShapeDtypeStruct((tok, width), BF)
-    return pl.pallas_call(
-        functools.partial(key_value_inner_kernel, head),
-        grid=(width // step,),
-        in_specs=[ANY, spec, spec, spec, spec],
-        out_specs=[spec, spec],
-        out_shape=[shape, shape],
-        compiler_params=params(),
-        cost_estimate=cost(0, 0),
-        name="key_value_inner",
-    )(after, q, k, v, g)
-
-
-def key_value_outer_kernel(head, me_ref, k_ref, v_ref, ki_ref, vi_ref, s_ref, qd_ref, t_ref, ko_ref, vo_ref):
-    core = me_ref[0] % 2
-    for j in range(k_ref.shape[1] // head):
         at, row = slice(j * head, (j + 1) * head), slice(j // 2 * head, (j // 2 + 1) * head)
         near = s_ref[row, :].astype(F32) + (1 - core).astype(F32) * qd_ref[row, :].astype(F32)
+        q, k, v, g = q_ref[:, at], k_ref[:, at], v_ref[:, at], g_ref[:, at]
         adj = jnp.where(core == j % 2, near.astype(BF), t_ref[row, :])
-        ko_ref[:, at] = (dot(v_ref[:, at], adj, 1, 1) + ki_ref[:, at].astype(F32)).astype(BF)
-        vo_ref[:, at] = (dot(k_ref[:, at], adj, 1, 0) + vi_ref[:, at].astype(F32)).astype(BF)
-
-
-def key_value_outer(me, k, v, key_inner, value_inner, adjoint, qd, other, head):
-    tok, width = k.shape
+        first, second = causal_apply(v, g, q, True)
+        over = dot(v, adj, 1, 1)
+        ko_ref[:half, at] = (first + over[:half]).astype(BF)
+        ko_ref[half:, at] = (second + over[half:]).astype(BF)
+        first, second = causal_apply(k, q, g, True)
+        over = dot(k, adj, 1, 0)
+        vo_ref[:half, at] = (first + over[:half]).astype(BF)
+        vo_ref[half:, at] = (second + over[half:]).astype(BF)
+
+
+def pair_key_value_grad(me, after, q, k, v, g, adjoint, qd, other, head):
+    tok, width = g.shape
     step = min(4 * head, width)
     spec = pl.BlockSpec((tok, step), lambda i, m: (0, i))
     rows = pl.BlockSpec((step // 2, head), lambda i, m: (i, 0))
     shape = jax.ShapeDtypeStruct((tok, width), BF)
     return pl.pallas_call(
-        functools.partial(key_value_outer_kernel, head),
+        functools.partial(pair_key_value_kernel, head),
         grid_spec=pltpu.PrefetchScalarGridSpec(
             num_scalar_prefetch=1,
             grid=(width // step,),
-            in_specs=[spec, spec, spec, spec, rows, rows, rows],
+            in_specs=[ANY, spec, spec, spec, spec, rows, rows, rows],
             out_specs=[spec, spec],
         ),
         out_shape=[shape, shape],
         compiler_params=params(),
         cost_estimate=cost(0, 0),
-        name="key_value_outer",
-    )(me, k, v, key_inner, value_inner, adjoint, qd, other)
+        name="key_value_grad",
+    )(me, after, q, k, v, g, adjoint, qd, other)
 
 
 def local_paired(queries, keys, values, cotangent, out_weight, memory):
@@ -715,11 +693,10 @@
     same = quad_weight(which, (scanned,), mine, received_near, cots, 0)
     neighbour = swap(same[1], 4)
     query_g = pair_query_grad(who, 1, summed, query_g, *query_args)
-    inners = key_value_inner(query_g, queries, keys, values, grad, head)
-    after_chip = passed_after(after_chip, (inners[0],), 0)
+    after_chip = passed_after(after_chip, (query_g,), 0)
     adjoint_other = swap(added(after_chip, core, qd_mine), 1)
-    key_g, value_g = key_value_outer(
-        who, keys, values, *inners, after_chip, qd_other, adjoint_other, head
+    key_g, value_g = pair_key_value_grad(
+        who, query_g, queries, keys, values, grad, after_chip, qd_other, adjoint_other, head
     )
     total = same[0].astype(F32) + neighbour.astype(F32) + crossed.astype(F32)
     return query_g, key_g, value_g, total

time: 134 us -> 131 us (0.978)
  Pallas kernels: 76 us -> 72.7 us
    pallas_call x2 -> x1, Pallas kernels: 16.9 us -> 13.8 us  [pair_key_value_grad(): pl.pallas_call(functools.partial(pair_key_value_kernel, head), grid_spec=...]
  transfers between devices with their start and end apart: 21 -> 21, of which waited for: 4 -> 4; matrix products, arithmetic and copies ran while one was open for 3% -> 3% of each run, Pallas kernels for 56% -> 55%
where the time goes in v6:
time: 131 us; the launch traced here: 130 us
  Pallas kernels  72.7 us (55%)
  starting transfers between devices  36.7 us (28%)
  local copies, waits for them, and re-layouts  8.74 us (7%)
  waiting for transfers between devices  6.47 us (5%)
  other arithmetic  4.17 us (3%)
    all_to_all x4, starting transfers between devices, across(): return lax.all_to_all(x, 'ctx', 0, 0, axis_index_groups=groups, tiled=True)  19.1 us
    ppermute x15, starting transfers between devices, swap(): return lax.ppermute(x, 'ctx', [(c, c ^ bit) for c in range(n)])  14.4 us
    pallas_call x2, Pallas kernels, quad_weight(): pl.pallas_call(functools.partial(quad_weight_kernel, len(after)), grid_sp...  14.4 us
    pallas_call x1, Pallas kernels, pair_key_value_grad(): pl.pallas_call(functools.partial(pair_key_value_kernel, head), grid_spec=...  13.8 us
    pallas_call x2, Pallas kernels, pair_query_grad(): pl.pallas_call(functools.partial(pair_query_kernel, head), grid_spec=pltp...  10.3 us
    pallas_call x1, Pallas kernels, pair_grad(): pl.pallas_call(functools.partial(pair_grad_kernel, head, len(after)), gri...  9.74 us
    pallas_call x1, Pallas kernels, pair_intra(): pl.pallas_call(functools.partial(pair_intra_kernel, head, len(after)), gr...  9.36 us
    unnamed x42, local copies, waits for them, and re-layouts  8.11 us
  transfers between devices with their start and end apart: 21, of which 4 were waited for; matrix products, arithmetic and copies ran while one was open for 3% of the time, Pallas kernels for 55%

profile of v6, /device:TPU:0, one launch (start us, length us, event | category | flops | bytes accessed | tf_op | source)
XLA Modules:
  0.0 129.7 jit_solution(13980666095143122149)
XLA Ops:
  0.6 3.0 %collective-permute-start.2 = (bf16[512,1024]{1,0:T(8,128)(2,1)}, bf16[512,1024]{1,0:T(8,128)(2,1)}, u32[]{:S(2)}, u32[]{:S(2)}) collective-permute-start(bf16[512,1024]{1,0:T(8,128)(2,1)} %refs_0_.3), channel_id=1, source_target_pairs={{0,4},{2,6},{4,0},{6,2},{8,12},{10,14},{12,8},{14,10},{16,20},{18,... | collective-permute-start | bytes 3145736 | tf_op jit(solution)/shard_map/ppermute | solution.py:649
  3.7 1.5 %collective-permute-start = (bf16[512,1024]{1,0:T(8,128)(2,1)}, bf16[512,1024]{1,0:T(8,128)(2,1)S(1)}, u32[]{:S(2)}, u32[]{:S(2)}) collective-permute-start(bf16[512,1024]{1,0:T(8,128)(2,1)} %refs_0_.3), channel_id=1, source_target_pairs={{0,1},{1,0},{2,3},{3,2},{4,5},{5,4},{6,7},{7,6},{8,9},{9,8},{10,11... | collective-permute-start | bytes 3145736 | tf_op jit(solution)/shard_map/ppermute | solution.py:652
  5.2 4.5 %pair_sums.1 = (bf16[1024,128]{1,0:T(8,128)(2,1)}, bf16[1024,128]{1,0:T(8,128)(2,1)}) custom-call(s32[1]{0:T(128)} %bitcast.me_ref, bf16[512,2048]{1,0:T(8,128)(2,1)} %k_ref.5, bf16[512,2048]{1,0:T(8,128)(2,1)} %v_ref.5), custom_call_target="tpu_custom_call" | custom-call | flops 268435456 | bytes 4194304 | tf_op jit(solution)/shard_map/pair_sums/pallas_call | solution.py:305
  9.6 1.7 %collective-permute-done.1.oth_ref.kv_ref = bf16[1024,128]{1,0:T(8,128)(2,1)S(1)} collective-permute-done((bf16[1024,128]{1,0:T(8,128)(2,1)}, bf16[1024,128]{1,0:T(8,128)(2,1)S(1)}, u32[]{:S(2)}, u32[]{:S(2)}) %collective-permute-start.1) | collective-permute-done | bytes 262176 | tf_op jit(solution)/shard_map/ppermute | solution.py:649
  11.4 1.8 %add_convert_fusion.2.refs_0_ = bf16[1024,128]{1,0:T(8,128)(2,1)} fusion(bf16[1024,128]{1,0:T(8,128)(2,1)S(1)} %collective-permute-done.1.oth_ref.kv_ref, bf16[1024,128]{1,0:T(8,128)(2,1)} %get-tuple-element.23.own_ref), kind=kLoop, calls=%fused_computation.3 | loop fusion | flops 524288 | bytes 786432 | tf_op jit(solution)/shard_map/convert_element_type | solution.py:658
  13.2 4.9 %all-to-all-start = ((bf16[8,128,128]{2,1,0:T(8,128)(2,1)}), bf16[8,128,128]{2,1,0:T(8,128)(2,1)S(1)}, u32[]{:S(2)}, u32[]{:S(2)}) async-start(bf16[8,128,128]{2,1,0:T(8,128)(2,1)} %bitcast.2), calls=%async_computation | async-start | bytes 524288 | tf_op jit(solution)/shard_map/all_to_all | solution.py:655
  18.1 0.6 dynamic-slice_bitcast_fusion.refs_0_
  18.7 9.4 %pair_intra.1 = (bf16[1024,512]{1,0:T(8,128)(2,1)}, bf16[2048,512]{1,0:T(8,128)(2,1)}) custom-call(s32[1]{0:T(128)} %bitcast.me_ref, bf16[1024,128]{1,0:T(8,128)(2,1)} %add_convert_fusion.2.refs_0_, bf16[512,2048]{1,0:T(8,128)(2,1)} %q_ref.3, bf16[512,2048]{1,0:T(8,128)(2,1)} %k_ref.5, bf16[512,2048]{1,0:T(8,128)(2,1)} %v_ref.5), custom_call_target="tpu_custom_call" | custom-call | flops 2147483648 | bytes 9437184 | tf_op jit(solution)/shard_map/pair_intra/pallas_call | solution.py:337
  28.1 1.8 %all-to-all-done = bf16[8,128,128]{2,1,0:T(8,128)(2,1)S(1)} async-done(((bf16[8,128,128]{2,1,0:T(8,128)(2,1)}), bf16[8,128,128]{2,1,0:T(8,128)(2,1)S(1)}, u32[]{:S(2)}, u32[]{:S(2)}) %all-to-all-start) | async-done | bytes 262176 | tf_op jit(solution)/shard_map/all_to_all | solution.py:655
  29.9 0.7 copy-done.18
  30.6 0.4 copy-done.6
  30.9 1.7 %scan_blocks.2 = (bf16[1024,128]{1,0:T(8,128)(2,1)}, bf16[2048,512]{1,0:T(8,128)(2,1)}) custom-call(bf16[1024,128]{1,0:T(8,128)(2,1)} %bitcast.19, f32[128,128]{1,0:T(8,128)} %dynamic-slice_bitcast_fusion.refs_0_, bf16[1024,512]{1,0:T(8,128)(2,1)} %get-tuple-element.25.refs_1_.i_ref, bf16[512,1024]{1,0:T(8,128)(2,1)} %copy-done.6, ...), custom_call_target="tpu_custom_call", output_to_operand_aliasing={{1}: (5, {})} | custom-call | flops 20000000000 | tf_op jit(solution)/shard_map/scan_blocks/pallas_call | solution.py:269
  32.6 1.7 %collective-permute-start.9 = (bf16[512,1024]{1,0:T(8,128)(2,1)}, bf16[512,1024]{1,0:T(8,128)(2,1)}, u32[]{:S(2)}, u32[]{:S(2)}) collective-permute-start(bf16[512,1024]{1,0:T(8,128)(2,1)} %collective-permute-done.2.refs_3_.refs_1_.refs_4_), channel_id=1, source_target_pairs={{0,1},{1,0},{2,3},{3,2},{4,5},{5,4},{6,7},{7,6},{8,9},{9,8},{10,11... | collective-permute-start | bytes 3145736 | tf_op jit(solution)/shard_map/ppermute | solution.py:652
  34.3 5.8 %all-to-all-start.1 = ((bf16[8,128,128]{2,1,0:T(8,128)(2,1)}), bf16[8,128,128]{2,1,0:T(8,128)(2,1)S(1)}, u32[]{:S(2)}, u32[]{:S(2)}) async-start(bf16[8,128,128]{2,1,0:T(8,128)(2,1)} %bitcast.20), calls=%async_computation.1 | async-start | bytes 524288 | tf_op jit(solution)/shard_map/all_to_all | solution.py:655
  40.2 9.7 %out_grad.1 = (bf16[512,2048]{1,0:T(8,128)(2,1)}, bf16[1024,128]{1,0:T(8,128)(2,1)}, bf16[1024,128]{1,0:T(8,128)(2,1)}) custom-call(s32[1]{0:T(128)} %bitcast.me_ref, s32[1]{0:T(128)} %bitcast.1.tp_ref, bf16[512,1024]{1,0:T(8,128)(2,1)} %refs_0_.3, bf16[512,1024]{1,0:T(8,128)(2,1)} %copy-done.6, bf16[2048,2048]{1,0:T(8,128)(2,1)} %w_ref.1, ...), custom_call_target="tpu_custom_call" | custom-call | flops 4294967296 | bytes 12582912 | tf_op jit(solution)/shard_map/out_grad/pallas_call | solution.py:545
  49.9 0.7 copy-done.2
  50.6 0.7 copy-done.4
  51.3 5.5 %pair_attended.1 = (bf16[4,2,128,512]{3,2,1,0:T(8,128)(2,1)}, bf16[2,2,128,512]{3,2,1,0:T(8,128)(2,1)}, bf16[2,2,128,512]{3,2,1,0:T(8,128)(2,1)}, bf16[1024,128]{1,0:T(8,128)(2,1)}) custom-call(s32[1]{0:T(128)} %bitcast.me_ref, bf16[512,2048]{1,0:T(8,128)(2,1)} %get-tuple-element.28.after_ref.so_far_ref.g_ref, bf16[512,2048]{1,0:T(8,128)(2,1)} %q_ref.3, ...), custom_call_target="tpu_custom_call" | custom-call | flops 268435456 | bytes 10485760 | tf_op jit(solution)/shard_map/pair_attended/pallas_call | solution.py:397
  56.8 2.1 %collective-permute-start.4 = (bf16[2,2,128,512]{3,2,1,0:T(8,128)(2,1)}, bf16[2,2,128,512]{3,2,1,0:T(8,128)(2,1)S(1)}, u32[]{:S(2)}, u32[]{:S(2)}) collective-permute-start(bf16[2,2,128,512]{3,2,1,0:T(8,128)(2,1)} %get-tuple-element.31.after_ref), channel_id=1, source_target_pairs={{0,4},{2,6},{4,0},{6,2},{8,12},{10,14},{12,8},{14,10},{16,20},{18,... | collective-permute-start | bytes 1572872 | tf_op jit(solution)/shard_map/ppermute | solution.py:649
  58.9 0.5 collective-permute-start.6
  59.4 1.4 %collective-permute-done.5.b_ref.qd_ref = bf16[1024,128]{1,0:T(8,128)(2,1)S(1)} collective-permute-done((bf16[1024,128]{1,0:T(8,128)(2,1)S(1)}, bf16[1024,128]{1,0:T(8,128)(2,1)S(1)}, u32[]{:S(2)}, u32[]{:S(2)}) %collective-permute-start.5) | collective-permute-done | bytes 262176 | tf_op jit(solution)/shard_map/ppermute | solution.py:649
  60.9 0.6 copy-done.10
  61.5 1.8 %add_after.1.after_ref = bf16[1024,128]{1,0:T(8,128)(2,1)} custom-call(bf16[2,2,128,512]{3,2,1,0:T(8,128)(2,1)} %get-tuple-element.31.after_ref, bf16[1024,128]{1,0:T(8,128)(2,1)} %get-tuple-element.32.a_ref, bf16[1024,128]{1,0:T(8,128)(2,1)} %copy-done.10), custom_call_target="tpu_custom_call" | custom-call | tf_op jit(solution)/shard_map/add_after/pallas_call | solution.py:590
  63.3 4.5 %all-to-all-start.2 = ((bf16[8,128,128]{2,1,0:T(8,128)(2,1)}), bf16[8,128,128]{2,1,0:T(8,128)(2,1)S(1)}, u32[]{:S(2)}, u32[]{:S(2)}) async-start(bf16[8,128,128]{2,1,0:T(8,128)(2,1)} %bitcast.16), calls=%async_computation.2 | async-start | bytes 524288 | tf_op jit(solution)/shard_map/all_to_all | solution.py:655
  67.9 0.5 collective-permute-start.11
  68.4 0.2 copy-done.11
  68.6 5.1 %query_grad.2.refs_1_.so_far_ref = bf16[512,2048]{1,0:T(8,128)(2,1)} custom-call(s32[1]{0:T(128)} %bitcast.me_ref, bf16[1024,128]{1,0:T(8,128)(2,1)} %add_after.1.after_ref, bf16[512,2048]{1,0:T(8,128)(2,1)} %get-tuple-element.28.after_ref.so_far_ref.g_ref, bf16[512,2048]{1,0:T(8,128)(2,1)} %get-tuple-element.28.after_ref.so_far_ref.g_ref, ...), custom_call_target="tpu_custom_call" | custom-call | tf_op jit(solution)/shard_map/query_grad/pallas_call | solution.py:502
  73.8 2.0 %collective-permute-start.14 = (bf16[2,2,128,512]{3,2,1,0:T(8,128)(2,1)}, bf16[2,2,128,512]{3,2,1,0:T(8,128)(2,1)S(1)}, u32[]{:S(2)}, u32[]{:S(2)}) collective-permute-start(bf16[2,2,128,512]{3,2,1,0:T(8,128)(2,1)} %get-tuple-element.39), channel_id=1, source_target_pairs={{0,4},{2,6},{4,0},{6,2},{8,12},{10,14},{12,8},{14,10},{16,20},{18,... | collective-permute-start | bytes 1572872 | tf_op jit(solution)/shard_map/ppermute | solution.py:649
  75.8 0.9 copy-done.7
  76.7 0.3 copy-done.8
  77.1 0.3 copy-done.9
  77.4 7.2 %quad_weight.2 = (bf16[128,2048]{1,0:T(8,128)(2,1)}, bf16[128,2048]{1,0:T(8,128)(2,1)}) custom-call(s32[1]{0:T(128)} %bitcast.1.tp_ref, bf16[4,2,128,512]{3,2,1,0:T(8,128)(2,1)} %get-tuple-element.30.a_ref, bf16[2,2,128,512]{3,2,1,0:T(8,128)(2,1)} %passed_after.2.b_ref, bf16[512,1024]{1,0:T(8,128)(2,1)} %refs_0_.3, bf16[512,1024]{1,0:T(8,128)(2,1)} %copy-done.6, ...), custom_call_target="tpu_custom_call" | custom-call | flops 20000000000 | tf_op jit(solution)/shard_map/quad_weight/pallas_call | solution.py:460
  84.6 1.5 %collective-permute-start.12 = (bf16[128,2048]{1,0:T(8,128)(2,1)}, bf16[128,2048]{1,0:T(8,128)(2,1)S(1)}, u32[]{:S(2)}, u32[]{:S(2)}) collective-permute-start(bf16[128,2048]{1,0:T(8,128)(2,1)} %get-tuple-element.36), channel_id=1, source_target_pairs={{0,8},{2,10},{4,12},{6,14},{8,0},{10,2},{12,4},{14,6},{16,24},{18,... | collective-permute-start | bytes 1572872 | tf_op jit(solution)/shard_map/ppermute | solution.py:649
  86.1 0.7 copy-done.17
  86.9 1.7 %scan_blocks.3.refs_8_ = bf16[1024,128]{1,0:T(8,128)(2,1)} custom-call(bf16[1024,128]{1,0:T(8,128)(2,1)} %bitcast.18, bf16[128,2048]{1,0:T(8,128)(2,1)} %get-tuple-element.35.refs_0_), custom_call_target="tpu_custom_call" | custom-call | flops 20000000000 | tf_op jit(solution)/shard_map/scan_blocks/pallas_call | solution.py:269
  88.5 3.9 %all-to-all-start.3 = ((bf16[8,128,128]{2,1,0:T(8,128)(2,1)}), bf16[8,128,128]{2,1,0:T(8,128)(2,1)S(1)}, u32[]{:S(2)}, u32[]{:S(2)}) async-start(bf16[8,128,128]{2,1,0:T(8,128)(2,1)} %bitcast.17), calls=%async_computation.3 | async-start | bytes 524288 | tf_op jit(solution)/shard_map/all_to_all | solution.py:655
  92.4 0.8 copy-done.14
  93.2 7.2 %quad_weight.3 = (bf16[128,2048]{1,0:T(8,128)(2,1)}, bf16[128,2048]{1,0:T(8,128)(2,1)}) custom-call(s32[1]{0:T(128)} %bitcast.1.tp_ref, bf16[4,2,128,512]{3,2,1,0:T(8,128)(2,1)} %get-tuple-element.30.a_ref, bf16[2,2,128,512]{3,2,1,0:T(8,128)(2,1)} %copy-done.14, bf16[512,1024]{1,0:T(8,128)(2,1)} %refs_0_.3, bf16[512,1024]{1,0:T(8,128)(2,1)} %copy-done.6, ...), custom_call_target="tpu_custom_call" | custom-call | tf_op jit(solution)/shard_map/quad_weight/pallas_call | solution.py:460
  100.4 2.1 %collective-permute-start.15 = (bf16[128,2048]{1,0:T(8,128)(2,1)}, bf16[128,2048]{1,0:T(8,128)(2,1)S(1)}, u32[]{:S(2)}, u32[]{:S(2)}) collective-permute-start(bf16[128,2048]{1,0:T(8,128)(2,1)} %get-tuple-element.41), channel_id=1, source_target_pairs={{0,8},{2,10},{4,12},{6,14},{8,0},{10,2},{12,4},{14,6},{16,24},{18,... | collective-permute-start | bytes 1572872 | tf_op jit(solution)/shard_map/ppermute | solution.py:649
  102.7 2.4 %collective-permute-start.16 = (bf16[128,2048]{1,0:T(8,128)(2,1)S(1)}, bf16[128,2048]{1,0:T(8,128)(2,1)S(1)}, u32[]{:S(2)}, u32[]{:S(2)}) collective-permute-start(bf16[128,2048]{1,0:T(8,128)(2,1)S(1)} %add_convert_fusion.after_ref), channel_id=1, source_target_pairs={{0,16},{2,18},{4,20},{6,22},{8,24},{10,26},{12,28},{14,30},{16,0},... | collective-permute-start | bytes 1572872 | tf_op jit(solution)/shard_map/ppermute | solution.py:649
  105.1 5.2 %query_grad.3.refs_1_.after_ref = bf16[512,2048]{1,0:T(8,128)(2,1)} custom-call(s32[1]{0:T(128)} %bitcast.me_ref, bf16[128,2048]{1,0:T(8,128)(2,1)} %copy-done.5, bf16[512,2048]{1,0:T(8,128)(2,1)} %query_grad.2.refs_1_.so_far_ref, bf16[512,2048]{1,0:T(8,128)(2,1)} %get-tuple-element.28.after_ref.so_far_ref.g_ref, ...), custom_call_target="tpu_custom_call", output_to_operand_aliasing={{}: (2, {})} | custom-call | tf_op jit(solution)/shard_map/query_grad/pallas_call | solution.py:502
  110.3 0.7 copy-done.3
  111.0 0.3 copy-done.12
  111.3 1.0 add_convert_fusion.1
  112.4 1.5 %collective-permute-done.13.t_ref = bf16[1024,128]{1,0:T(8,128)(2,1)S(1)} collective-permute-done((bf16[1024,128]{1,0:T(8,128)(2,1)S(1)}, bf16[1024,128]{1,0:T(8,128)(2,1)S(1)}, u32[]{:S(2)}, u32[]{:S(2)}) %collective-permute-start.13) | collective-permute-done | bytes 262176 | tf_op jit(solution)/shard_map/ppermute | solution.py:649
  114.0 0.7 copy-done.16
  114.7 13.8 %key_value_grad.1 = (bf16[512,2048]{1,0:T(8,128)(2,1)}, bf16[512,2048]{1,0:T(8,128)(2,1)}) custom-call(s32[1]{0:T(128)} %bitcast.me_ref, bf16[512,2048]{1,0:T(8,128)(2,1)} %query_grad.3.refs_1_.after_ref, bf16[512,2048]{1,0:T(8,128)(2,1)} %q_ref.3, bf16[512,2048]{1,0:T(8,128)(2,1)} %k_ref.5, bf16[512,2048]{1,0:T(8,128)(2,1)} %v_ref.5, ...), custom_call_target="tpu_custom_call" | custom-call | tf_op jit(solution)/shard_map/key_value_grad/pallas_call | solution.py:625
  128.5 1.2 convert_add_fusion
  (55 shorter events, 0.5 us)
Async XLA Ops:
  0.6 17.4 %copy-start = (f32[16,128,128]{2,1,0:T(8,128)S(1)}, f32[16,128,128]{2,1,0:T(8,128)}, u32[]{:S(2)}) copy-start(f32[16,128,128]{2,1,0:T(8,128)} %param.11) | copy-start | bytes 3145732
  0.6 29.2 %collective-permute-start.2 = (bf16[512,1024]{1,0:T(8,128)(2,1)}, bf16[512,1024]{1,0:T(8,128)(2,1)}, u32[]{:S(2)}, u32[]{:S(2)}) collective-permute-start(bf16[512,1024]{1,0:T(8,128)(2,1)} %refs_0_.3), channel_id=1, source_target_pairs={{0,4},{2,6},{4,0},{6,2},{8,12},{10,14},{12,8},{14,10},{16,20},{18,... | collective-permute-start | bytes 3145736 | tf_op jit(solution)/shard_map/ppermute | solution.py:649
  3.7 26.2 %collective-permute-start = (bf16[512,1024]{1,0:T(8,128)(2,1)}, bf16[512,1024]{1,0:T(8,128)(2,1)S(1)}, u32[]{:S(2)}, u32[]{:S(2)}) collective-permute-start(bf16[512,1024]{1,0:T(8,128)(2,1)} %refs_0_.3), channel_id=1, source_target_pairs={{0,1},{1,0},{2,3},{3,2},{4,5},{5,4},{6,7},{7,6},{8,9},{9,8},{10,11... | collective-permute-start | bytes 3145736 | tf_op jit(solution)/shard_map/ppermute | solution.py:652
  9.6 1.7 %collective-permute-start.1 = (bf16[1024,128]{1,0:T(8,128)(2,1)}, bf16[1024,128]{1,0:T(8,128)(2,1)S(1)}, u32[]{:S(2)}, u32[]{:S(2)}) collective-permute-start(bf16[1024,128]{1,0:T(8,128)(2,1)} %get-tuple-element.24), channel_id=1, source_target_pairs={{0,2},{2,0},{4,6},{6,4},{8,10},{10,8},{12,14},{14,12},{16,18},{18,... | collective-permute-start | bytes 786440 | tf_op jit(solution)/shard_map/ppermute | solution.py:649
  11.4 16.7 %copy-start.1 = (bf16[1024,128]{1,0:T(8,128)(2,1)}, bf16[1024,128]{1,0:T(8,128)(2,1)S(1)}, u32[]{:S(2)}) copy-start(bf16[1024,128]{1,0:T(8,128)(2,1)S(1)} %collective-permute-done.1.oth_ref.kv_ref) | copy-start | bytes 786436
  13.2 16.7 %all-to-all-start = ((bf16[8,128,128]{2,1,0:T(8,128)(2,1)}), bf16[8,128,128]{2,1,0:T(8,128)(2,1)S(1)}, u32[]{:S(2)}, u32[]{:S(2)}) async-start(bf16[8,128,128]{2,1,0:T(8,128)(2,1)} %bitcast.2), calls=%async_computation | async-start | bytes 524288 | tf_op jit(solution)/shard_map/all_to_all | solution.py:655
  29.9 0.7 copy-start.18
  29.9 1.0 copy-start.6
  32.6 17.3 %collective-permute-start.3 = (bf16[2048,512]{1,0:T(8,128)(2,1)}, bf16[2048,512]{1,0:T(8,128)(2,1)S(1)}, u32[]{:S(2)}, u32[]{:S(2)}) collective-permute-start(bf16[2048,512]{1,0:T(8,128)(2,1)} %get-tuple-element.29), channel_id=1, source_target_pairs={{0,2},{2,0},{4,6},{6,4},{8,10},{10,8},{12,14},{14,12},{16,18},{18,... | collective-permute-start | bytes 6291464 | tf_op jit(solution)/shard_map/ppermute | solution.py:649
  32.6 35.2 %collective-permute-start.9 = (bf16[512,1024]{1,0:T(8,128)(2,1)}, bf16[512,1024]{1,0:T(8,128)(2,1)}, u32[]{:S(2)}, u32[]{:S(2)}) collective-permute-start(bf16[512,1024]{1,0:T(8,128)(2,1)} %collective-permute-done.2.refs_3_.refs_1_.refs_4_), channel_id=1, source_target_pairs={{0,1},{1,0},{2,3},{3,2},{4,5},{5,4},{6,7},{7,6},{8,9},{9,8},{10,11... | collective-permute-start | bytes 3145736 | tf_op jit(solution)/shard_map/ppermute | solution.py:652
  34.3 15.6 %all-to-all-start.1 = ((bf16[8,128,128]{2,1,0:T(8,128)(2,1)}), bf16[8,128,128]{2,1,0:T(8,128)(2,1)S(1)}, u32[]{:S(2)}, u32[]{:S(2)}) async-start(bf16[8,128,128]{2,1,0:T(8,128)(2,1)} %bitcast.20), calls=%async_computation.1 | async-start | bytes 524288 | tf_op jit(solution)/shard_map/all_to_all | solution.py:655
  49.9 0.7 copy-start.2
  49.9 1.4 %copy-start.4 = (bf16[2048,512]{1,0:T(8,128)(2,1)}, bf16[2048,512]{1,0:T(8,128)(2,1)S(1)}, u32[]{:S(2)}) copy-start(bf16[2048,512]{1,0:T(8,128)(2,1)S(1)} %collective-permute-done.3.far_ref) | copy-start | bytes 6291460
  51.3 7.6 %copy-start.20 = (bf16[1024,128]{1,0:T(8,128)(2,1)S(1)}, bf16[1024,128]{1,0:T(8,128)(2,1)}, u32[]{:S(2)}) copy-start(bf16[1024,128]{1,0:T(8,128)(2,1)} %get-tuple-element.33) | copy-start | bytes 786436
  56.8 16.9 %collective-permute-start.4 = (bf16[2,2,128,512]{3,2,1,0:T(8,128)(2,1)}, bf16[2,2,128,512]{3,2,1,0:T(8,128)(2,1)S(1)}, u32[]{:S(2)}, u32[]{:S(2)}) collective-permute-start(bf16[2,2,128,512]{3,2,1,0:T(8,128)(2,1)} %get-tuple-element.31.after_ref), channel_id=1, source_target_pairs={{0,4},{2,6},{4,0},{6,2},{8,12},{10,14},{12,8},{14,10},{16,20},{18,... | collective-permute-start | bytes 1572872 | tf_op jit(solution)/shard_map/ppermute | solution.py:649
  58.9 1.9 %collective-permute-start.5 = (bf16[1024,128]{1,0:T(8,128)(2,1)S(1)}, bf16[1024,128]{1,0:T(8,128)(2,1)S(1)}, u32[]{:S(2)}, u32[]{:S(2)}) collective-permute-start(bf16[1024,128]{1,0:T(8,128)(2,1)S(1)} %copy-done.20), channel_id=1, source_target_pairs={{0,2},{2,0},{4,6},{6,4},{8,10},{10,8},{12,14},{14,12},{16,18},{18,... | collective-permute-start | bytes 786440 | tf_op jit(solution)/shard_map/ppermute | solution.py:649
  58.9 9.0 %collective-permute-start.6 = (bf16[1024,128]{1,0:T(8,128)(2,1)}, bf16[1024,128]{1,0:T(8,128)(2,1)S(1)}, u32[]{:S(2)}, u32[]{:S(2)}) collective-permute-start(bf16[1024,128]{1,0:T(8,128)(2,1)} %get-tuple-element.34), channel_id=1, source_target_pairs={{0,2},{2,0},{4,6},{6,4},{8,10},{10,8},{12,14},{14,12},{16,18},{18,... | collective-permute-start | bytes 786440 | tf_op jit(solution)/shard_map/ppermute | solution.py:649
  59.4 16.3 %collective-permute-start.7 = (bf16[512,1024]{1,0:T(8,128)(2,1)}, bf16[512,1024]{1,0:T(8,128)(2,1)S(1)}, u32[]{:S(2)}, u32[]{:S(2)}) collective-permute-start(bf16[512,1024]{1,0:T(8,128)(2,1)} %refs_0_.3), channel_id=1, source_target_pairs={{0,2},{2,0},{4,6},{6,4},{8,10},{10,8},{12,14},{14,12},{16,18},{18,... | collective-permute-start | bytes 3145736 | tf_op jit(solution)/shard_map/ppermute | solution.py:649
  60.8 0.7 copy-start.10
  60.8 15.0 %collective-permute-start.10 = (bf16[512,1024]{1,0:T(8,128)(2,1)}, bf16[512,1024]{1,0:T(8,128)(2,1)}, u32[]{:S(2)}, u32[]{:S(2)}) collective-permute-start(bf16[512,1024]{1,0:T(8,128)(2,1)} %collective-permute-done.2.refs_3_.refs_1_.refs_4_), channel_id=1, source_target_pairs={{0,2},{2,0},{4,6},{6,4},{8,10},{10,8},{12,14},{14,12},{16,18},{18,... | collective-permute-start | bytes 3145736 | tf_op jit(solution)/shard_map/ppermute | solution.py:649
  63.3 22.9 %all-to-all-start.2 = ((bf16[8,128,128]{2,1,0:T(8,128)(2,1)}), bf16[8,128,128]{2,1,0:T(8,128)(2,1)S(1)}, u32[]{:S(2)}, u32[]{:S(2)}) async-start(bf16[8,128,128]{2,1,0:T(8,128)(2,1)} %bitcast.16), calls=%async_computation.2 | async-start | bytes 524288 | tf_op jit(solution)/shard_map/all_to_all | solution.py:655
  67.8 8.0 %collective-permute-start.8 = (bf16[512,1024]{1,0:T(8,128)(2,1)}, bf16[512,1024]{1,0:T(8,128)(2,1)S(1)}, u32[]{:S(2)}, u32[]{:S(2)}) collective-permute-start(bf16[512,1024]{1,0:T(8,128)(2,1)} %copy-done.6), channel_id=1, source_target_pairs={{0,2},{2,0},{4,6},{6,4},{8,10},{10,8},{12,14},{14,12},{16,18},{18,... | collective-permute-start | bytes 3145736 | tf_op jit(solution)/shard_map/ppermute | solution.py:649
  67.9 0.7 copy-start.11
  67.9 7.9 %collective-permute-start.11 = (bf16[512,1024]{1,0:T(8,128)(2,1)}, bf16[512,1024]{1,0:T(8,128)(2,1)S(1)}, u32[]{:S(2)}, u32[]{:S(2)}) collective-permute-start(bf16[512,1024]{1,0:T(8,128)(2,1)} %collective-permute-done.9.refs_5_), channel_id=1, source_target_pairs={{0,2},{2,0},{4,6},{6,4},{8,10},{10,8},{12,14},{14,12},{16,18},{18,... | collective-permute-start | bytes 3145736 | tf_op jit(solution)/shard_map/ppermute | solution.py:649
  73.7 2.0 %copy-start.19 = (bf16[2,2,128,512]{3,2,1,0:T(8,128)(2,1)}, bf16[2,2,128,512]{3,2,1,0:T(8,128)(2,1)S(1)}, u32[]{:S(2)}) copy-start(bf16[2,2,128,512]{3,2,1,0:T(8,128)(2,1)S(1)} %collective-permute-done.4.refs_0_) | copy-start | bytes 1572868
  73.8 18.6 %collective-permute-start.14 = (bf16[2,2,128,512]{3,2,1,0:T(8,128)(2,1)}, bf16[2,2,128,512]{3,2,1,0:T(8,128)(2,1)S(1)}, u32[]{:S(2)}, u32[]{:S(2)}) collective-permute-start(bf16[2,2,128,512]{3,2,1,0:T(8,128)(2,1)} %get-tuple-element.39), channel_id=1, source_target_pairs={{0,4},{2,6},{4,0},{6,2},{8,12},{10,14},{12,8},{14,10},{16,20},{18,... | collective-permute-start | bytes 1572872 | tf_op jit(solution)/shard_map/ppermute | solution.py:649
  75.8 1.0 copy-start.7
  75.8 1.3 copy-start.8
  75.8 1.6 %copy-start.9 = (bf16[512,1024]{1,0:T(8,128)(2,1)}, bf16[512,1024]{1,0:T(8,128)(2,1)S(1)}, u32[]{:S(2)}) copy-start(bf16[512,1024]{1,0:T(8,128)(2,1)S(1)} %collective-permute-done.11.refs_7_) | copy-start | bytes 3145732
  84.6 17.9 %collective-permute-start.12 = (bf16[128,2048]{1,0:T(8,128)(2,1)}, bf16[128,2048]{1,0:T(8,128)(2,1)S(1)}, u32[]{:S(2)}, u32[]{:S(2)}) collective-permute-start(bf16[128,2048]{1,0:T(8,128)(2,1)} %get-tuple-element.36), channel_id=1, source_target_pairs={{0,8},{2,10},{4,12},{6,14},{8,0},{10,2},{12,4},{14,6},{16,24},{18,... | collective-permute-start | bytes 1572872 | tf_op jit(solution)/shard_map/ppermute | solution.py:649
  86.1 0.7 copy-start.17
  88.5 21.7 %all-to-all-start.3 = ((bf16[8,128,128]{2,1,0:T(8,128)(2,1)}), bf16[8,128,128]{2,1,0:T(8,128)(2,1)S(1)}, u32[]{:S(2)}, u32[]{:S(2)}) async-start(bf16[8,128,128]{2,1,0:T(8,128)(2,1)} %bitcast.17), calls=%async_computation.3 | async-start | bytes 524288 | tf_op jit(solution)/shard_map/all_to_all | solution.py:655
  92.4 10.1 %copy-start.15 = (bf16[128,2048]{1,0:T(8,128)(2,1)S(1)}, bf16[128,2048]{1,0:T(8,128)(2,1)}, u32[]{:S(2)}) copy-start(bf16[128,2048]{1,0:T(8,128)(2,1)} %get-tuple-element.35.refs_0_) | copy-start | bytes 1572868
  92.4 0.8 copy-start.14
  100.4 28.1 %collective-permute-start.15 = (bf16[128,2048]{1,0:T(8,128)(2,1)}, bf16[128,2048]{1,0:T(8,128)(2,1)S(1)}, u32[]{:S(2)}, u32[]{:S(2)}) collective-permute-start(bf16[128,2048]{1,0:T(8,128)(2,1)} %get-tuple-element.41), channel_id=1, source_target_pairs={{0,8},{2,10},{4,12},{6,14},{8,0},{10,2},{12,4},{14,6},{16,24},{18,... | collective-permute-start | bytes 1572872 | tf_op jit(solution)/shard_map/ppermute | solution.py:649
  102.7 2.4 %copy-start.5 = (bf16[128,2048]{1,0:T(8,128)(2,1)}, bf16[128,2048]{1,0:T(8,128)(2,1)S(1)}, u32[]{:S(2)}) copy-start(bf16[128,2048]{1,0:T(8,128)(2,1)S(1)} %add_convert_fusion.after_ref) | copy-start | bytes 1572868
  102.7 25.8 %collective-permute-start.16 = (bf16[128,2048]{1,0:T(8,128)(2,1)S(1)}, bf16[128,2048]{1,0:T(8,128)(2,1)S(1)}, u32[]{:S(2)}, u32[]{:S(2)}) collective-permute-start(bf16[128,2048]{1,0:T(8,128)(2,1)S(1)} %add_convert_fusion.after_ref), channel_id=1, source_target_pairs={{0,16},{2,18},{4,20},{6,22},{8,24},{10,26},{12,28},{14,30},{16,0},... | collective-permute-start | bytes 1572872 | tf_op jit(solution)/shard_map/ppermute | solution.py:649
  110.3 1.0 copy-start.12
  110.3 0.7 copy-start.3
  112.3 16.2 %copy-start.13 = (bf16[128,2048]{1,0:T(8,128)(2,1)S(1)}, bf16[128,2048]{1,0:T(8,128)(2,1)}, u32[]{:S(2)}) copy-start(bf16[128,2048]{1,0:T(8,128)(2,1)} %get-tuple-element.40) | copy-start | bytes 1572868
  112.4 1.6 %collective-permute-start.13 = (bf16[1024,128]{1,0:T(8,128)(2,1)S(1)}, bf16[1024,128]{1,0:T(8,128)(2,1)S(1)}, u32[]{:S(2)}, u32[]{:S(2)}) collective-permute-start(bf16[1024,128]{1,0:T(8,128)(2,1)S(1)} %add_convert_fusion.1), channel_id=1, source_target_pairs={{0,2},{2,0},{4,6},{6,4},{8,10},{10,8},{12,14},{14,12},{16,18},{18,... | collective-permute-start | bytes 786440 | tf_op jit(solution)/shard_map/ppermute | solution.py:649
  114.0 0.7 copy-start.16

commit v7 on v6

--- a/solution.py
+++ b/solution.py
@@ -496,9 +496,10 @@
 def pair_query_grad(me, part, after, so_far, g, v, k, state, kv, other, head):
     tok, width = g.shape
     step = min(4 * head, width // 2)
-    steps = width // 2 // step
-    spec = pl.BlockSpec((tok, step), lambda i, m: (0, i + part * steps))
-    rows = pl.BlockSpec((step // 2, head), lambda i, m: (i + part * steps, 0))
+    first = max(1, width // step // 4)
+    steps = width // step - first if part else first
+    spec = pl.BlockSpec((tok, step), lambda i, m: (0, i + part * first))
+    rows = pl.BlockSpec((step // 2, head), lambda i, m: (i + part * first, 0))
     return pl.pallas_call(
         functools.partial(pair_query_kernel, head),
         grid_spec=pltpu.PrefetchScalarGridSpec(

time: 131 us -> 132 us (level)
  transfers between devices with their start and end apart: 21 -> 21, of which waited for: 4 -> 4; matrix products, arithmetic and copies ran while one was open for 3% -> 3% of each run, Pallas kernels for 55% -> 54%
where the time goes in v7:
time: 132 us; the launch traced here: 131 us
  Pallas kernels  72.8 us (55%)
  starting transfers between devices  37.6 us (28%)
  local copies, waits for them, and re-layouts  8.74 us (7%)
  waiting for transfers between devices  6.47 us (5%)
  other arithmetic  4.17 us (3%)
    all_to_all x4, starting transfers between devices, across(): return lax.all_to_all(x, 'ctx', 0, 0, axis_index_groups=groups, tiled=True)  19.9 us
    ppermute x15, starting transfers between devices, swap(): return lax.ppermute(x, 'ctx', [(c, c ^ bit) for c in range(n)])  14.5 us
    pallas_call x2, Pallas kernels, quad_weight(): pl.pallas_call(functools.partial(quad_weight_kernel, len(after)), grid_sp...  14.4 us
    pallas_call x1, Pallas kernels, pair_key_value_grad(): pl.pallas_call(functools.partial(pair_key_value_kernel, head), grid_spec=...  13.8 us
    pallas_call x2, Pallas kernels, pair_query_grad(): pl.pallas_call(functools.partial(pair_query_kernel, head), grid_spec=pltp...  10.3 us
    pallas_call x1, Pallas kernels, pair_grad(): pl.pallas_call(functools.partial(pair_grad_kernel, head, len(after)), gri...  9.74 us
    pallas_call x1, Pallas kernels, pair_intra(): pl.pallas_call(functools.partial(pair_intra_kernel, head, len(after)), gr...  9.36 us
    unnamed x42, local copies, waits for them, and re-layouts  8.11 us
  transfers between devices with their start and end apart: 21, of which 4 were waited for; matrix products, arithmetic and copies ran while one was open for 3% of the time, Pallas kernels for 54%

profile of v7, /device:TPU:0, one launch (start us, length us, event | category | flops | bytes accessed | tf_op | source)
XLA Modules:
  0.0 130.6 jit_solution(13698968071760001375)
XLA Ops:
  0.6 3.0 %collective-permute-start.2 = (bf16[512,1024]{1,0:T(8,128)(2,1)}, bf16[512,1024]{1,0:T(8,128)(2,1)}, u32[]{:S(2)}, u32[]{:S(2)}) collective-permute-start(bf16[512,1024]{1,0:T(8,128)(2,1)} %refs_0_.3), channel_id=1, source_target_pairs={{0,4},{2,6},{4,0},{6,2},{8,12},{10,14},{12,8},{14,10},{16,20},{18,... | collective-permute-start | bytes 3145736 | tf_op jit(solution)/shard_map/ppermute | solution.py:650
  3.7 1.5 %collective-permute-start = (bf16[512,1024]{1,0:T(8,128)(2,1)}, bf16[512,1024]{1,0:T(8,128)(2,1)S(1)}, u32[]{:S(2)}, u32[]{:S(2)}) collective-permute-start(bf16[512,1024]{1,0:T(8,128)(2,1)} %refs_0_.3), channel_id=1, source_target_pairs={{0,1},{1,0},{2,3},{3,2},{4,5},{5,4},{6,7},{7,6},{8,9},{9,8},{10,11... | collective-permute-start | bytes 3145736 | tf_op jit(solution)/shard_map/ppermute | solution.py:653
  5.2 4.5 %pair_sums.1 = (bf16[1024,128]{1,0:T(8,128)(2,1)}, bf16[1024,128]{1,0:T(8,128)(2,1)}) custom-call(s32[1]{0:T(128)} %bitcast.me_ref, bf16[512,2048]{1,0:T(8,128)(2,1)} %k_ref.5, bf16[512,2048]{1,0:T(8,128)(2,1)} %v_ref.5), custom_call_target="tpu_custom_call" | custom-call | flops 268435456 | bytes 4194304 | tf_op jit(solution)/shard_map/pair_sums/pallas_call | solution.py:305
  9.6 1.7 %collective-permute-done.1.oth_ref.kv_ref = bf16[1024,128]{1,0:T(8,128)(2,1)S(1)} collective-permute-done((bf16[1024,128]{1,0:T(8,128)(2,1)}, bf16[1024,128]{1,0:T(8,128)(2,1)S(1)}, u32[]{:S(2)}, u32[]{:S(2)}) %collective-permute-start.1) | collective-permute-done | bytes 262176 | tf_op jit(solution)/shard_map/ppermute | solution.py:650
  11.4 1.8 %add_convert_fusion.2.refs_0_ = bf16[1024,128]{1,0:T(8,128)(2,1)} fusion(bf16[1024,128]{1,0:T(8,128)(2,1)S(1)} %collective-permute-done.1.oth_ref.kv_ref, bf16[1024,128]{1,0:T(8,128)(2,1)} %get-tuple-element.23.own_ref), kind=kLoop, calls=%fused_computation.3 | loop fusion | flops 524288 | bytes 786432 | tf_op jit(solution)/shard_map/convert_element_type | solution.py:659
  13.2 4.9 %all-to-all-start = ((bf16[8,128,128]{2,1,0:T(8,128)(2,1)}), bf16[8,128,128]{2,1,0:T(8,128)(2,1)S(1)}, u32[]{:S(2)}, u32[]{:S(2)}) async-start(bf16[8,128,128]{2,1,0:T(8,128)(2,1)} %bitcast.2), calls=%async_computation | async-start | bytes 524288 | tf_op jit(solution)/shard_map/all_to_all | solution.py:656
  18.1 0.6 dynamic-slice_bitcast_fusion.refs_0_
  18.7 9.4 %pair_intra.1 = (bf16[1024,512]{1,0:T(8,128)(2,1)}, bf16[2048,512]{1,0:T(8,128)(2,1)}) custom-call(s32[1]{0:T(128)} %bitcast.me_ref, bf16[1024,128]{1,0:T(8,128)(2,1)} %add_convert_fusion.2.refs_0_, bf16[512,2048]{1,0:T(8,128)(2,1)} %q_ref.3, bf16[512,2048]{1,0:T(8,128)(2,1)} %k_ref.5, bf16[512,2048]{1,0:T(8,128)(2,1)} %v_ref.5), custom_call_target="tpu_custom_call" | custom-call | flops 2147483648 | bytes 9437184 | tf_op jit(solution)/shard_map/pair_intra/pallas_call | solution.py:337
  28.1 1.8 %all-to-all-done = bf16[8,128,128]{2,1,0:T(8,128)(2,1)S(1)} async-done(((bf16[8,128,128]{2,1,0:T(8,128)(2,1)}), bf16[8,128,128]{2,1,0:T(8,128)(2,1)S(1)}, u32[]{:S(2)}, u32[]{:S(2)}) %all-to-all-start) | async-done | bytes 262176 | tf_op jit(solution)/shard_map/all_to_all | solution.py:656
  29.9 0.7 copy-done.18
  30.6 0.4 copy-done.6
  30.9 1.7 %scan_blocks.2 = (bf16[1024,128]{1,0:T(8,128)(2,1)}, bf16[2048,512]{1,0:T(8,128)(2,1)}) custom-call(bf16[1024,128]{1,0:T(8,128)(2,1)} %bitcast.19, f32[128,128]{1,0:T(8,128)} %dynamic-slice_bitcast_fusion.refs_0_, bf16[1024,512]{1,0:T(8,128)(2,1)} %get-tuple-element.25.refs_1_.i_ref, bf16[512,1024]{1,0:T(8,128)(2,1)} %copy-done.6, ...), custom_call_target="tpu_custom_call", output_to_operand_aliasing={{1}: (5, {})} | custom-call | flops 20000000000 | tf_op jit(solution)/shard_map/scan_blocks/pallas_call | solution.py:269
  32.6 1.7 %collective-permute-start.9 = (bf16[512,1024]{1,0:T(8,128)(2,1)}, bf16[512,1024]{1,0:T(8,128)(2,1)}, u32[]{:S(2)}, u32[]{:S(2)}) collective-permute-start(bf16[512,1024]{1,0:T(8,128)(2,1)} %collective-permute-done.2.refs_3_.refs_1_.refs_4_), channel_id=1, source_target_pairs={{0,1},{1,0},{2,3},{3,2},{4,5},{5,4},{6,7},{7,6},{8,9},{9,8},{10,11... | collective-permute-start | bytes 3145736 | tf_op jit(solution)/shard_map/ppermute | solution.py:653
  34.3 5.8 %all-to-all-start.1 = ((bf16[8,128,128]{2,1,0:T(8,128)(2,1)}), bf16[8,128,128]{2,1,0:T(8,128)(2,1)S(1)}, u32[]{:S(2)}, u32[]{:S(2)}) async-start(bf16[8,128,128]{2,1,0:T(8,128)(2,1)} %bitcast.20), calls=%async_computation.1 | async-start | bytes 524288 | tf_op jit(solution)/shard_map/all_to_all | solution.py:656
  40.2 9.7 %out_grad.1 = (bf16[512,2048]{1,0:T(8,128)(2,1)}, bf16[1024,128]{1,0:T(8,128)(2,1)}, bf16[1024,128]{1,0:T(8,128)(2,1)}) custom-call(s32[1]{0:T(128)} %bitcast.me_ref, s32[1]{0:T(128)} %bitcast.1.tp_ref, bf16[512,1024]{1,0:T(8,128)(2,1)} %refs_0_.3, bf16[512,1024]{1,0:T(8,128)(2,1)} %copy-done.6, bf16[2048,2048]{1,0:T(8,128)(2,1)} %w_ref.1, ...), custom_call_target="tpu_custom_call" | custom-call | flops 4294967296 | bytes 12582912 | tf_op jit(solution)/shard_map/out_grad/pallas_call | solution.py:546
  49.9 0.7 copy-done.2
  50.6 0.7 copy-done.4
  51.3 5.5 %pair_attended.1 = (bf16[4,2,128,512]{3,2,1,0:T(8,128)(2,1)}, bf16[2,2,128,512]{3,2,1,0:T(8,128)(2,1)}, bf16[2,2,128,512]{3,2,1,0:T(8,128)(2,1)}, bf16[1024,128]{1,0:T(8,128)(2,1)}) custom-call(s32[1]{0:T(128)} %bitcast.me_ref, bf16[512,2048]{1,0:T(8,128)(2,1)} %get-tuple-element.28.after_ref.so_far_ref.g_ref, bf16[512,2048]{1,0:T(8,128)(2,1)} %q_ref.3, ...), custom_call_target="tpu_custom_call" | custom-call | flops 268435456 | bytes 10485760 | tf_op jit(solution)/shard_map/pair_attended/pallas_call | solution.py:397
  56.8 2.1 %collective-permute-start.4 = (bf16[2,2,128,512]{3,2,1,0:T(8,128)(2,1)}, bf16[2,2,128,512]{3,2,1,0:T(8,128)(2,1)S(1)}, u32[]{:S(2)}, u32[]{:S(2)}) collective-permute-start(bf16[2,2,128,512]{3,2,1,0:T(8,128)(2,1)} %get-tuple-element.31.after_ref), channel_id=1, source_target_pairs={{0,4},{2,6},{4,0},{6,2},{8,12},{10,14},{12,8},{14,10},{16,20},{18,... | collective-permute-start | bytes 1572872 | tf_op jit(solution)/shard_map/ppermute | solution.py:650
  58.9 0.5 collective-permute-start.6
  59.4 1.4 %collective-permute-done.5.b_ref.qd_ref = bf16[1024,128]{1,0:T(8,128)(2,1)S(1)} collective-permute-done((bf16[1024,128]{1,0:T(8,128)(2,1)S(1)}, bf16[1024,128]{1,0:T(8,128)(2,1)S(1)}, u32[]{:S(2)}, u32[]{:S(2)}) %collective-permute-start.5) | collective-permute-done | bytes 262176 | tf_op jit(solution)/shard_map/ppermute | solution.py:650
  60.9 0.6 copy-done.10
  61.5 1.8 %add_after.1.after_ref = bf16[1024,128]{1,0:T(8,128)(2,1)} custom-call(bf16[2,2,128,512]{3,2,1,0:T(8,128)(2,1)} %get-tuple-element.31.after_ref, bf16[1024,128]{1,0:T(8,128)(2,1)} %get-tuple-element.32.a_ref, bf16[1024,128]{1,0:T(8,128)(2,1)} %copy-done.10), custom_call_target="tpu_custom_call" | custom-call | tf_op jit(solution)/shard_map/add_after/pallas_call | solution.py:591
  63.3 4.5 %all-to-all-start.2 = ((bf16[8,128,128]{2,1,0:T(8,128)(2,1)}), bf16[8,128,128]{2,1,0:T(8,128)(2,1)S(1)}, u32[]{:S(2)}, u32[]{:S(2)}) async-start(bf16[8,128,128]{2,1,0:T(8,128)(2,1)} %bitcast.16), calls=%async_computation.2 | async-start | bytes 524288 | tf_op jit(solution)/shard_map/all_to_all | solution.py:656
  67.9 0.5 collective-permute-start.11
  68.4 0.2 copy-done.11
  68.6 3.6 %query_grad.2.refs_1_.so_far_ref = bf16[512,2048]{1,0:T(8,128)(2,1)} custom-call(s32[1]{0:T(128)} %bitcast.me_ref, bf16[1024,128]{1,0:T(8,128)(2,1)} %add_after.1.after_ref, bf16[512,2048]{1,0:T(8,128)(2,1)} %get-tuple-element.28.after_ref.so_far_ref.g_ref, bf16[512,2048]{1,0:T(8,128)(2,1)} %get-tuple-element.28.after_ref.so_far_ref.g_ref, ...), custom_call_target="tpu_custom_call" | custom-call | tf_op jit(solution)/shard_map/query_grad/pallas_call | solution.py:503
  72.2 1.9 %collective-permute-start.14 = (bf16[2,2,128,512]{3,2,1,0:T(8,128)(2,1)}, bf16[2,2,128,512]{3,2,1,0:T(8,128)(2,1)S(1)}, u32[]{:S(2)}, u32[]{:S(2)}) collective-permute-start(bf16[2,2,128,512]{3,2,1,0:T(8,128)(2,1)} %get-tuple-element.39), channel_id=1, source_target_pairs={{0,4},{2,6},{4,0},{6,2},{8,12},{10,14},{12,8},{14,10},{16,20},{18,... | collective-permute-start | bytes 1572872 | tf_op jit(solution)/shard_map/ppermute | solution.py:650
  74.3 0.9 copy-done.7
  75.2 0.3 copy-done.8
  75.5 0.3 copy-done.9
  75.9 7.2 %quad_weight.2 = (bf16[128,2048]{1,0:T(8,128)(2,1)}, bf16[128,2048]{1,0:T(8,128)(2,1)}) custom-call(s32[1]{0:T(128)} %bitcast.1.tp_ref, bf16[4,2,128,512]{3,2,1,0:T(8,128)(2,1)} %get-tuple-element.30.a_ref, bf16[2,2,128,512]{3,2,1,0:T(8,128)(2,1)} %passed_after.2.b_ref, bf16[512,1024]{1,0:T(8,128)(2,1)} %refs_0_.3, bf16[512,1024]{1,0:T(8,128)(2,1)} %copy-done.6, ...), custom_call_target="tpu_custom_call" | custom-call | flops 20000000000 | tf_op jit(solution)/shard_map/quad_weight/pallas_call | solution.py:460
  83.0 1.7 %collective-permute-start.12 = (bf16[128,2048]{1,0:T(8,128)(2,1)}, bf16[128,2048]{1,0:T(8,128)(2,1)S(1)}, u32[]{:S(2)}, u32[]{:S(2)}) collective-permute-start(bf16[128,2048]{1,0:T(8,128)(2,1)} %get-tuple-element.36), channel_id=1, source_target_pairs={{0,8},{2,10},{4,12},{6,14},{8,0},{10,2},{12,4},{14,6},{16,24},{18,... | collective-permute-start | bytes 1572872 | tf_op jit(solution)/shard_map/ppermute | solution.py:650
  84.8 0.7 copy-done.17
  85.5 1.7 %scan_blocks.3.refs_8_ = bf16[1024,128]{1,0:T(8,128)(2,1)} custom-call(bf16[1024,128]{1,0:T(8,128)(2,1)} %bitcast.18, bf16[128,2048]{1,0:T(8,128)(2,1)} %get-tuple-element.35.refs_0_), custom_call_target="tpu_custom_call" | custom-call | flops 20000000000 | tf_op jit(solution)/shard_map/scan_blocks/pallas_call | solution.py:269
  87.1 4.6 %all-to-all-start.3 = ((bf16[8,128,128]{2,1,0:T(8,128)(2,1)}), bf16[8,128,128]{2,1,0:T(8,128)(2,1)S(1)}, u32[]{:S(2)}, u32[]{:S(2)}) async-start(bf16[8,128,128]{2,1,0:T(8,128)(2,1)} %bitcast.17), calls=%async_computation.3 | async-start | bytes 524288 | tf_op jit(solution)/shard_map/all_to_all | solution.py:656
  91.8 0.8 copy-done.14
  92.6 7.2 %quad_weight.3 = (bf16[128,2048]{1,0:T(8,128)(2,1)}, bf16[128,2048]{1,0:T(8,128)(2,1)}) custom-call(s32[1]{0:T(128)} %bitcast.1.tp_ref, bf16[4,2,128,512]{3,2,1,0:T(8,128)(2,1)} %get-tuple-element.30.a_ref, bf16[2,2,128,512]{3,2,1,0:T(8,128)(2,1)} %copy-done.14, bf16[512,1024]{1,0:T(8,128)(2,1)} %refs_0_.3, bf16[512,1024]{1,0:T(8,128)(2,1)} %copy-done.6, ...), custom_call_target="tpu_custom_call" | custom-call | tf_op jit(solution)/shard_map/quad_weight/pallas_call | solution.py:460
  99.8 2.1 %collective-permute-start.15 = (bf16[128,2048]{1,0:T(8,128)(2,1)}, bf16[128,2048]{1,0:T(8,128)(2,1)S(1)}, u32[]{:S(2)}, u32[]{:S(2)}) collective-permute-start(bf16[128,2048]{1,0:T(8,128)(2,1)} %get-tuple-element.41), channel_id=1, source_target_pairs={{0,8},{2,10},{4,12},{6,14},{8,0},{10,2},{12,4},{14,6},{16,24},{18,... | collective-permute-start | bytes 1572872 | tf_op jit(solution)/shard_map/ppermute | solution.py:650
  102.1 2.4 %collective-permute-start.16 = (bf16[128,2048]{1,0:T(8,128)(2,1)S(1)}, bf16[128,2048]{1,0:T(8,128)(2,1)S(1)}, u32[]{:S(2)}, u32[]{:S(2)}) collective-permute-start(bf16[128,2048]{1,0:T(8,128)(2,1)S(1)} %add_convert_fusion.after_ref), channel_id=1, source_target_pairs={{0,16},{2,18},{4,20},{6,22},{8,24},{10,26},{12,28},{14,30},{16,0},... | collective-permute-start | bytes 1572872 | tf_op jit(solution)/shard_map/ppermute | solution.py:650
  104.5 6.7 %query_grad.3.refs_1_.after_ref = bf16[512,2048]{1,0:T(8,128)(2,1)} custom-call(s32[1]{0:T(128)} %bitcast.me_ref, bf16[128,2048]{1,0:T(8,128)(2,1)} %copy-done.5, bf16[512,2048]{1,0:T(8,128)(2,1)} %query_grad.2.refs_1_.so_far_ref, bf16[512,2048]{1,0:T(8,128)(2,1)} %get-tuple-element.28.after_ref.so_far_ref.g_ref, ...), custom_call_target="tpu_custom_call", output_to_operand_aliasing={{}: (2, {})} | custom-call | tf_op jit(solution)/shard_map/query_grad/pallas_call | solution.py:503
  111.2 0.7 copy-done.3
  111.9 0.3 copy-done.12
  112.2 1.0 add_convert_fusion.1
  113.4 1.5 %collective-permute-done.13.t_ref = bf16[1024,128]{1,0:T(8,128)(2,1)S(1)} collective-permute-done((bf16[1024,128]{1,0:T(8,128)(2,1)S(1)}, bf16[1024,128]{1,0:T(8,128)(2,1)S(1)}, u32[]{:S(2)}, u32[]{:S(2)}) %collective-permute-start.13) | collective-permute-done | bytes 262176 | tf_op jit(solution)/shard_map/ppermute | solution.py:650
  114.9 0.7 copy-done.16
  115.6 13.8 %key_value_grad.1 = (bf16[512,2048]{1,0:T(8,128)(2,1)}, bf16[512,2048]{1,0:T(8,128)(2,1)}) custom-call(s32[1]{0:T(128)} %bitcast.me_ref, bf16[512,2048]{1,0:T(8,128)(2,1)} %query_grad.3.refs_1_.after_ref, bf16[512,2048]{1,0:T(8,128)(2,1)} %q_ref.3, bf16[512,2048]{1,0:T(8,128)(2,1)} %k_ref.5, bf16[512,2048]{1,0:T(8,128)(2,1)} %v_ref.5, ...), custom_call_target="tpu_custom_call" | custom-call | tf_op jit(solution)/shard_map/key_value_grad/pallas_call | solution.py:626
  129.5 1.2 convert_add_fusion
  (55 shorter events, 0.5 us)
Async XLA Ops:
  0.6 17.4 %copy-start = (f32[16,128,128]{2,1,0:T(8,128)S(1)}, f32[16,128,128]{2,1,0:T(8,128)}, u32[]{:S(2)}) copy-start(f32[16,128,128]{2,1,0:T(8,128)} %param.11) | copy-start | bytes 3145732
  0.6 29.2 %collective-permute-start.2 = (bf16[512,1024]{1,0:T(8,128)(2,1)}, bf16[512,1024]{1,0:T(8,128)(2,1)}, u32[]{:S(2)}, u32[]{:S(2)}) collective-permute-start(bf16[512,1024]{1,0:T(8,128)(2,1)} %refs_0_.3), channel_id=1, source_target_pairs={{0,4},{2,6},{4,0},{6,2},{8,12},{10,14},{12,8},{14,10},{16,20},{18,... | collective-permute-start | bytes 3145736 | tf_op jit(solution)/shard_map/ppermute | solution.py:650
  3.7 26.2 %collective-permute-start = (bf16[512,1024]{1,0:T(8,128)(2,1)}, bf16[512,1024]{1,0:T(8,128)(2,1)S(1)}, u32[]{:S(2)}, u32[]{:S(2)}) collective-permute-start(bf16[512,1024]{1,0:T(8,128)(2,1)} %refs_0_.3), channel_id=1, source_target_pairs={{0,1},{1,0},{2,3},{3,2},{4,5},{5,4},{6,7},{7,6},{8,9},{9,8},{10,11... | collective-permute-start | bytes 3145736 | tf_op jit(solution)/shard_map/ppermute | solution.py:653
  9.6 1.7 %collective-permute-start.1 = (bf16[1024,128]{1,0:T(8,128)(2,1)}, bf16[1024,128]{1,0:T(8,128)(2,1)S(1)}, u32[]{:S(2)}, u32[]{:S(2)}) collective-permute-start(bf16[1024,128]{1,0:T(8,128)(2,1)} %get-tuple-element.24), channel_id=1, source_target_pairs={{0,2},{2,0},{4,6},{6,4},{8,10},{10,8},{12,14},{14,12},{16,18},{18,... | collective-permute-start | bytes 786440 | tf_op jit(solution)/shard_map/ppermute | solution.py:650
  11.4 16.7 %copy-start.1 = (bf16[1024,128]{1,0:T(8,128)(2,1)}, bf16[1024,128]{1,0:T(8,128)(2,1)S(1)}, u32[]{:S(2)}) copy-start(bf16[1024,128]{1,0:T(8,128)(2,1)S(1)} %collective-permute-done.1.oth_ref.kv_ref) | copy-start | bytes 786436
  13.2 16.7 %all-to-all-start = ((bf16[8,128,128]{2,1,0:T(8,128)(2,1)}), bf16[8,128,128]{2,1,0:T(8,128)(2,1)S(1)}, u32[]{:S(2)}, u32[]{:S(2)}) async-start(bf16[8,128,128]{2,1,0:T(8,128)(2,1)} %bitcast.2), calls=%async_computation | async-start | bytes 524288 | tf_op jit(solution)/shard_map/all_to_all | solution.py:656
  29.9 0.7 copy-start.18
  29.9 1.0 copy-start.6
  32.6 17.3 %collective-permute-start.3 = (bf16[2048,512]{1,0:T(8,128)(2,1)}, bf16[2048,512]{1,0:T(8,128)(2,1)S(1)}, u32[]{:S(2)}, u32[]{:S(2)}) collective-permute-start(bf16[2048,512]{1,0:T(8,128)(2,1)} %get-tuple-element.29), channel_id=1, source_target_pairs={{0,2},{2,0},{4,6},{6,4},{8,10},{10,8},{12,14},{14,12},{16,18},{18,... | collective-permute-start | bytes 6291464 | tf_op jit(solution)/shard_map/ppermute | solution.py:650
  32.6 35.2 %collective-permute-start.9 = (bf16[512,1024]{1,0:T(8,128)(2,1)}, bf16[512,1024]{1,0:T(8,128)(2,1)}, u32[]{:S(2)}, u32[]{:S(2)}) collective-permute-start(bf16[512,1024]{1,0:T(8,128)(2,1)} %collective-permute-done.2.refs_3_.refs_1_.refs_4_), channel_id=1, source_target_pairs={{0,1},{1,0},{2,3},{3,2},{4,5},{5,4},{6,7},{7,6},{8,9},{9,8},{10,11... | collective-permute-start | bytes 3145736 | tf_op jit(solution)/shard_map/ppermute | solution.py:653
  34.3 15.6 %all-to-all-start.1 = ((bf16[8,128,128]{2,1,0:T(8,128)(2,1)}), bf16[8,128,128]{2,1,0:T(8,128)(2,1)S(1)}, u32[]{:S(2)}, u32[]{:S(2)}) async-start(bf16[8,128,128]{2,1,0:T(8,128)(2,1)} %bitcast.20), calls=%async_computation.1 | async-start | bytes 524288 | tf_op jit(solution)/shard_map/all_to_all | solution.py:656
  49.9 0.7 copy-start.2
  49.9 1.4 %copy-start.4 = (bf16[2048,512]{1,0:T(8,128)(2,1)}, bf16[2048,512]{1,0:T(8,128)(2,1)S(1)}, u32[]{:S(2)}) copy-start(bf16[2048,512]{1,0:T(8,128)(2,1)S(1)} %collective-permute-done.3.far_ref) | copy-start | bytes 6291460
  51.3 7.6 %copy-start.20 = (bf16[1024,128]{1,0:T(8,128)(2,1)S(1)}, bf16[1024,128]{1,0:T(8,128)(2,1)}, u32[]{:S(2)}) copy-start(bf16[1024,128]{1,0:T(8,128)(2,1)} %get-tuple-element.33) | copy-start | bytes 786436
  56.8 15.4 %collective-permute-start.4 = (bf16[2,2,128,512]{3,2,1,0:T(8,128)(2,1)}, bf16[2,2,128,512]{3,2,1,0:T(8,128)(2,1)S(1)}, u32[]{:S(2)}, u32[]{:S(2)}) collective-permute-start(bf16[2,2,128,512]{3,2,1,0:T(8,128)(2,1)} %get-tuple-element.31.after_ref), channel_id=1, source_target_pairs={{0,4},{2,6},{4,0},{6,2},{8,12},{10,14},{12,8},{14,10},{16,20},{18,... | collective-permute-start | bytes 1572872 | tf_op jit(solution)/shard_map/ppermute | solution.py:650
  58.9 1.9 %collective-permute-start.5 = (bf16[1024,128]{1,0:T(8,128)(2,1)S(1)}, bf16[1024,128]{1,0:T(8,128)(2,1)S(1)}, u32[]{:S(2)}, u32[]{:S(2)}) collective-permute-start(bf16[1024,128]{1,0:T(8,128)(2,1)S(1)} %copy-done.20), channel_id=1, source_target_pairs={{0,2},{2,0},{4,6},{6,4},{8,10},{10,8},{12,14},{14,12},{16,18},{18,... | collective-permute-start | bytes 786440 | tf_op jit(solution)/shard_map/ppermute | solution.py:650
  58.9 9.0 %collective-permute-start.6 = (bf16[1024,128]{1,0:T(8,128)(2,1)}, bf16[1024,128]{1,0:T(8,128)(2,1)S(1)}, u32[]{:S(2)}, u32[]{:S(2)}) collective-permute-start(bf16[1024,128]{1,0:T(8,128)(2,1)} %get-tuple-element.34), channel_id=1, source_target_pairs={{0,2},{2,0},{4,6},{6,4},{8,10},{10,8},{12,14},{14,12},{16,18},{18,... | collective-permute-start | bytes 786440 | tf_op jit(solution)/shard_map/ppermute | solution.py:650
  59.4 14.8 %collective-permute-start.7 = (bf16[512,1024]{1,0:T(8,128)(2,1)}, bf16[512,1024]{1,0:T(8,128)(2,1)S(1)}, u32[]{:S(2)}, u32[]{:S(2)}) collective-permute-start(bf16[512,1024]{1,0:T(8,128)(2,1)} %refs_0_.3), channel_id=1, source_target_pairs={{0,2},{2,0},{4,6},{6,4},{8,10},{10,8},{12,14},{14,12},{16,18},{18,... | collective-permute-start | bytes 3145736 | tf_op jit(solution)/shard_map/ppermute | solution.py:650
  60.8 0.7 copy-start.10
  60.8 13.4 %collective-permute-start.10 = (bf16[512,1024]{1,0:T(8,128)(2,1)}, bf16[512,1024]{1,0:T(8,128)(2,1)}, u32[]{:S(2)}, u32[]{:S(2)}) collective-permute-start(bf16[512,1024]{1,0:T(8,128)(2,1)} %collective-permute-done.2.refs_3_.refs_1_.refs_4_), channel_id=1, source_target_pairs={{0,2},{2,0},{4,6},{6,4},{8,10},{10,8},{12,14},{14,12},{16,18},{18,... | collective-permute-start | bytes 3145736 | tf_op jit(solution)/shard_map/ppermute | solution.py:650
  63.3 21.5 %all-to-all-start.2 = ((bf16[8,128,128]{2,1,0:T(8,128)(2,1)}), bf16[8,128,128]{2,1,0:T(8,128)(2,1)S(1)}, u32[]{:S(2)}, u32[]{:S(2)}) async-start(bf16[8,128,128]{2,1,0:T(8,128)(2,1)} %bitcast.16), calls=%async_computation.2 | async-start | bytes 524288 | tf_op jit(solution)/shard_map/all_to_all | solution.py:656
  67.8 6.4 %collective-permute-start.8 = (bf16[512,1024]{1,0:T(8,128)(2,1)}, bf16[512,1024]{1,0:T(8,128)(2,1)S(1)}, u32[]{:S(2)}, u32[]{:S(2)}) collective-permute-start(bf16[512,1024]{1,0:T(8,128)(2,1)} %copy-done.6), channel_id=1, source_target_pairs={{0,2},{2,0},{4,6},{6,4},{8,10},{10,8},{12,14},{14,12},{16,18},{18,... | collective-permute-start | bytes 3145736 | tf_op jit(solution)/shard_map/ppermute | solution.py:650
  67.9 0.7 copy-start.11
  67.9 6.3 %collective-permute-start.11 = (bf16[512,1024]{1,0:T(8,128)(2,1)}, bf16[512,1024]{1,0:T(8,128)(2,1)S(1)}, u32[]{:S(2)}, u32[]{:S(2)}) collective-permute-start(bf16[512,1024]{1,0:T(8,128)(2,1)} %collective-permute-done.9.refs_5_), channel_id=1, source_target_pairs={{0,2},{2,0},{4,6},{6,4},{8,10},{10,8},{12,14},{14,12},{16,18},{18,... | collective-permute-start | bytes 3145736 | tf_op jit(solution)/shard_map/ppermute | solution.py:650
  72.2 2.0 %copy-start.19 = (bf16[2,2,128,512]{3,2,1,0:T(8,128)(2,1)}, bf16[2,2,128,512]{3,2,1,0:T(8,128)(2,1)S(1)}, u32[]{:S(2)}) copy-start(bf16[2,2,128,512]{3,2,1,0:T(8,128)(2,1)S(1)} %collective-permute-done.4.refs_0_) | copy-start | bytes 1572868
  72.2 19.5 %collective-permute-start.14 = (bf16[2,2,128,512]{3,2,1,0:T(8,128)(2,1)}, bf16[2,2,128,512]{3,2,1,0:T(8,128)(2,1)S(1)}, u32[]{:S(2)}, u32[]{:S(2)}) collective-permute-start(bf16[2,2,128,512]{3,2,1,0:T(8,128)(2,1)} %get-tuple-element.39), channel_id=1, source_target_pairs={{0,4},{2,6},{4,0},{6,2},{8,12},{10,14},{12,8},{14,10},{16,20},{18,... | collective-permute-start | bytes 1572872 | tf_op jit(solution)/shard_map/ppermute | solution.py:650
  74.2 1.0 copy-start.7
  74.2 1.3 copy-start.8
  74.3 1.6 %copy-start.9 = (bf16[512,1024]{1,0:T(8,128)(2,1)}, bf16[512,1024]{1,0:T(8,128)(2,1)S(1)}, u32[]{:S(2)}) copy-start(bf16[512,1024]{1,0:T(8,128)(2,1)S(1)} %collective-permute-done.11.refs_7_) | copy-start | bytes 3145732
  83.0 18.9 %collective-permute-start.12 = (bf16[128,2048]{1,0:T(8,128)(2,1)}, bf16[128,2048]{1,0:T(8,128)(2,1)S(1)}, u32[]{:S(2)}, u32[]{:S(2)}) collective-permute-start(bf16[128,2048]{1,0:T(8,128)(2,1)} %get-tuple-element.36), channel_id=1, source_target_pairs={{0,8},{2,10},{4,12},{6,14},{8,0},{10,2},{12,4},{14,6},{16,24},{18,... | collective-permute-start | bytes 1572872 | tf_op jit(solution)/shard_map/ppermute | solution.py:650
  84.8 0.7 copy-start.17
  87.1 24.1 %all-to-all-start.3 = ((bf16[8,128,128]{2,1,0:T(8,128)(2,1)}), bf16[8,128,128]{2,1,0:T(8,128)(2,1)S(1)}, u32[]{:S(2)}, u32[]{:S(2)}) async-start(bf16[8,128,128]{2,1,0:T(8,128)(2,1)} %bitcast.17), calls=%async_computation.3 | async-start | bytes 524288 | tf_op jit(solution)/shard_map/all_to_all | solution.py:656
  91.8 10.1 %copy-start.15 = (bf16[128,2048]{1,0:T(8,128)(2,1)S(1)}, bf16[128,2048]{1,0:T(8,128)(2,1)}, u32[]{:S(2)}) copy-start(bf16[128,2048]{1,0:T(8,128)(2,1)} %get-tuple-element.35.refs_0_) | copy-start | bytes 1572868
  91.8 0.8 copy-start.14
  99.8 29.6 %collective-permute-start.15 = (bf16[128,2048]{1,0:T(8,128)(2,1)}, bf16[128,2048]{1,0:T(8,128)(2,1)S(1)}, u32[]{:S(2)}, u32[]{:S(2)}) collective-permute-start(bf16[128,2048]{1,0:T(8,128)(2,1)} %get-tuple-element.41), channel_id=1, source_target_pairs={{0,8},{2,10},{4,12},{6,14},{8,0},{10,2},{12,4},{14,6},{16,24},{18,... | collective-permute-start | bytes 1572872 | tf_op jit(solution)/shard_map/ppermute | solution.py:650
  102.0 2.4 %copy-start.5 = (bf16[128,2048]{1,0:T(8,128)(2,1)}, bf16[128,2048]{1,0:T(8,128)(2,1)S(1)}, u32[]{:S(2)}) copy-start(bf16[128,2048]{1,0:T(8,128)(2,1)S(1)} %add_convert_fusion.after_ref) | copy-start | bytes 1572868
  102.1 27.4 %collective-permute-start.16 = (bf16[128,2048]{1,0:T(8,128)(2,1)S(1)}, bf16[128,2048]{1,0:T(8,128)(2,1)S(1)}, u32[]{:S(2)}, u32[]{:S(2)}) collective-permute-start(bf16[128,2048]{1,0:T(8,128)(2,1)S(1)} %add_convert_fusion.after_ref), channel_id=1, source_target_pairs={{0,16},{2,18},{4,20},{6,22},{8,24},{10,26},{12,28},{14,30},{16,0},... | collective-permute-start | bytes 1572872 | tf_op jit(solution)/shard_map/ppermute | solution.py:650
  111.2 1.0 copy-start.12
  111.2 0.7 copy-start.3
  113.3 16.2 %copy-start.13 = (bf16[128,2048]{1,0:T(8,128)(2,1)S(1)}, bf16[128,2048]{1,0:T(8,128)(2,1)}, u32[]{:S(2)}) copy-start(bf16[128,2048]{1,0:T(8,128)(2,1)} %get-tuple-element.40) | copy-start | bytes 1572868
  113.3 1.6 %collective-permute-start.13 = (bf16[1024,128]{1,0:T(8,128)(2,1)S(1)}, bf16[1024,128]{1,0:T(8,128)(2,1)S(1)}, u32[]{:S(2)}, u32[]{:S(2)}) collective-permute-start(bf16[1024,128]{1,0:T(8,128)(2,1)S(1)} %add_convert_fusion.1), channel_id=1, source_target_pairs={{0,2},{2,0},{4,6},{6,4},{8,10},{10,8},{12,14},{14,12},{16,18},{18,... | collective-permute-start | bytes 786440 | tf_op jit(solution)/shard_map/ppermute | solution.py:650
  114.9 0.7 copy-start.16
